TPU v7x, 32 devices: a whole 2x2x4 slice. The times are simulated.
32 devices in a mesh: dp: 8 (over y, x, core), tensor: 4 (over z).
Axes of the slice: x: 2, y: 2, z: 4, core: 2. Of those that a mesh axis runs over, the one named last changes fastest.
Arguments:
- activations: bfloat16 [2, 128, 8192], P(None, 'dp', 'tensor'), may hold values from -6 to 6
- gate_weight: bfloat16 [8192, 28672], P('tensor', 'dp'), may hold values from -0.0625 to 0.0625
- up_weight: bfloat16 [8192, 28672], P('tensor', 'dp'), may hold values from -0.0625 to 0.0625
- down_weight: bfloat16 [28672, 8192], P('dp', 'tensor'), may hold values from -0.03125 to 0.03125
- shrink_weight: bfloat16 [8192, 1024], P('tensor', 'dp'), may hold values from -0.0625 to 0.0625
- expand_weight: bfloat16 [2, 32, 16, 28672], P(None, 'tensor', None, 'dp'), may hold values from -1.5 to 1.5
- adapter_scale: float32 [32], P('dp'), may hold values from 0.5 to 2
- adapter_ids: int32 [128], replicated, may hold values from 0 to 31, as said below
Outputs:
- mixed: bfloat16 [2, 128, 8192], P(None, 'dp', 'tensor')
Inputs may be any that keep to these rules, and one draw needn't show every extreme that they name: `adapter_ids`: at most 64 rows name adapters of one adapter block of 8 consecutive adapters, and in every draw some block is named by exactly 64 rows.
All inputs are finite; a program needn't handle non-finite values.
Results may differ from a plain program's by a relative error of at most 0.03.
Values may be sent and summed in bfloat16 or wider, within the bound.
No kernel may reach another device: no remote copies, remote signals or barrier semaphores. Data moves between devices by JAX's collectives and lax.ppermute only.
A program may use at most 128 MiB of HBM per device.

v0:
```python
import jax
import jax.numpy as jnp
from jax import lax
from jax.sharding import PartitionSpec as P


def per_device(
    activations,
    gate_weight,
    up_weight,
    down_weight,
    shrink_weight,
    expand_weight,
    adapter_scale,
    adapter_ids,
):
    dp_index = lax.axis_index("dp")
    tp_index = lax.axis_index("tensor")
    adp_local = adapter_scale.shape[0]
    adp_block = expand_weight.shape[1]
    low_rank = expand_weight.shape[2]
    ff_local = expand_weight.shape[3]
    total_rows = adapter_ids.shape[0]
    local_ids = jnp.arange(adp_local, dtype=jnp.int32)
    owned = (adapter_ids[:, None] == dp_index * adp_local + local_ids[None, :]).astype(jnp.float32)
    owned_scale = owned * adapter_scale[None, :]
    block_ids = jnp.arange(adp_block, dtype=jnp.int32)
    in_block = (adapter_ids[:, None] == tp_index * adp_block + block_ids[None, :]).astype(
        jnp.bfloat16
    )
    spread_mask = jnp.repeat(in_block, low_rank, axis=1)
    gate_expand = expand_weight[0].reshape(adp_block * low_rank, ff_local)
    up_expand = expand_weight[1].reshape(adp_block * low_rank, ff_local)

    def expand_rows(low_inputs, mask_rows):
        gate_low = jnp.tile(low_inputs[:, :, :low_rank], (1, 1, adp_block)) * mask_rows[None]
        up_low = jnp.tile(low_inputs[:, :, low_rank:], (1, 1, adp_block)) * mask_rows[None]
        gate_delta = jnp.einsum(
            "src,cf->srf", gate_low, gate_expand, preferred_element_type=jnp.float32
        )
        up_delta = jnp.einsum("src,cf->srf", up_low, up_expand, preferred_element_type=jnp.float32)
        return (gate_delta, up_delta)

    def process(features_in):
        num_steps = features_in.shape[0]
        gathered = lax.all_gather(features_in, "dp", axis=1, tiled=True)
        shrunk = jnp.einsum(
            "srd,dc->src", gathered, shrink_weight, preferred_element_type=jnp.float32
        )
        shrunk = shrunk.reshape(num_steps, total_rows, adp_local, 2 * low_rank)
        partial_low = jnp.einsum(
            "srec,re->src", shrunk, owned_scale, precision=lax.Precision.HIGHEST
        )
        packed = partial_low.reshape(num_steps, total_rows * 2 * low_rank // 128, 128)
        summed = lax.psum(packed, ("dp", "tensor"))
        low_inputs = summed.reshape(num_steps, total_rows, 2 * low_rank).astype(jnp.bfloat16)
        gate_part = jnp.einsum(
            "srd,df->srf", gathered, gate_weight, preferred_element_type=jnp.float32
        )
        up_part = jnp.einsum("srd,df->srf", gathered, up_weight, preferred_element_type=jnp.float32)
        gate_delta, up_delta = expand_rows(low_inputs, spread_mask)
        gate_part = gate_part + gate_delta
        up_part = up_part + up_delta
        gate_round = gate_part.astype(jnp.bfloat16)
        up_round = up_part.astype(jnp.bfloat16)
        gate_sum, up_sum = (
            lax.psum(gate_round, "tensor").astype(jnp.float32),
            lax.psum(up_round, "tensor").astype(jnp.float32),
        )
        hidden = (jax.nn.silu(gate_sum) * up_sum).astype(jnp.bfloat16)
        down_part = jnp.einsum(
            "srf,fd->srd", hidden, down_weight, preferred_element_type=jnp.float32
        )
        return lax.psum_scatter(
            down_part.astype(jnp.bfloat16), "dp", scatter_dimension=1, tiled=True
        )

    pieces = [
        process(activations[step_index : step_index + 1])
        for step_index in range(activations.shape[0])
    ]
    return jnp.concatenate(pieces, axis=0)


def solution(mesh):
    placed = (
        P(None, "dp", "tensor"),
        P("tensor", "dp"),
        P("tensor", "dp"),
        P("dp", "tensor"),
        P("tensor", "dp"),
        P(None, "tensor", None, "dp"),
        P("dp"),
        P(),
    )
    return jax.shard_map(
        per_device, mesh=mesh, in_specs=placed, out_specs=P(None, "dp", "tensor"), check_vma=False
    )
```

profile of v0, /device:TPU:0, one launch (start us, length us, event | category | flops | bytes accessed | tf_op | source)
XLA Modules:
  0.0 329.3 jit_solution(13234681324216408328)
XLA Ops:
  6.5 0.0 all-reduce.4.cloned.1.call-start
  6.5 0.9 fusion.39
  7.4 11.3 %all_gather.6 = bf16[1,128,2048]{2,1,0:T(8,128)(2,1)S(1)} all-gather(bf16[1,16,2048]{2,1,0:T(8,128)(2,1)S(1)} %get-tuple-element.13), channel_id=1, replica_groups=mesh['dp'=8,'tensor'=4] {'dp'}, dimensions={1}, use_global_device_ids=true | all-gather | bytes 589824 | tf_op jit(solution)/shard_map/all_gather | solution.py:46
  18.7 1.4 copy.9
  20.1 9.8 %all_gather.7 = bf16[1,128,2048]{2,1,0:T(8,128)(2,1)S(1)} all-gather(bf16[1,16,2048]{2,1,0:T(8,128)(2,1)S(1)} %get-tuple-element.14), channel_id=1, replica_groups=mesh['dp'=8,'tensor'=4] {'dp'}, dimensions={1}, use_global_device_ids=true | all-gather | bytes 589824 | tf_op jit(solution)/shard_map/all_gather | solution.py:46
  30.0 0.3 fusion.30
  30.3 0.3 fusion.24
  30.6 0.0 slice-start.1
  30.6 0.0 slice-start.2
  30.7 0.0 slice-start.3
  30.7 0.0 slice-start.4
  30.7 0.0 slice-start.5
  30.7 8.7 %fusion.28 = f32[128,3584]{1,0:T(8,128)} fusion(bf16[2048,3584]{1,0:T(8,128)(2,1)} %param.9, bf16[1,128,2048]{2,1,0:T(8,128)(2,1)S(1)} %all_gather.7), kind=kOutput, calls=%fused_computation.36 | convolution fusion | flops 1879048192 | bytes 17039360 | tf_op jit(solution)/shard_map/srd,df->srf/dot_general | solution.py:57
  39.4 0.0 slice-done
  39.4 0.0 slice-done.1
  39.4 0.0 slice-done.2
  39.4 0.8 slice-done.3
  40.1 3.3 %fusion.34 = f32[128,3584]{1,0:T(8,128)} fusion(bf16[2048,3584]{1,0:T(8,128)(2,1)S(1)} %bitcast.79, bf16[1,128,2048]{2,1,0:T(8,128)(2,1)S(1)} %all_gather.6), kind=kOutput, calls=%fused_computation.42 | convolution fusion | flops 1879048192 | bytes 17039360 | tf_op jit(solution)/shard_map/srd,df->srf/dot_general | solution.py:57
  43.4 0.0 slice-done.4
  43.4 0.0 slice-done.5
  43.4 1.2 slice-done.6
  44.6 0.6 slice-done.7
  45.2 3.4 %fusion.32 = f32[128,3584]{1,0:T(8,128)} fusion(bf16[2048,3584]{1,0:T(8,128)(2,1)S(1)} %bitcast.81, bf16[1,128,2048]{2,1,0:T(8,128)(2,1)S(1)} %all_gather.6), kind=kOutput, calls=%fused_computation.40 | convolution fusion | flops 1879048192 | bytes 17039360 | tf_op jit(solution)/shard_map/srd,df->srf/dot_general | solution.py:60
  48.6 2.1 fusion.26
  50.8 0.1 copy.14
  51.0 0.0 copy-done.3
  51.0 0.0 copy-done.4
  51.0 0.1 compare_select_fusion
  51.1 1.0 fusion.40
  52.0 0.1 transpose.16
  52.1 0.2 copy.17
  52.3 1.0 fusion.41
  53.2 0.1 transpose.17
  53.3 40.0 %all-reduce = (bf16[1,32,128]{2,1,0:T(8,128)(2,1)S(1)}, bf16[1,32,128]{2,1,0:T(8,128)(2,1)S(1)}) all-reduce(f32[1,32,128]{2,1,0:T(8,128)S(1)} %transpose.17, f32[1,32,128]{2,1,0:T(8,128)S(1)} %transpose.16), channel_id=1, replica_groups=mesh['dp'=8,'tensor'=4] {'dp','tensor'}, use_global_device_ids=true, to_apply=%region_4.5 | all-reduce | flops 8192 | bytes 49152 | tf_op jit(solution)/shard_map/psum | solution.py:55
  93.3 0.1 convert_element_type.87
  93.4 0.1 slice_bitcast_fusion.3
  93.5 0.1 copy.10
  93.5 0.1 copy.11
  93.6 0.1 convert_element_type.99
  93.7 0.1 slice_bitcast_fusion.1
  93.8 0.1 copy.12
  93.9 0.1 copy.13
  94.0 0.1 compare_convert_fusion
  94.1 1.7 fusion.38
  95.8 0.3 copy-done.2
  96.1 1.4 fusion.5
  97.5 0.4 copy-done.1
  97.9 1.4 fusion.7
  99.3 0.4 copy-done
  99.6 1.4 fusion.6
  101.0 1.4 fusion.4
  102.4 0.0 all-reduce.4.cloned.1.call-update
  102.4 0.0 reduce-scatter.3.cloned.1.call-start
  102.5 139.0 %all-reduce.4.cloned.1.call-done = (bf16[1,128,3584]{2,1,0:T(8,128)(2,1)}, bf16[1,128,3584]{2,1,0:T(8,128)(2,1)}, bf16[1,128,3584]{2,1,0:T(8,128)(2,1)}, bf16[1,128,3584]{2,1,0:T(8,128)(2,1)}) async-done(((bf16[1,128,3584]{2,1,0:T(8,128)(2,1)}, bf16[1,128,3584]{2,1,0:T(8,128)(2,1)}, bf16[1,128,3584]{2,1,0:T(8,128)(2,1)}, bf16[1,128,3584]{2,1,0:T(8,128)(2,1)}), (bf16[1,128,3584]{2,1,0:T(8,128)(2,1)}, ...) | async-done | bytes 3670032 | tf_op jit(solution)/shard_map/psum | solution.py:68
  241.5 8.9 %fusion.8 = bf16[1,128,2048]{2,1,0:T(8,128)(2,1)} fusion(bf16[3584,2048]{1,0:T(8,128)(2,1)} %param.11, bf16[1,128,3584]{2,1,0:T(8,128)(2,1)} %get-tuple-element.9, bf16[1,128,3584]{2,1,0:T(8,128)(2,1)} %get-tuple-element.10), kind=kOutput, calls=%fused_computation.14 | convolution fusion | flops 1882980352 | bytes 17039360 | tf_op jit(solution)/shard_map/srf,fd->srd/dot_general | solution.py:71
  250.4 0.0 reduce-scatter.3.cloned.1.call-update
  250.4 0.0 reduce-scatter.5.cloned.1.call-start
  250.5 0.0 copy-done.5
  250.5 0.0 copy-done.6
  250.5 8.3 %fusion.9 = bf16[1,128,2048]{2,1,0:T(8,128)(2,1)} fusion(bf16[3584,2048]{1,0:T(8,128)(2,1)} %param.11, bf16[1,128,3584]{2,1,0:T(8,128)(2,1)S(1)} %copy-done.5, bf16[1,128,3584]{2,1,0:T(8,128)(2,1)S(1)} %copy-done.6), kind=kOutput, calls=%fused_computation.15 | convolution fusion | flops 1882980352 | bytes 17039360 | tf_op jit(solution)/shard_map/srf,fd->srd/dot_general | solution.py:71
  258.8 0.0 reduce-scatter.5.cloned.1.call-update
  258.9 24.8 %reduce-scatter.3.cloned.1.call-done = bf16[1,16,2048]{2,1,0:T(8,128)(2,1)} async-done(((bf16[1,128,2048]{2,1,0:T(8,128)(2,1)}), bf16[1,16,2048]{2,1,0:T(8,128)(2,1)}) %reduce-scatter.3.cloned.1.call-update) | async-done | bytes 65552 | tf_op jit(solution)/shard_map/reduce_scatter | solution.py:74
  283.6 37.6 %reduce-scatter.5.cloned.1.call-done = bf16[1,16,2048]{2,1,0:T(8,128)(2,1)} async-done(((bf16[1,128,2048]{2,1,0:T(8,128)(2,1)}), bf16[1,16,2048]{2,1,0:T(8,128)(2,1)}) %reduce-scatter.5.cloned.1.call-update) | async-done | bytes 65552 | tf_op jit(solution)/shard_map/reduce_scatter | solution.py:74
  321.2 1.5 pad_maximum_fusion
  (15 shorter events, 0.0 us)
Async XLA Ops:
  6.5 235.0 %all-reduce.4.cloned.1.call-start = ((), (), s32[]{:S(2)}) async-start(), calls=%async_computation.4 | async-start | bytes 7340032 | tf_op jit(solution)/shard_map/psum | solution.py:68
  18.7 20.6 %slice-start = ((s8[14680064]{0:T(1024)(128)(4,1)}), s8[2097152]{0:T(1024)(128)(4,1)S(1)}, s32[]{:S(2)}) async-start(s8[14680064]{0:T(1024)(128)(4,1)} %bitcast.78), calls=%async_computation.5 | async-start | bytes 4194304
  30.6 8.7 %slice-start.1 = ((s8[14680064]{0:T(1024)(128)(4,1)}), s8[4194304]{0:T(1024)(128)(4,1)S(1)}, s32[]{:S(2)}) async-start(s8[14680064]{0:T(1024)(128)(4,1)} %bitcast.78), calls=%async_computation.6 | async-start | bytes 8388608
  30.6 8.7 %slice-start.2 = ((s8[14680064]{0:T(1024)(128)(4,1)}), s8[4194304]{0:T(1024)(128)(4,1)S(1)}, s32[]{:S(2)}) async-start(s8[14680064]{0:T(1024)(128)(4,1)} %bitcast.78), calls=%async_computation.7 | async-start | bytes 8388608
  30.7 9.5 %slice-start.3 = ((s8[14680064]{0:T(1024)(128)(4,1)}), s8[4194304]{0:T(1024)(128)(4,1)S(1)}, s32[]{:S(2)}) async-start(s8[14680064]{0:T(1024)(128)(4,1)} %bitcast.78), calls=%async_computation.8 | async-start | bytes 8388608
  30.7 12.8 %slice-start.4 = ((s8[14680064]{0:T(1024)(128)(4,1)}), s8[4194304]{0:T(1024)(128)(4,1)S(1)}, s32[]{:S(2)}) async-start(s8[14680064]{0:T(1024)(128)(4,1)} %bitcast.80), calls=%async_computation.9 | async-start | bytes 8388608
  30.7 12.8 %slice-start.5 = ((s8[14680064]{0:T(1024)(128)(4,1)}), s8[4194304]{0:T(1024)(128)(4,1)S(1)}, s32[]{:S(2)}) async-start(s8[14680064]{0:T(1024)(128)(4,1)} %bitcast.80), calls=%async_computation.10 | async-start | bytes 8388608
  40.1 4.5 %slice-start.6 = ((s8[14680064]{0:T(1024)(128)(4,1)}), s8[4194304]{0:T(1024)(128)(4,1)S(1)}, s32[]{:S(2)}) async-start(s8[14680064]{0:T(1024)(128)(4,1)} %bitcast.80), calls=%async_computation.11 | async-start | bytes 8388608
  40.1 5.1 %slice-start.7 = ((s8[14680064]{0:T(1024)(128)(4,1)}), s8[2097152]{0:T(1024)(128)(4,1)S(1)}, s32[]{:S(2)}) async-start(s8[14680064]{0:T(1024)(128)(4,1)} %bitcast.80), calls=%async_computation.12 | async-start | bytes 4194304
  48.6 2.3 copy-start.3
  48.6 2.3 copy-start.4
  94.1 2.1 copy-start.2
  96.1 1.7 copy-start.1
  97.9 1.8 copy-start
  102.4 181.2 %reduce-scatter.3.cloned.1.call-start = ((), (), s32[]{:S(2)}) async-start(), calls=%async_computation.2 | async-start | bytes 589824 | tf_op jit(solution)/shard_map/reduce_scatter | solution.py:74
  241.5 9.0 %copy-start.5 = (bf16[1,128,3584]{2,1,0:T(8,128)(2,1)S(1)}, bf16[1,128,3584]{2,1,0:T(8,128)(2,1)}, u32[]{:S(2)}) copy-start(bf16[1,128,3584]{2,1,0:T(8,128)(2,1)} %get-tuple-element.7) | copy-start | bytes 2752516
  241.5 9.0 %copy-start.6 = (bf16[1,128,3584]{2,1,0:T(8,128)(2,1)S(1)}, bf16[1,128,3584]{2,1,0:T(8,128)(2,1)}, u32[]{:S(2)}) copy-start(bf16[1,128,3584]{2,1,0:T(8,128)(2,1)} %get-tuple-element.8) | copy-start | bytes 2752516
  250.4 70.8 %reduce-scatter.5.cloned.1.call-start = ((), (), s32[]{:S(2)}) async-start(), calls=%async_computation.3 | async-start | bytes 589824 | tf_op jit(solution)/shard_map/reduce_scatter | solution.py:74
Sparse Core Ops, SparseCore 0:
  102.6 138.9 all-reduce.3
  250.6 33.0 reduce-scatter.2
  287.0 34.1 reduce-scatter.4
where the time goes:
time: 330 us; the launch traced here: 329 us
  waiting for transfers between devices  201 us (61%)
  blocking collectives  61.2 us (19%)
  matrix products  42.8 us (13%)
  between operations  13.3 us (4%)
  local copies, waits for them, and re-layouts  8.75 us (3%)
    psum x1, waiting for transfers between devices, process(): lax.psum(up_round, 'tensor').astype(jnp.float32)  139 us
    reduce_scatter x2, waiting for transfers between devices, process(): lax.psum_scatter(down_part.astype(jnp.bfloat16), 'dp', scatter_dimension=...  62.3 us
    psum x1, blocking collectives, process(): summed = lax.psum(packed, ('dp', 'tensor'))  40 us
    all_gather x2, blocking collectives, process(): gathered = lax.all_gather(features_in, 'dp', axis=1, tiled=True)  21.2 us
    dot_general x2, matrix products, process(): jnp.einsum('srf,fd->srd', hidden, down_weight, preferred_element_type=jnp...  17.2 us
    dot_general x2, matrix products, process(): jnp.einsum('srd,df->srf', gathered, gate_weight, preferred_element_type=j...  12 us
  transfers between devices with their start and end apart: 3, of which 3 were waited for; matrix products, arithmetic and copies ran while one was open for 3% of the time, Pallas kernels for 0%

commit v1 on v0

v1 whole, which is shorter than its diff:
```python
import functools
import jax
import jax.numpy as jnp
from jax import lax
from jax.experimental import pallas as pl
from jax.experimental.pallas import tpu as pltpu
from jax.sharding import PartitionSpec as P

SHARES = (2, 3, 3, 3, 2, 1)
EARLY = 2
LIMIT = 16 * 1024 * 1024
PROJECT_LIMIT = 50 * 1024 * 1024


def transposed_dot(lows, maps):
    return lax.dot_general(lows, maps, (((0,), (0,)), ((), ())), preferred_element_type=jnp.float32)


def exact_dot(left, right):
    return jnp.dot(
        left, right, precision=lax.Precision.HIGHEST, preferred_element_type=jnp.float32
    )


def local_order(home, rows, entries, dp, dp_index):
    entry = lax.broadcasted_iota(jnp.int32, (entries, entries), 0)
    target = lax.broadcasted_iota(jnp.int32, (entries, entries), 1)
    local_row = entry % rows
    slot = local_row // home
    relative = jnp.where(slot < dp // 2, 2 * slot, 2 * slot - dp + 1)
    true_row = jnp.bitwise_xor(relative, dp_index) * home + local_row % home
    return (entry - local_row + true_row == target).astype(jnp.float32)


def shrink_kernel(home, dp, where_ref, scale_ref, x_ref, shrink_ref, ids_ref, *rest):
    out_ref = rest[-1]
    entries = x_ref.shape[0]
    wide = out_ref.shape[0]
    owner = where_ref[0]
    shrunk = lax.dot_general(
        shrink_ref[...], x_ref[...], (((0,), (1,)), ((), ())), preferred_element_type=jnp.float32
    )
    total = jnp.zeros(out_ref.shape, jnp.float32)
    order = local_order(home, home * dp, entries, dp, owner)
    ordered = exact_dot(shrunk, order)
    held = scale_ref.shape[0]
    for a in range(held):
        mine = jnp.where(ids_ref[...] == owner * held + a, scale_ref[a], 0.0)
        total = total + ordered[wide * a : wide * (a + 1)] * mine
    out_ref[...] = total


def lows_kernel(home, dp, count, rank, adapters, where_ref, ids_ref, *refs):
    low = refs[0][...]
    for ref in refs[1:count]:
        low = low + ref[...]
    out_ref = refs[-1]
    entries = low.shape[1]
    low = low.astype(jnp.bfloat16).astype(jnp.float32)
    order = local_order(home, home * dp, entries, dp, where_ref[0]).astype(jnp.bfloat16)
    depth = adapters * rank
    holder = lax.broadcasted_iota(jnp.int32, (depth, entries), 0) // rank
    for place in range(out_ref.shape[1] // depth):
        member = ids_ref[...] == where_ref[1 + place] * adapters + holder
        for j in range(2):
            tiled = jnp.concatenate([low[rank * j : rank * (j + 1)]] * adapters, axis=0)
            chosen = jnp.where(member, tiled, 0.0).astype(jnp.bfloat16)
            out_ref[j, depth * place : depth * (place + 1)] = lax.dot_general(
                chosen, order, (((1,), (1,)), ((), ())), preferred_element_type=jnp.float32
            ).astype(jnp.bfloat16)


def project_kernel(with_lows, x_ref, gate_ref, up_ref, *rest):
    out_ref = rest[-1]
    for j, weight_ref in enumerate((gate_ref, up_ref)):
        value = jnp.dot(x_ref[...], weight_ref[...], preferred_element_type=jnp.float32)
        if with_lows:
            depth = rest[1].shape[1]
            value = value + transposed_dot(rest[0][j, :depth], rest[1][j])
        out_ref[j] = value.astype(out_ref.dtype)


def fold_kernel(tile, first, maps, part_ref, got_ref, *rest):
    out_ref = rest[-1]
    for lo in range(0, out_ref.shape[2], tile):
        cols = slice(lo, lo + tile)
        for j in range(2):
            value = part_ref[j, :, cols].astype(jnp.float32) + got_ref[j, :, cols].astype(jnp.float32)
            for n in range(maps):
                depth = rest[1 + n].shape[1]
                value = value + transposed_dot(
                    rest[0][j, depth * n : depth * (n + 1)],
                    rest[1 + n][j, :, first + lo : first + lo + tile],
                )
            out_ref[j, :, cols] = value.astype(out_ref.dtype)


def hidden_kernel(tile, part_ref, *rest):
    out_ref = rest[-1]
    for lo in range(0, out_ref.shape[1], tile):
        cols = slice(lo, lo + tile)
        gate, up = part_ref[0, :, cols].astype(jnp.float32), part_ref[1, :, cols].astype(jnp.float32)
        if rest[0].shape == part_ref.shape:
            gate = gate + rest[0][0, :, cols].astype(jnp.float32)
            up = up + rest[0][1, :, cols].astype(jnp.float32)
        out_ref[:, cols] = (gate / (1.0 + jnp.exp(-gate)) * up).astype(out_ref.dtype)


def per_device(
    activations,
    gate_weight,
    up_weight,
    down_weight,
    shrink_weight,
    expand_weight,
    adapter_scale,
    adapter_ids,
):
    f32, bf16 = jnp.float32, jnp.bfloat16
    dp, tp = lax.axis_size("dp"), lax.axis_size("tensor")
    dp_index, tp_index = lax.axis_index("dp"), lax.axis_index("tensor")
    steps, home, feat = activations.shape
    rows = home * dp
    entries = steps * rows
    adp_block, low_rank, ff_local = expand_weight.shape[1:]
    depth = adp_block * low_rank
    out_feat = down_weight.shape[1]
    left = tp_index < tp // 2
    number = lambda value: jnp.asarray(value, jnp.int32).reshape(1)
    inner = tp // 2
    tile = 256 if ff_local % 256 == 0 else 128

    def dp_xor(value, k):
        return lax.ppermute(value, "dp", [(s, s ^ k) for s in range(dp)])

    def tp_send(value, pairs):
        return lax.ppermute(value, "tensor", pairs)

    def gated(value, *others):
        return lax.optimization_barrier((value,) + others)[0] if others else value

    groups, done, bounds = ff_local // tile, 0, [0]
    for share in SHARES:
        done += share
        bounds.append(groups * done // sum(SHARES) * tile)
    spans = [(lo, hi) for lo, hi in zip(bounds[:-1], bounds[1:]) if hi > lo]
    widths = [hi - lo for lo, hi in spans]
    count = len(spans)
    fold = [[(s, s + 1), (tp - 1 - s, tp - 2 - s)] for s in range(inner - 1)]
    across = [(inner - 1, inner), (inner, inner - 1)]
    unfold = [[(inner - 1 - s, inner - 2 - s), (inner + s, inner + s + 1)] for s in range(inner - 1)]

    params = pltpu.CompilerParams(vmem_limit_bytes=LIMIT)
    scalar = pl.BlockSpec(memory_space=pltpu.SMEM)
    anywhere = pl.BlockSpec(memory_space=pl.ANY)

    def whole(value):
        return pl.BlockSpec(value.shape, lambda *t: (0,) * value.ndim)

    def cost(flops, nbytes):
        return pl.CostEstimate(flops=1, bytes_accessed=1, transcendentals=0)

    even = [activations] + [dp_xor(activations, k) for k in range(2, dp, 2)]
    odd = [dp_xor(value, 1) for value in even]
    x_all = jnp.concatenate(even + odd, axis=1).reshape(entries, feat)

    expand = expand_weight.reshape(2, depth, ff_local)
    early = min(EARLY, count - 1)
    maps = [expand[:, :, : spans[early - 1][1]]]
    maps.append(tp_send(maps[0], fold[0]))
    blocks = [tp_index, jnp.where(left, tp_index - 1, tp_index + 1)]

    def project(c, *after):
        lo, hi = spans[c]
        wide = 2 * tile if lo % (2 * tile) == 0 and hi % (2 * tile) == 0 else tile
        first = lo // wide
        weights = pl.BlockSpec((feat, wide), lambda t: (0, first + t))
        operands, specs = [x_all, gate_weight, up_weight], [whole(x_all), weights, weights]
        if c >= early:
            operands += [lows, expand]
            specs += [whole(lows), pl.BlockSpec((2, depth, wide), lambda t: (0, 0, first + t))]
        return pl.pallas_call(
            functools.partial(project_kernel, c >= early),
            grid=((hi - lo) // wide,),
            in_specs=specs + [anywhere] * len(after),
            out_specs=pl.BlockSpec((2, entries, wide), lambda t: (0, 0, t)),
            out_shape=jax.ShapeDtypeStruct((2, entries, hi - lo), bf16),
            compiler_params=pltpu.CompilerParams(vmem_limit_bytes=PROJECT_LIMIT),
            cost_estimate=cost(4 * entries * feat * (hi - lo), 8 * feat * (hi - lo)),
            name="project",
        )(*operands, *after)

    global_ids = jnp.tile(adapter_ids, (steps,)).reshape(1, entries)
    partial = pl.pallas_call(
        functools.partial(shrink_kernel, home, dp),
        in_specs=[scalar, scalar, whole(x_all), whole(shrink_weight), whole(global_ids)],
        out_specs=pl.BlockSpec((2 * low_rank, entries), lambda: (0, 0)),
        out_shape=jax.ShapeDtypeStruct((2 * low_rank, entries), f32),
        compiler_params=params,
        cost_estimate=cost(2**27, 2**21),
        name="shrink",
    )(number(dp_index), adapter_scale, x_all, shrink_weight, global_ids)
    low = functools.reduce(
        jnp.add, [partial] + [tp_send(partial, [(s, s ^ k) for s in range(tp)]) for k in range(1, tp)]
    )
    parts = {0: project(0, low)}
    first_got = {0: tp_send(parts[0], fold[0])}
    low = functools.reduce(
        jnp.add, [gated(low, parts[0])] + [dp_xor(low, k) for k in range(2, dp, 2)]
    )
    for c in range(1, early):
        parts[c] = project(c, low, maps[1])
        first_got[c] = tp_send(parts[c], fold[0])
    pieces = [low, dp_xor(low, 1)]
    lows = pl.pallas_call(
        functools.partial(lows_kernel, home, dp, len(pieces), low_rank, adp_block),
        in_specs=[scalar, whole(global_ids)] + [whole(low)] * len(pieces),
        out_specs=pl.BlockSpec((2, len(blocks) * depth, entries), lambda: (0, 0, 0)),
        out_shape=jax.ShapeDtypeStruct((2, len(blocks) * depth, entries), bf16),
        compiler_params=params,
        cost_estimate=cost(2**27, 2**20),
        name="lows",
    )(
        jnp.concatenate([number(dp_index)] + [number(block) for block in blocks]), global_ids, *pieces
    )

    def small(kernel, name, shape, operands, *after):
        return pl.pallas_call(
            kernel,
            in_specs=[whole(value) for value in operands] + [anywhere] * len(after),
            out_specs=pl.BlockSpec(shape, lambda: (0,) * len(shape)),
            out_shape=jax.ShapeDtypeStruct(shape, bf16),
            compiler_params=params,
            cost_estimate=cost(2**24, 2**22),
            name=name,
        )(*operands, *after)

    folded, cross_got, hiddens, full_got = {}, {}, {}, {}

    def stage_fold(c, *after):
        part = parts[c]
        for s, pairs in enumerate(fold):
            got = first_got[c] if s == 0 else tp_send(part, pairs)
            extra = [lows] + maps if c < early and s == 0 else []
            part = small(
                functools.partial(fold_kernel, tile, spans[c][0], len(extra[1:])),
                "fold",
                part.shape,
                [part, got] + extra,
                *after,
            )
        folded[c] = part
        cross_got[c] = tp_send(part, across)

    def stage_hidden(c, *after):
        hidden = small(
            functools.partial(hidden_kernel, tile),
            "hidden",
            (entries, widths[c]),
            [folded[c], cross_got[c]],
            *after,
        )
        hiddens[c] = hidden
        for s, pairs in enumerate(unfold):
            got = tp_send(hidden, pairs)
            if s < len(unfold) - 1:
                fresh = (tp_index == inner - 2 - s) | (tp_index == inner + s + 1)
                hidden = jnp.where(fresh, got, hidden)
        full_got[c] = (hidden, got)

    def down(c, hidden, total, *after):
        value = jnp.dot(gated(hidden, *after), down_weight[slice(*spans[c])], preferred_element_type=f32)
        return value if total is None else total + value

    outermost = (tp_index == 0) | (tp_index == tp - 1)

    def stage_down(c, total, *after):
        hidden, got = full_got[c]
        return down(c, jnp.where(outermost, gated(got, *after), hidden), total)

    latest, total = [], None
    for t in range(count + 2):
        if t < count:
            stage_fold(t, *latest)
            latest = [folded[t]]
        if t + 2 < count:
            if t == 0:
                parts[2] = project(2, folded[0])
                latest = [parts[2]]
            first_got[t + 2] = tp_send(gated(parts[t + 2], folded[t]), fold[0])
        if t + 3 < count:
            parts[t + 3] = project(t + 3, *latest)
            latest = [parts[t + 3]]
        for c in (t - 1, t):
            ahead = c + 1 < count and widths[c + 1] > widths[c]
            if 0 <= c < count and ahead == (c == t):
                stage_hidden(c, *latest)
                latest = [hiddens[c]]
        if t >= 2:
            total = stage_down(t - 2, total, *latest)
            latest = [total]

    total = total.reshape(steps, rows, out_feat)
    got = dp_xor(total[:, rows // 2 :].astype(bf16), 1)
    pair = total[:, : rows // 2] + got.astype(f32)
    pair_sent = pair.astype(bf16)
    mixed = pair[:, :home]
    for e in range(1, dp // 2):
        mixed = mixed + dp_xor(pair_sent[:, e * home : (e + 1) * home], 2 * e).astype(f32)
    mixed = mixed.astype(bf16)
    return mixed


def solution(mesh):
    placed = (
        P(None, "dp", "tensor"),
        P("tensor", "dp"),
        P("tensor", "dp"),
        P("dp", "tensor"),
        P("tensor", "dp"),
        P(None, "tensor", None, "dp"),
        P("dp"),
        P(),
    )
    return jax.shard_map(
        per_device, mesh=mesh, in_specs=placed, out_specs=P(None, "dp", "tensor"), check_vma=False
    )
```

time: 330 us -> 162 us (0.49)
  waiting for transfers between devices: 201 us -> 46.7 us
  blocking collectives: 61.2 us -> 0 us
  starting transfers between devices: 0.09 us -> 58.4 us
  Pallas kernels: 0 us -> 37.1 us
  matrix products: 42.8 us -> 15.2 us
  between operations: 13.3 us -> 0.52 us
  local copies, waits for them, and re-layouts: 8.75 us -> 2.39 us
    psum x1 -> x0, waiting for transfers between devices: 139 us -> none  [process(): lax.psum(up_round, 'tensor').astype(jnp.float32)]
    reduce_scatter x2 -> x0, waiting for transfers between devices: 62.3 us -> none  [process(): lax.psum_scatter(down_part.astype(jnp.bfloat16), 'dp', scatter_dimension=...]
    ppermute x0 -> x37, starting transfers between devices: none -> 58.4 us  [the longest x22 45.9 us: tp_send(): return lax.ppermute(value, 'tensor', pairs)]
    ppermute x0 -> x37, waiting for transfers between devices: none -> 46.7 us  [the longest x22 33.2 us: tp_send(): return lax.ppermute(value, 'tensor', pairs)]
    psum x1 -> x0, blocking collectives: 40 us -> none  [process(): summed = lax.psum(packed, ('dp', 'tensor'))]
    pallas_call x0 -> x20, Pallas kernels: none -> 37.1 us  [the longest x6 24.9 us: project(): pl.pallas_call(functools.partial(project_kernel, c >= early), grid=((hi -...]
    dot_general x14 -> x6, matrix products: 42.8 us -> 15.2 us  [down(): jnp.dot(gated(hidden, *after), down_weight[slice(*spans[c])], preferred_e...]
    all_gather x2 -> x0, blocking collectives: 21.2 us -> none  [process(): gathered = lax.all_gather(features_in, 'dp', axis=1, tiled=True)]
  transfers between devices with their start and end apart: 3 -> 37, of which waited for: 3 -> 19; matrix products, arithmetic and copies ran while one was open for 3% -> 10% of each run, Pallas kernels for 0% -> 23%
where the time goes in v1:
time: 162 us; the launch traced here: 161 us
  starting transfers between devices  58.4 us (36%)
  waiting for transfers between devices  46.7 us (29%)
  Pallas kernels  37.1 us (23%)
  matrix products  15.2 us (9%)
  local copies, waits for them, and re-layouts  2.39 us (1%)
    ppermute x22, starting transfers between devices, tp_send(): return lax.ppermute(value, 'tensor', pairs)  45.9 us
    ppermute x22, waiting for transfers between devices, tp_send(): return lax.ppermute(value, 'tensor', pairs)  33.2 us
    pallas_call x6, Pallas kernels, project(): pl.pallas_call(functools.partial(project_kernel, c >= early), grid=((hi -...  24.9 us
    dot_general x6, matrix products, down(): jnp.dot(gated(hidden, *after), down_weight[slice(*spans[c])], preferred_e...  15.2 us
    ppermute x15, waiting for transfers between devices, dp_xor(): return lax.ppermute(value, 'dp', [(s, s ^ k) for s in range(dp)])  13.4 us
    ppermute x15, starting transfers between devices, dp_xor(): return lax.ppermute(value, 'dp', [(s, s ^ k) for s in range(dp)])  12.5 us
    pallas_call x12, Pallas kernels, small(): pl.pallas_call(kernel, in_specs=[whole(value) for value in operands] + [a...  9.97 us
  transfers between devices with their start and end apart: 37, of which 19 were waited for; matrix products, arithmetic and copies ran while one was open for 10% of the time, Pallas kernels for 23%

profile of v1, /device:TPU:0, one launch (start us, length us, event | category | flops | bytes accessed | tf_op | source)
XLA Modules:
  0.0 161.4 jit_solution(15804336006673353989)
XLA Ops:
  0.0 3.0 %collective-permute-start = (bf16[2,16,2048]{2,1,0:T(8,128)(2,1)}, bf16[2,16,2048]{2,1,0:T(8,128)(2,1)S(1)}, u32[]{:S(2)}, u32[]{:S(2)}) collective-permute-start(bf16[2,16,2048]{2,1,0:T(8,128)(2,1)} %param.8), channel_id=1, source_target_pairs={{0,8},{4,12},{8,0},{12,4},{16,24},{20,28},{24,16},{28,20},{1,9},{5... | collective-permute-start | bytes 393224 | tf_op jit(solution)/shard_map/ppermute | solution.py:134
  3.0 1.5 collective-permute-start.1
  4.6 1.1 slice.53.rest_1_
  5.7 4.0 %collective-permute-start.15 = (bf16[2,128,1280]{2,1,0:T(8,128)(2,1)S(1)}, bf16[2,128,1280]{2,1,0:T(8,128)(2,1)S(1)}, u32[]{:S(2)}, u32[]{:S(2)}) collective-permute-start(bf16[2,128,1280]{2,1,0:T(8,128)(2,1)S(1)} %slice.53.rest_1_), channel_id=1, source_target_pairs={{0,1},{3,2},{4,5},{7,6},{8,9},{11,10},{12,13},{15,14},{16,17},{19,... | collective-permute-start | bytes 1966088 | tf_op jit(solution)/shard_map/ppermute | solution.py:137
  9.7 0.9 constant_dynamic-update-slice_fusion.7
  12.8 1.4 shrink.1
  14.2 1.5 collective-permute-start.7
  15.7 2.6 %collective-permute-start.8 = (f32[32,256]{1,0:T(8,128)S(1)}, f32[32,256]{1,0:T(8,128)S(1)}, u32[]{:S(2)}, u32[]{:S(2)}) collective-permute-start(f32[32,256]{1,0:T(8,128)S(1)} %shrink.1), channel_id=1, source_target_pairs={{0,2},{1,3},{2,0},{3,1},{4,6},{5,7},{6,4},{7,5},{8,10},{9,11},{10,... | collective-permute-start | bytes 98312 | tf_op jit(solution)/shard_map/ppermute | solution.py:137
  18.6 6.7 %collective-permute-done.7 = f32[32,256]{1,0:T(8,128)S(1)} collective-permute-done((f32[32,256]{1,0:T(8,128)S(1)}, f32[32,256]{1,0:T(8,128)S(1)}, u32[]{:S(2)}, u32[]{:S(2)}) %collective-permute-start.7) | collective-permute-done | bytes 32800 | tf_op jit(solution)/shard_map/ppermute | solution.py:137
  25.4 0.7 collective-permute-done.8
  26.1 3.2 %collective-permute-done.9 = f32[32,256]{1,0:T(8,128)S(1)} collective-permute-done((f32[32,256]{1,0:T(8,128)S(1)}, f32[32,256]{1,0:T(8,128)S(1)}, u32[]{:S(2)}, u32[]{:S(2)}) %collective-permute-start.9) | collective-permute-done | bytes 32800 | tf_op jit(solution)/shard_map/ppermute | solution.py:137
  29.3 4.3 %project.6.part_ref = bf16[2,256,512]{2,1,0:T(8,128)(2,1)} custom-call(bf16[256,2048]{1,0:T(8,128)(2,1)S(1)} %bitcast.8, bf16[2048,3584]{1,0:T(8,128)(2,1)} %gate_ref.11, bf16[2048,3584]{1,0:T(8,128)(2,1)} %up_ref.11, f32[32,256]{1,0:T(8,128)S(1)} %add_add_fusion.1.rest_0_), custom_call_target="tpu_custom_call" | custom-call | flops 1 | bytes 1 | tf_op jit(solution)/shard_map/project/pallas_call | solution.py:182
  33.6 2.9 %collective-permute-start.10 = (bf16[2,256,512]{2,1,0:T(8,128)(2,1)}, bf16[2,256,512]{2,1,0:T(8,128)(2,1)}, u32[]{:S(2)}, u32[]{:S(2)}) collective-permute-start(bf16[2,256,512]{2,1,0:T(8,128)(2,1)} %project.6.part_ref), channel_id=1, source_target_pairs={{0,1},{3,2},{4,5},{7,6},{8,9},{11,10},{12,13},{15,14},{16,17},{19,... | collective-permute-start | bytes 1572872 | tf_op jit(solution)/shard_map/ppermute | solution.py:137
  36.5 1.5 collective-permute-start.11
  38.0 1.5 collective-permute-start.12
  40.6 1.5 collective-permute-done.12
  42.1 2.3 %collective-permute-done.13 = f32[32,256]{1,0:T(8,128)S(1)} collective-permute-done((f32[32,256]{1,0:T(8,128)S(1)}, f32[32,256]{1,0:T(8,128)S(1)}, u32[]{:S(2)}, u32[]{:S(2)}) %collective-permute-start.13) | collective-permute-done | bytes 32800 | tf_op jit(solution)/shard_map/ppermute | solution.py:134
  44.4 4.6 %project.9.part_ref = bf16[2,256,768]{2,1,0:T(8,128)(2,1)S(1)} custom-call(bf16[256,2048]{1,0:T(8,128)(2,1)S(1)} %bitcast.9, bf16[2048,3584]{1,0:T(8,128)(2,1)} %gate_ref.11, bf16[2048,3584]{1,0:T(8,128)(2,1)} %up_ref.11, f32[32,256]{1,0:T(8,128)S(1)} %add_add_fusion.refs_0_.rest_0_, bf16[2,128,1280]{2,1,0:T(8,128)(2,1)S(1)} %collective-permute-done.15.rest_2_.rest_1_), custom_call_target="tpu_custom_call" | custom-call | flops 1 | bytes 1 | tf_op jit(solution)/shard_map/project/pallas_call | solution.py:182
  49.0 2.2 %collective-permute-start.18 = (bf16[2,256,768]{2,1,0:T(8,128)(2,1)S(1)}, bf16[2,256,768]{2,1,0:T(8,128)(2,1)}, u32[]{:S(2)}, u32[]{:S(2)}) collective-permute-start(bf16[2,256,768]{2,1,0:T(8,128)(2,1)S(1)} %project.9.part_ref), channel_id=1, source_target_pairs={{0,1},{3,2},{4,5},{7,6},{8,9},{11,10},{12,13},{15,14},{16,17},{19,... | collective-permute-start | bytes 2359304 | tf_op jit(solution)/shard_map/ppermute | solution.py:137
  51.2 1.1 collective-permute-done.14.refs_1_
  52.4 0.9 lows.1.rest_0_
  53.2 1.7 %fold.6.rest_2_.part_ref = bf16[2,256,512]{2,1,0:T(8,128)(2,1)S(1)} custom-call(bf16[2,256,512]{2,1,0:T(8,128)(2,1)} %project.6.part_ref, bf16[2,256,512]{2,1,0:T(8,128)(2,1)} %collective-permute-done.10.got_ref, bf16[2,256,256]{2,1,0:T(8,128)(2,1)S(1)} %lows.1.rest_0_, bf16[2,128,1280]{2,1,0:T(8,128)(2,1)S(1)} %slice.53.rest_1_, ...), custom_call_target="tpu_custom_call" | custom-call | flops 1 | bytes 1 | tf_op jit(solution)/shard_map/fold/pallas_call | solution.py:228
  54.9 0.7 collective-permute-start.16
  55.6 4.8 %project.7.rest_2_.part_ref = bf16[2,256,768]{2,1,0:T(8,128)(2,1)S(1)} custom-call(bf16[256,2048]{1,0:T(8,128)(2,1)S(1)} %bitcast.10, bf16[2048,3584]{1,0:T(8,128)(2,1)} %gate_ref.11, bf16[2048,3584]{1,0:T(8,128)(2,1)} %up_ref.11, bf16[2,256,256]{2,1,0:T(8,128)(2,1)S(1)} %lows.1.rest_0_, bf16[2,128,3584]{2,1,0:T(8,128)(2,1)} %bitcast.17, ...), custom_call_target="tpu_custom_call" | custom-call | flops 1 | bytes 1 | tf_op jit(solution)/shard_map/project/pallas_call | solution.py:182
  60.5 1.5 collective-permute-start.20
  61.9 5.6 %project.8.rest_1_.part_ref = bf16[2,256,768]{2,1,0:T(8,128)(2,1)} custom-call(bf16[256,2048]{1,0:T(8,128)(2,1)S(1)} %bitcast.11, bf16[2048,3584]{1,0:T(8,128)(2,1)} %gate_ref.11, bf16[2048,3584]{1,0:T(8,128)(2,1)} %up_ref.11, bf16[2,256,256]{2,1,0:T(8,128)(2,1)S(1)} %lows.1.rest_0_, bf16[2,128,3584]{2,1,0:T(8,128)(2,1)} %bitcast.18, ...), custom_call_target="tpu_custom_call" | custom-call | flops 1 | bytes 1 | tf_op jit(solution)/shard_map/project/pallas_call | solution.py:182
  67.5 0.9 hidden.6.rest_3_
  68.7 1.7 %fold.7.rest_2_.part_ref = bf16[2,256,768]{2,1,0:T(8,128)(2,1)S(1)} custom-call(bf16[2,256,768]{2,1,0:T(8,128)(2,1)S(1)} %copy-done.1, bf16[2,256,768]{2,1,0:T(8,128)(2,1)} %collective-permute-done.18.got_ref, bf16[2,256,256]{2,1,0:T(8,128)(2,1)S(1)} %lows.1.rest_0_, bf16[2,128,1280]{2,1,0:T(8,128)(2,1)S(1)} %slice.53.rest_1_, ...), custom_call_target="tpu_custom_call" | custom-call | flops 1 | bytes 1 | tf_op jit(solution)/shard_map/fold/pallas_call | solution.py:228
  70.4 1.6 collective-permute-start.19
  72.0 4.5 %collective-permute-start.23 = (bf16[2,256,768]{2,1,0:T(8,128)(2,1)}, bf16[2,256,768]{2,1,0:T(8,128)(2,1)}, u32[]{:S(2)}, u32[]{:S(2)}) collective-permute-start(bf16[2,256,768]{2,1,0:T(8,128)(2,1)} %project.8.rest_1_.part_ref), channel_id=1, source_target_pairs={{0,1},{3,2},{4,5},{7,6},{8,9},{11,10},{12,13},{15,14},{16,17},{19,... | collective-permute-start | bytes 2359304 | tf_op jit(solution)/shard_map/ppermute | solution.py:137
  76.5 1.3 collective-permute-start.17
  77.8 3.3 %project.10.rest_0_.part_ref = bf16[2,256,512]{2,1,0:T(8,128)(2,1)S(1)} custom-call(bf16[256,2048]{1,0:T(8,128)(2,1)S(1)} %bitcast.12, bf16[2048,3584]{1,0:T(8,128)(2,1)} %gate_ref.11, bf16[2048,3584]{1,0:T(8,128)(2,1)} %up_ref.11, bf16[2,256,256]{2,1,0:T(8,128)(2,1)S(1)} %lows.1.rest_0_, bf16[2,128,3584]{2,1,0:T(8,128)(2,1)} %bitcast.19, ...), custom_call_target="tpu_custom_call" | custom-call | flops 1 | bytes 1 | tf_op jit(solution)/shard_map/project/pallas_call | solution.py:182
  81.1 2.9 %collective-permute-done.20.got_ref = bf16[2,256,768]{2,1,0:T(8,128)(2,1)S(1)} collective-permute-done((bf16[2,256,768]{2,1,0:T(8,128)(2,1)S(1)}, bf16[2,256,768]{2,1,0:T(8,128)(2,1)S(1)}, u32[]{:S(2)}, u32[]{:S(2)}) %collective-permute-start.20) | collective-permute-done | bytes 786464 | tf_op jit(solution)/shard_map/ppermute | solution.py:137
  84.2 1.6 collective-permute-start.22
  85.7 2.4 %project.11.rest_1_.part_ref = bf16[2,256,256]{2,1,0:T(8,128)(2,1)S(1)} custom-call(bf16[256,2048]{1,0:T(8,128)(2,1)S(1)} %bitcast.13, bf16[2048,3584]{1,0:T(8,128)(2,1)} %gate_ref.11, bf16[2048,3584]{1,0:T(8,128)(2,1)} %up_ref.11, bf16[2,256,256]{2,1,0:T(8,128)(2,1)S(1)} %lows.1.rest_0_, bf16[2,128,3584]{2,1,0:T(8,128)(2,1)} %bitcast.20, ...), custom_call_target="tpu_custom_call" | custom-call | flops 1 | bytes 1 | tf_op jit(solution)/shard_map/project/pallas_call | solution.py:182
  88.1 1.5 hidden.7
  89.6 1.3 collective-permute-start.21
  90.9 2.4 %fusion.16.rest_0_ = f32[256,2048]{1,0:T(8,128)S(1)} fusion(bf16[3584,2048]{1,0:T(8,128)(2,1)} %param.11, bf16[256,512]{1,0:T(8,128)(2,1)} %collective-permute-done.17, bf16[256,512]{1,0:T(8,128)(2,1)} %hidden.6.rest_3_, pred[]{:T(512)S(6)} %or.3), kind=kOutput, calls=%fused_computation.12 | convolution fusion | flops 537001984 | bytes 4718593 | tf_op jit(solution)/shard_map/dot_general | solution.py:272
  93.3 5.3 %collective-permute-done.23.got_ref = bf16[2,256,768]{2,1,0:T(8,128)(2,1)} collective-permute-done((bf16[2,256,768]{2,1,0:T(8,128)(2,1)}, bf16[2,256,768]{2,1,0:T(8,128)(2,1)}, u32[]{:S(2)}, u32[]{:S(2)}) %collective-permute-start.23) | collective-permute-done | bytes 786464 | tf_op jit(solution)/shard_map/ppermute | solution.py:137
  98.6 1.6 fold.9.rest_1_.part_ref
  100.1 0.7 collective-permute-start.25
  100.8 6.1 %collective-permute-start.26 = (bf16[2,256,512]{2,1,0:T(8,128)(2,1)S(1)}, bf16[2,256,512]{2,1,0:T(8,128)(2,1)S(1)}, u32[]{:S(2)}, u32[]{:S(2)}) collective-permute-start(bf16[2,256,512]{2,1,0:T(8,128)(2,1)S(1)} %project.10.rest_0_.part_ref), channel_id=1, source_target_pairs={{0,1},{3,2},{4,5},{7,6},{8,9},{11,10},{12,13},{15,14},{16,17},{19,... | collective-permute-start | bytes 1572872 | tf_op jit(solution)/shard_map/ppermute | solution.py:137
  106.9 1.5 hidden.8
  108.4 1.3 collective-permute-start.24
  109.7 2.9 %fusion.6.rest_0_ = f32[256,2048]{1,0:T(8,128)S(1)} fusion(f32[256,2048]{1,0:T(8,128)S(1)} %fusion.16.rest_0_, bf16[3584,2048]{1,0:T(8,128)(2,1)} %param.11, bf16[256,768]{1,0:T(8,128)(2,1)S(1)} %collective-permute-done.21, bf16[256,768]{1,0:T(8,128)(2,1)S(1)} %hidden.7, pred[]{:T(512)S(6)} %or.3), kind=kOutput, calls=%fused_computation.6 | convolution fusion | flops 806027264 | bytes 8126465 | tf_op jit(solution)/shard_map/dot_general | solution.py:272
  112.6 3.7 %collective-permute-done.26.got_ref = bf16[2,256,512]{2,1,0:T(8,128)(2,1)S(1)} collective-permute-done((bf16[2,256,512]{2,1,0:T(8,128)(2,1)S(1)}, bf16[2,256,512]{2,1,0:T(8,128)(2,1)S(1)}, u32[]{:S(2)}, u32[]{:S(2)}) %collective-permute-start.26) | collective-permute-done | bytes 524320 | tf_op jit(solution)/shard_map/ppermute | solution.py:137
  116.5 0.7 collective-permute-start.28
  117.2 6.5 %collective-permute-start.29 = (bf16[2,256,256]{2,1,0:T(8,128)(2,1)S(1)}, bf16[2,256,256]{2,1,0:T(8,128)(2,1)S(1)}, u32[]{:S(2)}, u32[]{:S(2)}) collective-permute-start(bf16[2,256,256]{2,1,0:T(8,128)(2,1)S(1)} %project.11.rest_1_.part_ref), channel_id=1, source_target_pairs={{0,1},{3,2},{4,5},{7,6},{8,9},{11,10},{12,13},{15,14},{16,17},{19,... | collective-permute-start | bytes 786440 | tf_op jit(solution)/shard_map/ppermute | solution.py:137
  124.0 1.5 collective-permute-start.27
  125.5 2.9 %fusion.9.rest_0_ = f32[256,2048]{1,0:T(8,128)S(1)} fusion(f32[256,2048]{1,0:T(8,128)S(1)} %fusion.6.rest_0_, bf16[3584,2048]{1,0:T(8,128)(2,1)} %param.11, bf16[256,768]{1,0:T(8,128)(2,1)S(1)} %collective-permute-done.24, bf16[256,768]{1,0:T(8,128)(2,1)S(1)} %hidden.8, pred[]{:T(512)S(6)} %or.3), kind=kOutput, calls=%fused_computation.7 | convolution fusion | flops 806027264 | bytes 8126465 | tf_op jit(solution)/shard_map/dot_general | solution.py:272
  128.6 0.7 collective-permute-start.31
  129.5 1.3 collective-permute-start.30
  130.8 4.4 %collective-permute-done.27 = bf16[256,768]{1,0:T(8,128)(2,1)S(1)} collective-permute-done((bf16[256,768]{1,0:T(8,128)(2,1)S(1)}, bf16[256,768]{1,0:T(8,128)(2,1)S(1)}, u32[]{:S(2)}, u32[]{:S(2)}) %collective-permute-start.27) | collective-permute-done | bytes 393248 | tf_op jit(solution)/shard_map/ppermute | solution.py:137
  135.2 2.9 %fusion.12.rest_1_ = f32[256,2048]{1,0:T(8,128)S(1)} fusion(f32[256,2048]{1,0:T(8,128)S(1)} %fusion.9.rest_0_, bf16[3584,2048]{1,0:T(8,128)(2,1)} %param.11, bf16[256,768]{1,0:T(8,128)(2,1)S(1)} %collective-permute-done.27, bf16[256,768]{1,0:T(8,128)(2,1)S(1)} %hidden.9, pred[]{:T(512)S(6)} %or.3), kind=kOutput, calls=%fused_computation.8 | convolution fusion | flops 806027264 | bytes 8126465 | tf_op jit(solution)/shard_map/dot_general | solution.py:272
  138.2 1.3 collective-permute-start.32
  139.5 6.3 %collective-permute-done.30 = bf16[256,512]{1,0:T(8,128)(2,1)S(1)} collective-permute-done((bf16[256,512]{1,0:T(8,128)(2,1)S(1)}, bf16[256,512]{1,0:T(8,128)(2,1)S(1)}, u32[]{:S(2)}, u32[]{:S(2)}) %collective-permute-start.30) | collective-permute-done | bytes 262176 | tf_op jit(solution)/shard_map/ppermute | solution.py:137
  145.9 2.3 %convolution_add_fusion = f32[256,2048]{1,0:T(8,128)S(1)} fusion(f32[256,2048]{1,0:T(8,128)S(1)} %fusion.12.rest_1_, bf16[3584,2048]{1,0:T(8,128)(2,1)} %param.11, bf16[256,512]{1,0:T(8,128)(2,1)S(1)} %collective-permute-done.30, bf16[256,512]{1,0:T(8,128)(2,1)S(1)} %hidden.10, pred[]{:T(512)S(6)} %or.3), kind=kOutput, calls=%fused_computation.9 | convolution fusion | flops 537526272 | bytes 6815745 | tf_op jit(solution)/shard_map/dot_general | solution.py:272
  148.2 1.7 %convolution_add_fusion.1 = f32[256,2048]{1,0:T(8,128)S(1)} fusion(f32[256,2048]{1,0:T(8,128)S(1)} %convolution_add_fusion, bf16[3584,2048]{1,0:T(8,128)(2,1)} %param.11, bf16[256,256]{1,0:T(8,128)(2,1)S(1)} %collective-permute-done.32, bf16[256,256]{1,0:T(8,128)(2,1)S(1)} %hidden.11, pred[]{:T(512)S(6)} %or.3), kind=kOutput, calls=%fused_computation.10 | convolution fusion | flops 269025280 | bytes 5505025 | tf_op jit(solution)/shard_map/dot_general | solution.py:272
  150.1 1.9 %collective-permute-done.33 = bf16[2,64,2048]{2,1,0:T(8,128)(2,1)S(1)} collective-permute-done((bf16[2,64,2048]{2,1,0:T(8,128)(2,1)S(1)}, bf16[2,64,2048]{2,1,0:T(8,128)(2,1)S(1)}, u32[]{:S(2)}, u32[]{:S(2)}) %collective-permute-start.33) | collective-permute-done | bytes 524320 | tf_op jit(solution)/shard_map/ppermute | solution.py:134
  152.4 1.0 collective-permute-start.35
  153.5 2.2 %collective-permute-start.36 = (bf16[2,16,2048]{2,1,0:T(8,128)(2,1)S(1)}, bf16[2,16,2048]{2,1,0:T(8,128)(2,1)S(1)}, u32[]{:S(2)}, u32[]{:S(2)}) collective-permute-start(bf16[2,16,2048]{2,1,0:T(8,128)(2,1)S(1)} %get-tuple-element.30), channel_id=1, source_target_pairs={{0,24},{4,28},{8,16},{12,20},{16,8},{20,12},{24,0},{28,4},{1,25},{... | collective-permute-start | bytes 393224 | tf_op jit(solution)/shard_map/ppermute | solution.py:134
  155.7 2.9 %collective-permute-done.34 = bf16[2,16,2048]{2,1,0:T(8,128)(2,1)S(1)} collective-permute-done((bf16[2,16,2048]{2,1,0:T(8,128)(2,1)S(1)}, bf16[2,16,2048]{2,1,0:T(8,128)(2,1)S(1)}, u32[]{:S(2)}, u32[]{:S(2)}) %collective-permute-start.34) | collective-permute-done | bytes 131104 | tf_op jit(solution)/shard_map/ppermute | solution.py:134
  158.6 2.1 %collective-permute-done.35 = bf16[2,16,2048]{2,1,0:T(8,128)(2,1)S(1)} collective-permute-done((bf16[2,16,2048]{2,1,0:T(8,128)(2,1)S(1)}, bf16[2,16,2048]{2,1,0:T(8,128)(2,1)S(1)}, u32[]{:S(2)}, u32[]{:S(2)}) %collective-permute-start.35) | collective-permute-done | bytes 131104 | tf_op jit(solution)/shard_map/ppermute | solution.py:134
  160.6 0.7 fusion.27
  (63 shorter events, 5.5 us)
Async XLA Ops:
  0.0 12.7 %copy-start.4 = (s32[128]{0:T(128)S(1)}, s32[128]{0:T(128)}, u32[]{:S(2)}) copy-start(s32[128]{0:T(128)} %param.15) | copy-start | bytes 1540
  0.0 12.7 %copy-start.2 = (bf16[2048,128]{1,0:T(8,128)(2,1)S(1)}, bf16[2048,128]{1,0:T(8,128)(2,1)}, u32[]{:S(2)}) copy-start(bf16[2048,128]{1,0:T(8,128)(2,1)} %shrink_ref.1) | copy-start | bytes 1572868
  0.0 12.8 %copy-start.3 = (f32[4]{0:T(128)S(1)}, f32[4]{0:T(128)}, u32[]{:S(2)}) copy-start(f32[4]{0:T(128)} %scale_ref.1) | copy-start | bytes 52
  0.0 10.6 %collective-permute-start = (bf16[2,16,2048]{2,1,0:T(8,128)(2,1)}, bf16[2,16,2048]{2,1,0:T(8,128)(2,1)S(1)}, u32[]{:S(2)}, u32[]{:S(2)}) collective-permute-start(bf16[2,16,2048]{2,1,0:T(8,128)(2,1)} %param.8), channel_id=1, source_target_pairs={{0,8},{4,12},{8,0},{12,4},{16,24},{20,28},{24,16},{28,20},{1,9},{5... | collective-permute-start | bytes 393224 | tf_op jit(solution)/shard_map/ppermute | solution.py:134
  3.0 8.0 %collective-permute-start.1 = (bf16[2,16,2048]{2,1,0:T(8,128)(2,1)}, bf16[2,16,2048]{2,1,0:T(8,128)(2,1)S(1)}, u32[]{:S(2)}, u32[]{:S(2)}) collective-permute-start(bf16[2,16,2048]{2,1,0:T(8,128)(2,1)} %param.8), channel_id=1, source_target_pairs={{0,16},{4,20},{8,24},{12,28},{16,0},{20,4},{24,8},{28,12},{1,17},{... | collective-permute-start | bytes 393224 | tf_op jit(solution)/shard_map/ppermute | solution.py:134
  4.5 6.8 %collective-permute-start.2 = (bf16[2,16,2048]{2,1,0:T(8,128)(2,1)}, bf16[2,16,2048]{2,1,0:T(8,128)(2,1)S(1)}, u32[]{:S(2)}, u32[]{:S(2)}) collective-permute-start(bf16[2,16,2048]{2,1,0:T(8,128)(2,1)} %param.8), channel_id=1, source_target_pairs={{0,24},{4,28},{8,16},{12,20},{16,8},{20,12},{24,0},{28,4},{1,25},{... | collective-permute-start | bytes 393224 | tf_op jit(solution)/shard_map/ppermute | solution.py:134
  4.6 7.1 %collective-permute-start.3 = (bf16[2,16,2048]{2,1,0:T(8,128)(2,1)}, bf16[2,16,2048]{2,1,0:T(8,128)(2,1)S(1)}, u32[]{:S(2)}, u32[]{:S(2)}) collective-permute-start(bf16[2,16,2048]{2,1,0:T(8,128)(2,1)} %param.8), channel_id=1, source_target_pairs={{0,4},{4,0},{8,12},{12,8},{16,20},{20,16},{24,28},{28,24},{1,5},{5... | collective-permute-start | bytes 393224 | tf_op jit(solution)/shard_map/ppermute | solution.py:134
  5.7 38.7 %collective-permute-start.15 = (bf16[2,128,1280]{2,1,0:T(8,128)(2,1)S(1)}, bf16[2,128,1280]{2,1,0:T(8,128)(2,1)S(1)}, u32[]{:S(2)}, u32[]{:S(2)}) collective-permute-start(bf16[2,128,1280]{2,1,0:T(8,128)(2,1)S(1)} %slice.53.rest_1_), channel_id=1, source_target_pairs={{0,1},{3,2},{4,5},{7,6},{8,9},{11,10},{12,13},{15,14},{16,17},{19,... | collective-permute-start | bytes 1966088 | tf_op jit(solution)/shard_map/ppermute | solution.py:137
  10.6 1.4 collective-permute-start.4
  11.0 1.3 collective-permute-start.5
  11.3 1.4 collective-permute-start.6
  14.2 11.2 %collective-permute-start.7 = (f32[32,256]{1,0:T(8,128)S(1)}, f32[32,256]{1,0:T(8,128)S(1)}, u32[]{:S(2)}, u32[]{:S(2)}) collective-permute-start(f32[32,256]{1,0:T(8,128)S(1)} %shrink.1), channel_id=1, source_target_pairs={{0,1},{1,0},{2,3},{3,2},{4,5},{5,4},{6,7},{7,6},{8,9},{9,8},{10,11... | collective-permute-start | bytes 98312 | tf_op jit(solution)/shard_map/ppermute | solution.py:137
  15.7 10.4 %collective-permute-start.8 = (f32[32,256]{1,0:T(8,128)S(1)}, f32[32,256]{1,0:T(8,128)S(1)}, u32[]{:S(2)}, u32[]{:S(2)}) collective-permute-start(f32[32,256]{1,0:T(8,128)S(1)} %shrink.1), channel_id=1, source_target_pairs={{0,2},{1,3},{2,0},{3,1},{4,6},{5,7},{6,4},{7,5},{8,10},{9,11},{10,... | collective-permute-start | bytes 98312 | tf_op jit(solution)/shard_map/ppermute | solution.py:137
  18.3 11.0 %collective-permute-start.9 = (f32[32,256]{1,0:T(8,128)S(1)}, f32[32,256]{1,0:T(8,128)S(1)}, u32[]{:S(2)}, u32[]{:S(2)}) collective-permute-start(f32[32,256]{1,0:T(8,128)S(1)} %shrink.1), channel_id=1, source_target_pairs={{0,3},{1,2},{2,1},{3,0},{4,7},{5,6},{6,5},{7,4},{8,11},{9,10},{10,... | collective-permute-start | bytes 98312 | tf_op jit(solution)/shard_map/ppermute | solution.py:137
  33.6 19.6 %collective-permute-start.10 = (bf16[2,256,512]{2,1,0:T(8,128)(2,1)}, bf16[2,256,512]{2,1,0:T(8,128)(2,1)}, u32[]{:S(2)}, u32[]{:S(2)}) collective-permute-start(bf16[2,256,512]{2,1,0:T(8,128)(2,1)} %project.6.part_ref), channel_id=1, source_target_pairs={{0,1},{3,2},{4,5},{7,6},{8,9},{11,10},{12,13},{15,14},{16,17},{19,... | collective-permute-start | bytes 1572872 | tf_op jit(solution)/shard_map/ppermute | solution.py:137
  36.5 4.0 %collective-permute-start.11 = (f32[32,256]{1,0:T(8,128)S(1)}, f32[32,256]{1,0:T(8,128)S(1)}, u32[]{:S(2)}, u32[]{:S(2)}) collective-permute-start(f32[32,256]{1,0:T(8,128)S(1)} %add_add_fusion.1.rest_0_), channel_id=1, source_target_pairs={{0,8},{4,12},{8,0},{12,4},{16,24},{20,28},{24,16},{28,20},{1,9},{5... | collective-permute-start | bytes 98312 | tf_op jit(solution)/shard_map/ppermute | solution.py:134
  38.0 4.1 %collective-permute-start.12 = (f32[32,256]{1,0:T(8,128)S(1)}, f32[32,256]{1,0:T(8,128)S(1)}, u32[]{:S(2)}, u32[]{:S(2)}) collective-permute-start(f32[32,256]{1,0:T(8,128)S(1)} %add_add_fusion.1.rest_0_), channel_id=1, source_target_pairs={{0,16},{4,20},{8,24},{12,28},{16,0},{20,4},{24,8},{28,12},{1,17},{... | collective-permute-start | bytes 98312 | tf_op jit(solution)/shard_map/ppermute | solution.py:134
  39.5 4.8 %collective-permute-start.13 = (f32[32,256]{1,0:T(8,128)S(1)}, f32[32,256]{1,0:T(8,128)S(1)}, u32[]{:S(2)}, u32[]{:S(2)}) collective-permute-start(f32[32,256]{1,0:T(8,128)S(1)} %add_add_fusion.1.rest_0_), channel_id=1, source_target_pairs={{0,24},{4,28},{8,16},{12,20},{16,8},{20,12},{24,0},{28,4},{1,25},{... | collective-permute-start | bytes 98312 | tf_op jit(solution)/shard_map/ppermute | solution.py:134
  49.0 11.5 %copy-start = (bf16[2,256,768]{2,1,0:T(8,128)(2,1)}, bf16[2,256,768]{2,1,0:T(8,128)(2,1)S(1)}, u32[]{:S(2)}) copy-start(bf16[2,256,768]{2,1,0:T(8,128)(2,1)S(1)} %project.9.part_ref) | copy-start | bytes 2359300
  49.0 19.5 %collective-permute-start.18 = (bf16[2,256,768]{2,1,0:T(8,128)(2,1)S(1)}, bf16[2,256,768]{2,1,0:T(8,128)(2,1)}, u32[]{:S(2)}, u32[]{:S(2)}) collective-permute-start(bf16[2,256,768]{2,1,0:T(8,128)(2,1)S(1)} %project.9.part_ref), channel_id=1, source_target_pairs={{0,1},{3,2},{4,5},{7,6},{8,9},{11,10},{12,13},{15,14},{16,17},{19,... | collective-permute-start | bytes 2359304 | tf_op jit(solution)/shard_map/ppermute | solution.py:137
  51.2 1.2 collective-permute-start.14
  54.9 12.6 %collective-permute-start.16 = (bf16[2,256,512]{2,1,0:T(8,128)(2,1)S(1)}, bf16[2,256,512]{2,1,0:T(8,128)(2,1)S(1)}, u32[]{:S(2)}, u32[]{:S(2)}) collective-permute-start(bf16[2,256,512]{2,1,0:T(8,128)(2,1)S(1)} %fold.6.rest_2_.part_ref), channel_id=1, source_target_pairs={{1,2},{2,1},{5,6},{6,5},{9,10},{10,9},{13,14},{14,13},{17,18},{18,... | collective-permute-start | bytes 1572872 | tf_op jit(solution)/shard_map/ppermute | solution.py:137
  60.5 23.5 %collective-permute-start.20 = (bf16[2,256,768]{2,1,0:T(8,128)(2,1)S(1)}, bf16[2,256,768]{2,1,0:T(8,128)(2,1)S(1)}, u32[]{:S(2)}, u32[]{:S(2)}) collective-permute-start(bf16[2,256,768]{2,1,0:T(8,128)(2,1)S(1)} %project.7.rest_2_.part_ref), channel_id=1, source_target_pairs={{0,1},{3,2},{4,5},{7,6},{8,9},{11,10},{12,13},{15,14},{16,17},{19,... | collective-permute-start | bytes 2359304 | tf_op jit(solution)/shard_map/ppermute | solution.py:137
  67.5 1.1 copy-start.1
  70.4 17.7 %collective-permute-start.19 = (bf16[2,256,768]{2,1,0:T(8,128)(2,1)S(1)}, bf16[2,256,768]{2,1,0:T(8,128)(2,1)}, u32[]{:S(2)}, u32[]{:S(2)}) collective-permute-start(bf16[2,256,768]{2,1,0:T(8,128)(2,1)S(1)} %fold.7.rest_2_.part_ref), channel_id=1, source_target_pairs={{1,2},{2,1},{5,6},{6,5},{9,10},{10,9},{13,14},{14,13},{17,18},{18,... | collective-permute-start | bytes 2359304 | tf_op jit(solution)/shard_map/ppermute | solution.py:137
  72.0 26.6 %collective-permute-start.23 = (bf16[2,256,768]{2,1,0:T(8,128)(2,1)}, bf16[2,256,768]{2,1,0:T(8,128)(2,1)}, u32[]{:S(2)}, u32[]{:S(2)}) collective-permute-start(bf16[2,256,768]{2,1,0:T(8,128)(2,1)} %project.8.rest_1_.part_ref), channel_id=1, source_target_pairs={{0,1},{3,2},{4,5},{7,6},{8,9},{11,10},{12,13},{15,14},{16,17},{19,... | collective-permute-start | bytes 2359304 | tf_op jit(solution)/shard_map/ppermute | solution.py:137
  76.5 14.4 %collective-permute-start.17 = (bf16[256,512]{1,0:T(8,128)(2,1)}, bf16[256,512]{1,0:T(8,128)(2,1)}, u32[]{:S(2)}, u32[]{:S(2)}) collective-permute-start(bf16[256,512]{1,0:T(8,128)(2,1)} %hidden.6.rest_3_), channel_id=1, source_target_pairs={{1,0},{2,3},{5,4},{6,7},{9,8},{10,11},{13,12},{14,15},{17,16},{18,... | collective-permute-start | bytes 786440 | tf_op jit(solution)/shard_map/ppermute | solution.py:137
  84.2 22.7 %collective-permute-start.22 = (bf16[2,256,768]{2,1,0:T(8,128)(2,1)S(1)}, bf16[2,256,768]{2,1,0:T(8,128)(2,1)}, u32[]{:S(2)}, u32[]{:S(2)}) collective-permute-start(bf16[2,256,768]{2,1,0:T(8,128)(2,1)S(1)} %fold.8.rest_2_.part_ref), channel_id=1, source_target_pairs={{1,2},{2,1},{5,6},{6,5},{9,10},{10,9},{13,14},{14,13},{17,18},{18,... | collective-permute-start | bytes 2359304 | tf_op jit(solution)/shard_map/ppermute | solution.py:137
  89.6 20.1 %collective-permute-start.21 = (bf16[256,768]{1,0:T(8,128)(2,1)S(1)}, bf16[256,768]{1,0:T(8,128)(2,1)S(1)}, u32[]{:S(2)}, u32[]{:S(2)}) collective-permute-start(bf16[256,768]{1,0:T(8,128)(2,1)S(1)} %hidden.7), channel_id=1, source_target_pairs={{1,0},{2,3},{5,4},{6,7},{9,8},{10,11},{13,12},{14,15},{17,16},{18,... | collective-permute-start | bytes 1179656 | tf_op jit(solution)/shard_map/ppermute | solution.py:137
  100.1 23.6 %collective-permute-start.25 = (bf16[2,256,768]{2,1,0:T(8,128)(2,1)S(1)}, bf16[2,256,768]{2,1,0:T(8,128)(2,1)S(1)}, u32[]{:S(2)}, u32[]{:S(2)}) collective-permute-start(bf16[2,256,768]{2,1,0:T(8,128)(2,1)S(1)} %fold.9.rest_1_.part_ref), channel_id=1, source_target_pairs={{1,2},{2,1},{5,6},{6,5},{9,10},{10,9},{13,14},{14,13},{17,18},{18,... | collective-permute-start | bytes 2359304 | tf_op jit(solution)/shard_map/ppermute | solution.py:137
  100.8 15.5 %collective-permute-start.26 = (bf16[2,256,512]{2,1,0:T(8,128)(2,1)S(1)}, bf16[2,256,512]{2,1,0:T(8,128)(2,1)S(1)}, u32[]{:S(2)}, u32[]{:S(2)}) collective-permute-start(bf16[2,256,512]{2,1,0:T(8,128)(2,1)S(1)} %project.10.rest_0_.part_ref), channel_id=1, source_target_pairs={{0,1},{3,2},{4,5},{7,6},{8,9},{11,10},{12,13},{15,14},{16,17},{19,... | collective-permute-start | bytes 1572872 | tf_op jit(solution)/shard_map/ppermute | solution.py:137
  108.4 17.1 %collective-permute-start.24 = (bf16[256,768]{1,0:T(8,128)(2,1)S(1)}, bf16[256,768]{1,0:T(8,128)(2,1)S(1)}, u32[]{:S(2)}, u32[]{:S(2)}) collective-permute-start(bf16[256,768]{1,0:T(8,128)(2,1)S(1)} %hidden.8), channel_id=1, source_target_pairs={{1,0},{2,3},{5,4},{6,7},{9,8},{10,11},{13,12},{14,15},{17,16},{18,... | collective-permute-start | bytes 1179656 | tf_op jit(solution)/shard_map/ppermute | solution.py:137
  116.5 12.8 %collective-permute-start.28 = (bf16[2,256,512]{2,1,0:T(8,128)(2,1)S(1)}, bf16[2,256,512]{2,1,0:T(8,128)(2,1)S(1)}, u32[]{:S(2)}, u32[]{:S(2)}) collective-permute-start(bf16[2,256,512]{2,1,0:T(8,128)(2,1)S(1)} %fold.10.rest_1_.part_ref), channel_id=1, source_target_pairs={{1,2},{2,1},{5,6},{6,5},{9,10},{10,9},{13,14},{14,13},{17,18},{18,... | collective-permute-start | bytes 1572872 | tf_op jit(solution)/shard_map/ppermute | solution.py:137
  117.2 11.3 %collective-permute-start.29 = (bf16[2,256,256]{2,1,0:T(8,128)(2,1)S(1)}, bf16[2,256,256]{2,1,0:T(8,128)(2,1)S(1)}, u32[]{:S(2)}, u32[]{:S(2)}) collective-permute-start(bf16[2,256,256]{2,1,0:T(8,128)(2,1)S(1)} %project.11.rest_1_.part_ref), channel_id=1, source_target_pairs={{0,1},{3,2},{4,5},{7,6},{8,9},{11,10},{12,13},{15,14},{16,17},{19,... | collective-permute-start | bytes 786440 | tf_op jit(solution)/shard_map/ppermute | solution.py:137
  124.0 11.1 %collective-permute-start.27 = (bf16[256,768]{1,0:T(8,128)(2,1)S(1)}, bf16[256,768]{1,0:T(8,128)(2,1)S(1)}, u32[]{:S(2)}, u32[]{:S(2)}) collective-permute-start(bf16[256,768]{1,0:T(8,128)(2,1)S(1)} %hidden.9), channel_id=1, source_target_pairs={{1,0},{2,3},{5,4},{6,7},{9,8},{10,11},{13,12},{14,15},{17,16},{18,... | collective-permute-start | bytes 1179656 | tf_op jit(solution)/shard_map/ppermute | solution.py:137
  128.6 9.6 %collective-permute-start.31 = (bf16[2,256,256]{2,1,0:T(8,128)(2,1)S(1)}, bf16[2,256,256]{2,1,0:T(8,128)(2,1)S(1)}, u32[]{:S(2)}, u32[]{:S(2)}) collective-permute-start(bf16[2,256,256]{2,1,0:T(8,128)(2,1)S(1)} %fold.11.rest_1_.part_ref), channel_id=1, source_target_pairs={{1,2},{2,1},{5,6},{6,5},{9,10},{10,9},{13,14},{14,13},{17,18},{18,... | collective-permute-start | bytes 786440 | tf_op jit(solution)/shard_map/ppermute | solution.py:137
  129.5 16.4 %collective-permute-start.30 = (bf16[256,512]{1,0:T(8,128)(2,1)S(1)}, bf16[256,512]{1,0:T(8,128)(2,1)S(1)}, u32[]{:S(2)}, u32[]{:S(2)}) collective-permute-start(bf16[256,512]{1,0:T(8,128)(2,1)S(1)} %hidden.10), channel_id=1, source_target_pairs={{1,0},{2,3},{5,4},{6,7},{9,8},{10,11},{13,12},{14,15},{17,16},{18,... | collective-permute-start | bytes 786440 | tf_op jit(solution)/shard_map/ppermute | solution.py:137
  138.2 10.0 %collective-permute-start.32 = (bf16[256,256]{1,0:T(8,128)(2,1)S(1)}, bf16[256,256]{1,0:T(8,128)(2,1)S(1)}, u32[]{:S(2)}, u32[]{:S(2)}) collective-permute-start(bf16[256,256]{1,0:T(8,128)(2,1)S(1)} %hidden.11), channel_id=1, source_target_pairs={{1,0},{2,3},{5,4},{6,7},{9,8},{10,11},{13,12},{14,15},{17,16},{18,... | collective-permute-start | bytes 393224 | tf_op jit(solution)/shard_map/ppermute | solution.py:137
  150.0 2.0 %collective-permute-start.33 = (bf16[2,64,2048]{2,1,0:T(8,128)(2,1)S(1)}, bf16[2,64,2048]{2,1,0:T(8,128)(2,1)S(1)}, u32[]{:S(2)}, u32[]{:S(2)}) collective-permute-start(bf16[2,64,2048]{2,1,0:T(8,128)(2,1)S(1)} %slice.87), channel_id=1, source_target_pairs={{0,4},{4,0},{8,12},{12,8},{16,20},{20,16},{24,28},{28,24},{1,5},{5... | collective-permute-start | bytes 1572872 | tf_op jit(solution)/shard_map/ppermute | solution.py:134
  152.1 6.4 %collective-permute-start.34 = (bf16[2,16,2048]{2,1,0:T(8,128)(2,1)S(1)}, bf16[2,16,2048]{2,1,0:T(8,128)(2,1)S(1)}, u32[]{:S(2)}, u32[]{:S(2)}) collective-permute-start(bf16[2,16,2048]{2,1,0:T(8,128)(2,1)S(1)} %get-tuple-element.29), channel_id=1, source_target_pairs={{0,8},{4,12},{8,0},{12,4},{16,24},{20,28},{24,16},{28,20},{1,9},{5... | collective-permute-start | bytes 393224 | tf_op jit(solution)/shard_map/ppermute | solution.py:134
  152.4 8.2 %collective-permute-start.35 = (bf16[2,16,2048]{2,1,0:T(8,128)(2,1)S(1)}, bf16[2,16,2048]{2,1,0:T(8,128)(2,1)S(1)}, u32[]{:S(2)}, u32[]{:S(2)}) collective-permute-start(bf16[2,16,2048]{2,1,0:T(8,128)(2,1)S(1)} %get-tuple-element.31), channel_id=1, source_target_pairs={{0,16},{4,20},{8,24},{12,28},{16,0},{20,4},{24,8},{28,12},{1,17},{... | collective-permute-start | bytes 393224 | tf_op jit(solution)/shard_map/ppermute | solution.py:134
  153.5 7.2 %collective-permute-start.36 = (bf16[2,16,2048]{2,1,0:T(8,128)(2,1)S(1)}, bf16[2,16,2048]{2,1,0:T(8,128)(2,1)S(1)}, u32[]{:S(2)}, u32[]{:S(2)}) collective-permute-start(bf16[2,16,2048]{2,1,0:T(8,128)(2,1)S(1)} %get-tuple-element.30), channel_id=1, source_target_pairs={{0,24},{4,28},{8,16},{12,20},{16,8},{20,12},{24,0},{28,4},{1,25},{... | collective-permute-start | bytes 393224 | tf_op jit(solution)/shard_map/ppermute | solution.py:134

commit v2 on v1

--- a/solution.py
+++ b/solution.py
@@ -6,9 +6,11 @@
 from jax.experimental.pallas import tpu as pltpu
 from jax.sharding import PartitionSpec as P
 
-SHARES = (2, 3, 3, 3, 2, 1)
+SHARES = (1, 2, 3, 3, 3, 2)
+GROUPS = (1, 1, 1, 1, 1, 1, 1)
+AHEAD = (1, 1, 0, 0, 0)
 EARLY = 2
-LIMIT = 16 * 1024 * 1024
+LIMIT = 24 * 1024 * 1024
 PROJECT_LIMIT = 50 * 1024 * 1024
 
 
@@ -60,7 +62,7 @@
     order = local_order(home, home * dp, entries, dp, where_ref[0]).astype(jnp.bfloat16)
     depth = adapters * rank
     holder = lax.broadcasted_iota(jnp.int32, (depth, entries), 0) // rank
-    for place in range(out_ref.shape[1] // depth):
+    for place in range(2):
         member = ids_ref[...] == where_ref[1 + place] * adapters + holder
         for j in range(2):
             tiled = jnp.concatenate([low[rank * j : rank * (j + 1)]] * adapters, axis=0)
@@ -80,8 +82,8 @@
         out_ref[j] = value.astype(out_ref.dtype)
 
 
-def fold_kernel(tile, first, maps, part_ref, got_ref, *rest):
-    out_ref = rest[-1]
+def fold_kernel(tile, first, maps, outputs, part_ref, got_ref, *rest):
+    out_ref = rest[len(rest) - outputs]
     for lo in range(0, out_ref.shape[2], tile):
         cols = slice(lo, lo + tile)
         for j in range(2):
@@ -95,15 +97,21 @@
             out_ref[j, :, cols] = value.astype(out_ref.dtype)
 
 
-def hidden_kernel(tile, part_ref, *rest):
+def hidden_kernel(tile, earlier, part_ref, *rest):
     out_ref = rest[-1]
-    for lo in range(0, out_ref.shape[1], tile):
+    first = 0
+    for ref in rest[1 : 1 + earlier]:
+        width = ref.shape[1]
+        out_ref[:, first : first + width] = ref[...]
+        first += width
+    for lo in range(0, part_ref.shape[2], tile):
         cols = slice(lo, lo + tile)
         gate, up = part_ref[0, :, cols].astype(jnp.float32), part_ref[1, :, cols].astype(jnp.float32)
         if rest[0].shape == part_ref.shape:
             gate = gate + rest[0][0, :, cols].astype(jnp.float32)
             up = up + rest[0][1, :, cols].astype(jnp.float32)
-        out_ref[:, cols] = (gate / (1.0 + jnp.exp(-gate)) * up).astype(out_ref.dtype)
+        place = slice(first + lo, first + lo + tile)
+        out_ref[:, place] = (gate / (1.0 + jnp.exp(-gate)) * up).astype(out_ref.dtype)
 
 
 def per_device(
@@ -125,7 +133,6 @@
     adp_block, low_rank, ff_local = expand_weight.shape[1:]
     depth = adp_block * low_rank
     out_feat = down_weight.shape[1]
-    left = tp_index < tp // 2
     number = lambda value: jnp.asarray(value, jnp.int32).reshape(1)
     inner = tp // 2
     tile = 256 if ff_local % 256 == 0 else 128
@@ -168,7 +175,7 @@
     early = min(EARLY, count - 1)
     maps = [expand[:, :, : spans[early - 1][1]]]
     maps.append(tp_send(maps[0], fold[0]))
-    blocks = [tp_index, jnp.where(left, tp_index - 1, tp_index + 1)]
+    away = jnp.where(tp_index < inner, tp_index - 1, tp_index + 1)
 
     def project(c, *after):
         lo, hi = spans[c]
@@ -193,35 +200,35 @@
     global_ids = jnp.tile(adapter_ids, (steps,)).reshape(1, entries)
     partial = pl.pallas_call(
         functools.partial(shrink_kernel, home, dp),
-        in_specs=[scalar, scalar, whole(x_all), whole(shrink_weight), whole(global_ids)],
+        in_specs=[scalar, scalar, whole(x_all), whole(shrink_weight), whole(global_ids), anywhere],
         out_specs=pl.BlockSpec((2 * low_rank, entries), lambda: (0, 0)),
         out_shape=jax.ShapeDtypeStruct((2 * low_rank, entries), f32),
         compiler_params=params,
         cost_estimate=cost(2**27, 2**21),
         name="shrink",
-    )(number(dp_index), adapter_scale, x_all, shrink_weight, global_ids)
-    low = functools.reduce(
-        jnp.add, [partial] + [tp_send(partial, [(s, s ^ k) for s in range(tp)]) for k in range(1, tp)]
-    )
-    parts = {0: project(0, low)}
+    )(number(dp_index), adapter_scale, x_all, shrink_weight, global_ids, global_ids)
+    parts = {0: project(0, partial)}
     first_got = {0: tp_send(parts[0], fold[0])}
     low = functools.reduce(
-        jnp.add, [gated(low, parts[0])] + [dp_xor(low, k) for k in range(2, dp, 2)]
+        jnp.add, [gated(partial, parts[0])] + [tp_send(partial, [(s, s ^ k) for s in range(tp)]) for k in range(1, tp)]
     )
     for c in range(1, early):
-        parts[c] = project(c, low, maps[1])
+        parts[c] = project(c, low)
         first_got[c] = tp_send(parts[c], fold[0])
+    low = functools.reduce(
+        jnp.add, [gated(low, parts[early - 1])] + [dp_xor(low, k) for k in range(2, dp, 2)]
+    )
     pieces = [low, dp_xor(low, 1)]
     lows = pl.pallas_call(
         functools.partial(lows_kernel, home, dp, len(pieces), low_rank, adp_block),
         in_specs=[scalar, whole(global_ids)] + [whole(low)] * len(pieces),
-        out_specs=pl.BlockSpec((2, len(blocks) * depth, entries), lambda: (0, 0, 0)),
-        out_shape=jax.ShapeDtypeStruct((2, len(blocks) * depth, entries), bf16),
+        out_specs=pl.BlockSpec((2, 2 * depth, entries), lambda: (0, 0, 0)),
+        out_shape=jax.ShapeDtypeStruct((2, 2 * depth, entries), bf16),
         compiler_params=params,
         cost_estimate=cost(2**27, 2**20),
         name="lows",
     )(
-        jnp.concatenate([number(dp_index)] + [number(block) for block in blocks]), global_ids, *pieces
+        jnp.concatenate([number(dp_index), number(tp_index), number(away)]), global_ids, *pieces
     )
 
     def small(kernel, name, shape, operands, *after):
@@ -235,32 +242,68 @@
             name=name,
         )(*operands, *after)
 
+    def fold_call(c, part, got, ahead, *after):
+        shapes = [jax.ShapeDtypeStruct(part.shape, bf16)]
+        operands = [part, got]
+        specs = [whole(part), whole(got)]
+        outs = [pl.BlockSpec(part.shape, lambda: (0,) * part.ndim)]
+        extra = [lows] + maps if c < early else []
+        operands += extra
+        specs += [whole(value) for value in extra]
+        if ahead is not None:
+            operands.append(ahead)
+            specs.append(anywhere)
+            outs.append(anywhere)
+            shapes.append(jax.ShapeDtypeStruct(ahead.shape, bf16))
+        result = pl.pallas_call(
+            functools.partial(
+                fold_kernel, tile, spans[c][0] if extra else 0, len(extra[1:]), len(outs)
+            ),
+            in_specs=specs + [anywhere] * len(after),
+            out_specs=outs,
+            out_shape=shapes,
+            input_output_aliases={2 + len(extra): 1} if ahead is not None else {},
+            compiler_params=params,
+            cost_estimate=cost(2**24, 2**22),
+            name="fold",
+        )(*operands, *after)
+        return result if ahead is not None else (result[0], None)
+
     folded, cross_got, hiddens, full_got = {}, {}, {}, {}
 
     def stage_fold(c, *after):
         part = parts[c]
         for s, pairs in enumerate(fold):
             got = first_got[c] if s == 0 else tp_send(part, pairs)
-            extra = [lows] + maps if c < early and s == 0 else []
-            part = small(
-                functools.partial(fold_kernel, tile, spans[c][0], len(extra[1:])),
-                "fold",
-                part.shape,
-                [part, got] + extra,
-                *after,
-            )
+            ahead = parts.get(c + 2) if s == 0 and c + 2 not in first_got else None
+            part, ahead = fold_call(c if s == 0 else count, part, got, ahead, *after)
+            if ahead is not None:
+                parts[c + 2] = ahead
         folded[c] = part
         cross_got[c] = tp_send(part, across)
 
+    ends, first = {}, 0
+    for size in GROUPS:
+        last = min(first + size, count) - 1
+        if last >= first:
+            ends[last] = first
+        first = last + 1
+    if count - 1 not in ends:
+        ends[count - 1] = first
+
     def stage_hidden(c, *after):
+        earlier = list(range(ends[c], c)) if c in ends else []
+        width = sum(widths[n] for n in earlier + [c])
         hidden = small(
-            functools.partial(hidden_kernel, tile),
+            functools.partial(hidden_kernel, tile, len(earlier)),
             "hidden",
-            (entries, widths[c]),
-            [folded[c], cross_got[c]],
+            (entries, width),
+            [folded[c], cross_got[c]] + [hiddens[n] for n in earlier],
             *after,
         )
         hiddens[c] = hidden
+        if c not in ends:
+            return
         for s, pairs in enumerate(unfold):
             got = tp_send(hidden, pairs)
             if s < len(unfold) - 1:
@@ -268,15 +311,14 @@
                 hidden = jnp.where(fresh, got, hidden)
         full_got[c] = (hidden, got)
 
-    def down(c, hidden, total, *after):
-        value = jnp.dot(gated(hidden, *after), down_weight[slice(*spans[c])], preferred_element_type=f32)
-        return value if total is None else total + value
-
     outermost = (tp_index == 0) | (tp_index == tp - 1)
 
     def stage_down(c, total, *after):
         hidden, got = full_got[c]
-        return down(c, jnp.where(outermost, gated(got, *after), hidden), total)
+        hidden = gated(jnp.where(outermost, got, hidden), *after)
+        rows_of = slice(spans[ends[c]][0], spans[c][1])
+        value = jnp.dot(hidden, down_weight[rows_of], preferred_element_type=f32)
+        return value if total is None else total + value
 
     latest, total = [], None
     for t in range(count + 2):
@@ -284,19 +326,15 @@
             stage_fold(t, *latest)
             latest = [folded[t]]
         if t + 2 < count:
-            if t == 0:
-                parts[2] = project(2, folded[0])
-                latest = [parts[2]]
-            first_got[t + 2] = tp_send(gated(parts[t + 2], folded[t]), fold[0])
-        if t + 3 < count:
-            parts[t + 3] = project(t + 3, *latest)
-            latest = [parts[t + 3]]
+            parts[t + 2] = project(t + 2, *latest)
+            latest = [parts[t + 2]]
+            first_got[t + 2] = tp_send(parts[t + 2], fold[0])
         for c in (t - 1, t):
-            ahead = c + 1 < count and widths[c + 1] > widths[c]
+            ahead = c + 1 < count and bool(AHEAD[c])
             if 0 <= c < count and ahead == (c == t):
                 stage_hidden(c, *latest)
                 latest = [hiddens[c]]
-        if t >= 2:
+        if t - 2 in ends:
             total = stage_down(t - 2, total, *latest)
             latest = [total]
 

time: 162 us -> 152 us (0.938)
  Pallas kernels: 37.1 us -> 31.3 us
  matrix products: 15.2 us -> 9.84 us
    pallas_call x12 -> x6, Pallas kernels: 9.97 us -> 2.96 us  [small(): pl.pallas_call(kernel, in_specs=[whole(value) for value in operands] + [a...]
    dot_general x6, matrix products: 15.2 us -> 9.84 us  [stage_down(): value = jnp.dot(hidden, down_weight[rows_of], preferred_element_type=f32)]
    pallas_call x0 -> x6, Pallas kernels: none -> 2.59 us  [fold_call(): pl.pallas_call(functools.partial(fold_kernel, tile, spans[c][0] if extra...]
    ppermute x22, waiting for transfers between devices: 33.2 us -> 30.7 us  [tp_send(): return lax.ppermute(value, 'tensor', pairs)]
    ppermute x15, waiting for transfers between devices: 13.4 us -> 15.2 us  [dp_xor(): return lax.ppermute(value, 'dp', [(s, s ^ k) for s in range(dp)])]
  transfers between devices with their start and end apart: 37 -> 37, of which waited for: 19 -> 16; matrix products, arithmetic and copies ran while one was open for 10% -> 8% of each run, Pallas kernels for 23% -> 20%
where the time goes in v2:
time: 152 us; the launch traced here: 151 us
  starting transfers between devices  59.7 us (39%)
  waiting for transfers between devices  45.9 us (30%)
  Pallas kernels  31.3 us (21%)
  matrix products  9.84 us (6%)
  local copies, waits for them, and re-layouts  2.18 us (1%)
    ppermute x22, starting transfers between devices, tp_send(): return lax.ppermute(value, 'tensor', pairs)  47.4 us
    ppermute x22, waiting for transfers between devices, tp_send(): return lax.ppermute(value, 'tensor', pairs)  30.7 us
    pallas_call x6, Pallas kernels, project(): pl.pallas_call(functools.partial(project_kernel, c >= early), grid=((hi -...  23.5 us
    ppermute x15, waiting for transfers between devices, dp_xor(): return lax.ppermute(value, 'dp', [(s, s ^ k) for s in range(dp)])  15.2 us
    ppermute x15, starting transfers between devices, dp_xor(): return lax.ppermute(value, 'dp', [(s, s ^ k) for s in range(dp)])  12.4 us
    dot_general x6, matrix products, stage_down(): value = jnp.dot(hidden, down_weight[rows_of], preferred_element_type=f32)  9.84 us
  transfers between devices with their start and end apart: 37, of which 16 were waited for; matrix products, arithmetic and copies ran while one was open for 8% of the time, Pallas kernels for 20%

profile of v2, /device:TPU:0, one launch (start us, length us, event | category | flops | bytes accessed | tf_op | source)
XLA Modules:
  0.0 150.9 jit_solution(16403895457569623867)
XLA Ops:
  0.0 3.0 %collective-permute-start = (bf16[2,16,2048]{2,1,0:T(8,128)(2,1)}, bf16[2,16,2048]{2,1,0:T(8,128)(2,1)S(1)}, u32[]{:S(2)}, u32[]{:S(2)}) collective-permute-start(bf16[2,16,2048]{2,1,0:T(8,128)(2,1)} %param.8), channel_id=1, source_target_pairs={{0,8},{4,12},{8,0},{12,4},{16,24},{20,28},{24,16},{28,20},{1,9},{5... | collective-permute-start | bytes 393224 | tf_op jit(solution)/shard_map/ppermute | solution.py:141
  3.0 1.5 %collective-permute-start.1 = (bf16[2,16,2048]{2,1,0:T(8,128)(2,1)}, bf16[2,16,2048]{2,1,0:T(8,128)(2,1)S(1)}, u32[]{:S(2)}, u32[]{:S(2)}) collective-permute-start(bf16[2,16,2048]{2,1,0:T(8,128)(2,1)} %param.8), channel_id=1, source_target_pairs={{0,16},{4,20},{8,24},{12,28},{16,0},{20,4},{24,8},{28,12},{1,17},{... | collective-permute-start | bytes 393224 | tf_op jit(solution)/shard_map/ppermute | solution.py:141
  4.6 1.0 constant_dynamic-update-slice_fusion.7
  5.5 1.7 %collective-permute-done = bf16[2,16,2048]{2,1,0:T(8,128)(2,1)S(1)} collective-permute-done((bf16[2,16,2048]{2,1,0:T(8,128)(2,1)}, bf16[2,16,2048]{2,1,0:T(8,128)(2,1)S(1)}, u32[]{:S(2)}, u32[]{:S(2)}) %collective-permute-start) | collective-permute-done | bytes 131104 | tf_op jit(solution)/shard_map/ppermute | solution.py:141
  7.2 3.8 %collective-permute-done.1 = bf16[2,16,2048]{2,1,0:T(8,128)(2,1)S(1)} collective-permute-done((bf16[2,16,2048]{2,1,0:T(8,128)(2,1)}, bf16[2,16,2048]{2,1,0:T(8,128)(2,1)S(1)}, u32[]{:S(2)}, u32[]{:S(2)}) %collective-permute-start.1) | collective-permute-done | bytes 131104 | tf_op jit(solution)/shard_map/ppermute | solution.py:141
  11.0 0.6 collective-permute-start.6
  11.7 0.7 collective-permute-done.5
  12.6 1.4 shrink.1.rest_0_
  14.1 3.7 %collective-permute-start.10 = (f32[32,256]{1,0:T(8,128)S(1)}, f32[32,256]{1,0:T(8,128)S(1)}, u32[]{:S(2)}, u32[]{:S(2)}) collective-permute-start(f32[32,256]{1,0:T(8,128)S(1)} %shrink.1.rest_0_), channel_id=1, source_target_pairs={{0,3},{1,2},{2,1},{3,0},{4,7},{5,6},{6,5},{7,4},{8,11},{9,10},{10,... | collective-permute-start | bytes 98312 | tf_op jit(solution)/shard_map/ppermute | solution.py:144
  17.7 0.8 collective-permute-start.9
  18.5 1.0 slice.53.rest_1_
  19.5 3.2 %collective-permute-start.15 = (bf16[2,128,768]{2,1,0:T(8,128)(2,1)S(1)}, bf16[2,128,768]{2,1,0:T(8,128)(2,1)S(1)}, u32[]{:S(2)}, u32[]{:S(2)}) collective-permute-start(bf16[2,128,768]{2,1,0:T(8,128)(2,1)S(1)} %slice.53.rest_1_), channel_id=1, source_target_pairs={{0,1},{3,2},{4,5},{7,6},{8,9},{11,10},{12,13},{15,14},{16,17},{19,... | collective-permute-start | bytes 1179656 | tf_op jit(solution)/shard_map/ppermute | solution.py:144
  22.7 2.3 %project.6.part_ref = bf16[2,256,256]{2,1,0:T(8,128)(2,1)S(1)} custom-call(bf16[256,2048]{1,0:T(8,128)(2,1)S(1)} %bitcast.14, bf16[2048,3584]{1,0:T(8,128)(2,1)} %gate_ref.11, bf16[2048,3584]{1,0:T(8,128)(2,1)} %up_ref.11, f32[32,256]{1,0:T(8,128)S(1)} %shrink.1.rest_0_), custom_call_target="tpu_custom_call" | custom-call | flops 1 | bytes 1 | tf_op jit(solution)/shard_map/project/pallas_call | solution.py:189
  25.0 1.0 collective-permute-start.11
  26.1 1.1 collective-permute-start.12
  27.2 1.4 collective-permute-start.13
  28.6 1.4 collective-permute-start.7
  30.1 3.1 %project.7.part_ref = bf16[2,256,512]{2,1,0:T(8,128)(2,1)S(1)} custom-call(bf16[256,2048]{1,0:T(8,128)(2,1)S(1)} %bitcast.15, bf16[2048,3584]{1,0:T(8,128)(2,1)} %gate_ref.11, bf16[2048,3584]{1,0:T(8,128)(2,1)} %up_ref.11, f32[32,256]{1,0:T(8,128)S(1)} %add_add_fusion.1.rest_0_), custom_call_target="tpu_custom_call" | custom-call | flops 1 | bytes 1 | tf_op jit(solution)/shard_map/project/pallas_call | solution.py:189
  33.1 1.3 collective-permute-start.19
  34.7 1.1 collective-permute-done.14.refs_1_
  35.8 0.9 lows.1.rest_0_
  36.6 1.2 collective-permute-done.7.got_ref
  38.2 0.7 collective-permute-start.16
  38.8 4.9 %project.8.rest_1_.part_ref = bf16[2,256,768]{2,1,0:T(8,128)(2,1)S(1)} custom-call(bf16[256,2048]{1,0:T(8,128)(2,1)S(1)} %bitcast.16, bf16[2048,3584]{1,0:T(8,128)(2,1)} %gate_ref.11, bf16[2048,3584]{1,0:T(8,128)(2,1)} %up_ref.11, bf16[2,256,256]{2,1,0:T(8,128)(2,1)S(1)} %lows.1.rest_0_, bf16[2,128,3584]{2,1,0:T(8,128)(2,1)} %bitcast.24, ...), custom_call_target="tpu_custom_call" | custom-call | flops 1 | bytes 1 | tf_op jit(solution)/shard_map/project/pallas_call | solution.py:189
  43.8 7.1 %collective-permute-start.18 = (bf16[2,256,768]{2,1,0:T(8,128)(2,1)S(1)}, bf16[2,256,768]{2,1,0:T(8,128)(2,1)S(1)}, u32[]{:S(2)}, u32[]{:S(2)}) collective-permute-start(bf16[2,256,768]{2,1,0:T(8,128)(2,1)S(1)} %project.8.rest_1_.part_ref), channel_id=1, source_target_pairs={{0,1},{3,2},{4,5},{7,6},{8,9},{11,10},{12,13},{15,14},{16,17},{19,... | collective-permute-start | bytes 2359304 | tf_op jit(solution)/shard_map/ppermute | solution.py:144
  51.5 0.7 collective-permute-start.20
  52.2 4.8 %project.9.rest_1_.part_ref = bf16[2,256,768]{2,1,0:T(8,128)(2,1)S(1)} custom-call(bf16[256,2048]{1,0:T(8,128)(2,1)S(1)} %bitcast.17, bf16[2048,3584]{1,0:T(8,128)(2,1)} %gate_ref.11, bf16[2048,3584]{1,0:T(8,128)(2,1)} %up_ref.11, bf16[2,256,256]{2,1,0:T(8,128)(2,1)S(1)} %lows.1.rest_0_, bf16[2,128,3584]{2,1,0:T(8,128)(2,1)} %bitcast.25, ...), custom_call_target="tpu_custom_call" | custom-call | flops 1 | bytes 1 | tf_op jit(solution)/shard_map/project/pallas_call | solution.py:189
  57.1 5.1 %collective-permute-start.23 = (bf16[2,256,768]{2,1,0:T(8,128)(2,1)S(1)}, bf16[2,256,768]{2,1,0:T(8,128)(2,1)}, u32[]{:S(2)}, u32[]{:S(2)}) collective-permute-start(bf16[2,256,768]{2,1,0:T(8,128)(2,1)S(1)} %project.9.rest_1_.part_ref), channel_id=1, source_target_pairs={{0,1},{3,2},{4,5},{7,6},{8,9},{11,10},{12,13},{15,14},{16,17},{19,... | collective-permute-start | bytes 2359304 | tf_op jit(solution)/shard_map/ppermute | solution.py:144
  62.1 1.3 collective-permute-start.17
  63.7 5.2 %collective-permute-done.18.got_ref = bf16[2,256,768]{2,1,0:T(8,128)(2,1)S(1)} collective-permute-done((bf16[2,256,768]{2,1,0:T(8,128)(2,1)S(1)}, bf16[2,256,768]{2,1,0:T(8,128)(2,1)S(1)}, u32[]{:S(2)}, u32[]{:S(2)}) %collective-permute-start.18) | collective-permute-done | bytes 786464 | tf_op jit(solution)/shard_map/ppermute | solution.py:144
  69.0 1.6 %collective-permute-start.22 = (bf16[2,256,768]{2,1,0:T(8,128)(2,1)S(1)}, bf16[2,256,768]{2,1,0:T(8,128)(2,1)}, u32[]{:S(2)}, u32[]{:S(2)}) collective-permute-start(bf16[2,256,768]{2,1,0:T(8,128)(2,1)S(1)} %fold.8.rest_2_.part_ref), channel_id=1, source_target_pairs={{1,2},{2,1},{5,6},{6,5},{9,10},{10,9},{13,14},{14,13},{17,18},{18,... | collective-permute-start | bytes 2359304 | tf_op jit(solution)/shard_map/ppermute | solution.py:144
  70.6 4.8 %project.10.part_ref = bf16[2,256,768]{2,1,0:T(8,128)(2,1)S(1)} custom-call(bf16[256,2048]{1,0:T(8,128)(2,1)S(1)} %bitcast.18, bf16[2048,3584]{1,0:T(8,128)(2,1)} %gate_ref.11, bf16[2048,3584]{1,0:T(8,128)(2,1)} %up_ref.11, bf16[2,256,256]{2,1,0:T(8,128)(2,1)S(1)} %lows.1.rest_0_, bf16[2,128,3584]{2,1,0:T(8,128)(2,1)} %bitcast.26, ...), custom_call_target="tpu_custom_call" | custom-call | flops 1 | bytes 1 | tf_op jit(solution)/shard_map/project/pallas_call | solution.py:189
  75.5 1.3 collective-permute-start.21
  76.8 5.4 %collective-permute-start.26 = (bf16[2,256,768]{2,1,0:T(8,128)(2,1)S(1)}, bf16[2,256,768]{2,1,0:T(8,128)(2,1)S(1)}, u32[]{:S(2)}, u32[]{:S(2)}) collective-permute-start(bf16[2,256,768]{2,1,0:T(8,128)(2,1)S(1)} %project.10.part_ref), channel_id=1, source_target_pairs={{0,1},{3,2},{4,5},{7,6},{8,9},{11,10},{12,13},{15,14},{16,17},{19,... | collective-permute-start | bytes 2359304 | tf_op jit(solution)/shard_map/ppermute | solution.py:144
  82.1 1.7 %fusion.17.rest_0_ = f32[256,2048]{1,0:T(8,128)S(1)} fusion(bf16[256,256]{1,0:T(8,128)(2,1)S(1)} %broadcast_select_fusion.5, bf16[3584,2048]{1,0:T(8,128)(2,1)} %param.11), kind=kOutput, calls=%fused_computation.15 | convolution fusion | flops 268435456 | bytes 3276800 | tf_op jit(solution)/shard_map/dot_general | solution.py:320
  83.8 1.9 %collective-permute-done.23.got_ref = bf16[2,256,768]{2,1,0:T(8,128)(2,1)} collective-permute-done((bf16[2,256,768]{2,1,0:T(8,128)(2,1)S(1)}, bf16[2,256,768]{2,1,0:T(8,128)(2,1)}, u32[]{:S(2)}, u32[]{:S(2)}) %collective-permute-start.23) | collective-permute-done | bytes 786464 | tf_op jit(solution)/shard_map/ppermute | solution.py:144
  85.7 1.3 fold.9.rest_2_.part_ref
  87.0 0.7 collective-permute-start.25
  87.7 3.6 %project.11.rest_1_.part_ref = bf16[2,256,512]{2,1,0:T(8,128)(2,1)S(1)} custom-call(bf16[256,2048]{1,0:T(8,128)(2,1)S(1)} %bitcast.19, bf16[2048,3584]{1,0:T(8,128)(2,1)} %gate_ref.11, bf16[2048,3584]{1,0:T(8,128)(2,1)} %up_ref.11, bf16[2,256,256]{2,1,0:T(8,128)(2,1)S(1)} %lows.1.rest_0_, bf16[2,128,3584]{2,1,0:T(8,128)(2,1)} %bitcast.27, ...), custom_call_target="tpu_custom_call" | custom-call | flops 1 | bytes 1 | tf_op jit(solution)/shard_map/project/pallas_call | solution.py:189
  91.4 6.3 %collective-permute-start.29 = (bf16[2,256,512]{2,1,0:T(8,128)(2,1)S(1)}, bf16[2,256,512]{2,1,0:T(8,128)(2,1)S(1)}, u32[]{:S(2)}, u32[]{:S(2)}) collective-permute-start(bf16[2,256,512]{2,1,0:T(8,128)(2,1)S(1)} %project.11.rest_1_.part_ref), channel_id=1, source_target_pairs={{0,1},{3,2},{4,5},{7,6},{8,9},{11,10},{12,13},{15,14},{16,17},{19,... | collective-permute-start | bytes 1572872 | tf_op jit(solution)/shard_map/ppermute | solution.py:144
  97.7 1.6 %hidden.8 = bf16[256,768]{1,0:T(8,128)(2,1)S(1)} custom-call(bf16[2,256,768]{2,1,0:T(8,128)(2,1)S(1)} %fold.8.rest_2_.part_ref, bf16[2,256,768]{2,1,0:T(8,128)(2,1)} %collective-permute-done.22.rest_0_, bf16[2,256,512]{2,1,0:T(8,128)(2,1)S(1)} %project.11.rest_1_.part_ref), custom_call_target="tpu_custom_call" | custom-call | flops 1 | bytes 1 | tf_op jit(solution)/shard_map/hidden/pallas_call | solution.py:235
  99.3 1.3 collective-permute-start.24
  100.7 2.5 %convolution_add_fusion.1.rest_0_ = f32[256,2048]{1,0:T(8,128)S(1)} fusion(f32[256,2048]{1,0:T(8,128)S(1)} %fusion.17.rest_0_, bf16[256,512]{1,0:T(8,128)(2,1)S(1)} %broadcast_select_fusion.4, bf16[3584,2048]{1,0:T(8,128)(2,1)} %param.11), kind=kOutput, calls=%fused_computation.10 | convolution fusion | flops 537395200 | bytes 6553600 | tf_op jit(solution)/shard_map/dot_general | solution.py:320
  103.4 0.8 collective-permute-start.28
  104.6 1.3 collective-permute-start.27
  105.9 6.5 %collective-permute-done.24 = bf16[256,768]{1,0:T(8,128)(2,1)S(1)} collective-permute-done((bf16[256,768]{1,0:T(8,128)(2,1)S(1)}, bf16[256,768]{1,0:T(8,128)(2,1)S(1)}, u32[]{:S(2)}, u32[]{:S(2)}) %collective-permute-start.24) | collective-permute-done | bytes 393248 | tf_op jit(solution)/shard_map/ppermute | solution.py:144
  112.5 3.0 %fusion.6.rest_0_ = f32[256,2048]{1,0:T(8,128)S(1)} fusion(f32[256,2048]{1,0:T(8,128)S(1)} %convolution_add_fusion.1.rest_0_, bf16[256,768]{1,0:T(8,128)(2,1)S(1)} %broadcast_select_fusion.2, bf16[3584,2048]{1,0:T(8,128)(2,1)} %param.11), kind=kOutput, calls=%fused_computation.6 | convolution fusion | flops 805830656 | bytes 7733248 | tf_op jit(solution)/shard_map/dot_general | solution.py:320
  115.6 0.9 collective-permute-start.31
  116.5 1.0 collective-permute-done.27
  117.9 1.3 collective-permute-start.30
  119.2 1.0 fusion.9.rest_1_
  120.5 1.3 collective-permute-start.32
  121.8 12.8 %collective-permute-done.30 = bf16[256,768]{1,0:T(8,128)(2,1)S(1)} collective-permute-done((bf16[256,768]{1,0:T(8,128)(2,1)S(1)}, bf16[256,768]{1,0:T(8,128)(2,1)S(1)}, u32[]{:S(2)}, u32[]{:S(2)}) %collective-permute-start.30) | collective-permute-done | bytes 393248 | tf_op jit(solution)/shard_map/ppermute | solution.py:144
  134.6 1.0 fusion.12
  135.6 2.2 %collective-permute-done.32 = bf16[256,512]{1,0:T(8,128)(2,1)S(1)} collective-permute-done((bf16[256,512]{1,0:T(8,128)(2,1)S(1)}, bf16[256,512]{1,0:T(8,128)(2,1)S(1)}, u32[]{:S(2)}, u32[]{:S(2)}) %collective-permute-start.32) | collective-permute-done | bytes 262176 | tf_op jit(solution)/shard_map/ppermute | solution.py:144
  137.8 0.7 convolution_add_fusion
  138.7 1.9 %collective-permute-done.33 = bf16[2,64,2048]{2,1,0:T(8,128)(2,1)S(1)} collective-permute-done((bf16[2,64,2048]{2,1,0:T(8,128)(2,1)S(1)}, bf16[2,64,2048]{2,1,0:T(8,128)(2,1)S(1)}, u32[]{:S(2)}, u32[]{:S(2)}) %collective-permute-start.33) | collective-permute-done | bytes 524320 | tf_op jit(solution)/shard_map/ppermute | solution.py:141
  140.8 0.7 collective-permute-start.34
  141.5 1.4 collective-permute-start.35
  142.9 1.4 collective-permute-start.36
  144.4 2.9 %collective-permute-done.34 = bf16[2,16,2048]{2,1,0:T(8,128)(2,1)S(1)} collective-permute-done((bf16[2,16,2048]{2,1,0:T(8,128)(2,1)S(1)}, bf16[2,16,2048]{2,1,0:T(8,128)(2,1)S(1)}, u32[]{:S(2)}, u32[]{:S(2)}) %collective-permute-start.34) | collective-permute-done | bytes 131104 | tf_op jit(solution)/shard_map/ppermute | solution.py:141
  147.2 1.3 collective-permute-done.35
  148.5 1.6 %collective-permute-done.36 = bf16[2,16,2048]{2,1,0:T(8,128)(2,1)S(1)} collective-permute-done((bf16[2,16,2048]{2,1,0:T(8,128)(2,1)S(1)}, bf16[2,16,2048]{2,1,0:T(8,128)(2,1)S(1)}, u32[]{:S(2)}, u32[]{:S(2)}) %collective-permute-start.36) | collective-permute-done | bytes 131104 | tf_op jit(solution)/shard_map/ppermute | solution.py:141
  150.1 0.7 fusion.21
  (74 shorter events, 3.7 us)
Async XLA Ops:
  0.0 12.6 %copy-start.2 = (s32[128]{0:T(128)S(1)}, s32[128]{0:T(128)}, u32[]{:S(2)}) copy-start(s32[128]{0:T(128)} %param.15) | copy-start | bytes 1540
  0.0 12.6 %copy-start = (bf16[2048,128]{1,0:T(8,128)(2,1)S(1)}, bf16[2048,128]{1,0:T(8,128)(2,1)}, u32[]{:S(2)}) copy-start(bf16[2048,128]{1,0:T(8,128)(2,1)} %shrink_ref.1) | copy-start | bytes 1572868
  0.0 12.6 %copy-start.1 = (f32[4]{0:T(128)S(1)}, f32[4]{0:T(128)}, u32[]{:S(2)}) copy-start(f32[4]{0:T(128)} %scale_ref.1) | copy-start | bytes 52
  0.0 7.2 %collective-permute-start = (bf16[2,16,2048]{2,1,0:T(8,128)(2,1)}, bf16[2,16,2048]{2,1,0:T(8,128)(2,1)S(1)}, u32[]{:S(2)}, u32[]{:S(2)}) collective-permute-start(bf16[2,16,2048]{2,1,0:T(8,128)(2,1)} %param.8), channel_id=1, source_target_pairs={{0,8},{4,12},{8,0},{12,4},{16,24},{20,28},{24,16},{28,20},{1,9},{5... | collective-permute-start | bytes 393224 | tf_op jit(solution)/shard_map/ppermute | solution.py:141
  3.0 8.0 %collective-permute-start.1 = (bf16[2,16,2048]{2,1,0:T(8,128)(2,1)}, bf16[2,16,2048]{2,1,0:T(8,128)(2,1)S(1)}, u32[]{:S(2)}, u32[]{:S(2)}) collective-permute-start(bf16[2,16,2048]{2,1,0:T(8,128)(2,1)} %param.8), channel_id=1, source_target_pairs={{0,16},{4,20},{8,24},{12,28},{16,0},{20,4},{24,8},{28,12},{1,17},{... | collective-permute-start | bytes 393224 | tf_op jit(solution)/shard_map/ppermute | solution.py:141
  4.5 6.5 %collective-permute-start.2 = (bf16[2,16,2048]{2,1,0:T(8,128)(2,1)}, bf16[2,16,2048]{2,1,0:T(8,128)(2,1)S(1)}, u32[]{:S(2)}, u32[]{:S(2)}) collective-permute-start(bf16[2,16,2048]{2,1,0:T(8,128)(2,1)} %param.8), channel_id=1, source_target_pairs={{0,24},{4,28},{8,16},{12,20},{16,8},{20,12},{24,0},{28,4},{1,25},{... | collective-permute-start | bytes 393224 | tf_op jit(solution)/shard_map/ppermute | solution.py:141
  4.6 7.1 %collective-permute-start.3 = (bf16[2,16,2048]{2,1,0:T(8,128)(2,1)}, bf16[2,16,2048]{2,1,0:T(8,128)(2,1)S(1)}, u32[]{:S(2)}, u32[]{:S(2)}) collective-permute-start(bf16[2,16,2048]{2,1,0:T(8,128)(2,1)} %param.8), channel_id=1, source_target_pairs={{0,4},{4,0},{8,12},{12,8},{16,20},{20,16},{24,28},{28,24},{1,5},{5... | collective-permute-start | bytes 393224 | tf_op jit(solution)/shard_map/ppermute | solution.py:141
  7.2 4.4 %collective-permute-start.4 = (bf16[2,16,2048]{2,1,0:T(8,128)(2,1)S(1)}, bf16[2,16,2048]{2,1,0:T(8,128)(2,1)S(1)}, u32[]{:S(2)}, u32[]{:S(2)}) collective-permute-start(bf16[2,16,2048]{2,1,0:T(8,128)(2,1)S(1)} %collective-permute-done), channel_id=1, source_target_pairs={{0,4},{4,0},{8,12},{12,8},{16,20},{20,16},{24,28},{28,24},{1,5},{5... | collective-permute-start | bytes 393224 | tf_op jit(solution)/shard_map/ppermute | solution.py:141
  11.0 1.3 collective-permute-start.5
  11.0 1.6 %collective-permute-start.6 = (bf16[2,16,2048]{2,1,0:T(8,128)(2,1)S(1)}, bf16[2,16,2048]{2,1,0:T(8,128)(2,1)S(1)}, u32[]{:S(2)}, u32[]{:S(2)}) collective-permute-start(bf16[2,16,2048]{2,1,0:T(8,128)(2,1)S(1)} %collective-permute-done.2), channel_id=1, source_target_pairs={{0,4},{4,0},{8,12},{12,8},{16,20},{20,16},{24,28},{28,24},{1,5},{5... | collective-permute-start | bytes 393224 | tf_op jit(solution)/shard_map/ppermute | solution.py:141
  14.1 10.9 %collective-permute-start.10 = (f32[32,256]{1,0:T(8,128)S(1)}, f32[32,256]{1,0:T(8,128)S(1)}, u32[]{:S(2)}, u32[]{:S(2)}) collective-permute-start(f32[32,256]{1,0:T(8,128)S(1)} %shrink.1.rest_0_), channel_id=1, source_target_pairs={{0,3},{1,2},{2,1},{3,0},{4,7},{5,6},{6,5},{7,4},{8,11},{9,10},{10,... | collective-permute-start | bytes 98312 | tf_op jit(solution)/shard_map/ppermute | solution.py:144
  17.7 7.3 %collective-permute-start.8 = (f32[32,256]{1,0:T(8,128)S(1)}, f32[32,256]{1,0:T(8,128)S(1)}, u32[]{:S(2)}, u32[]{:S(2)}) collective-permute-start(f32[32,256]{1,0:T(8,128)S(1)} %shrink.1.rest_0_), channel_id=1, source_target_pairs={{0,1},{1,0},{2,3},{3,2},{4,5},{5,4},{6,7},{7,6},{8,9},{9,8},{10,11... | collective-permute-start | bytes 98312 | tf_op jit(solution)/shard_map/ppermute | solution.py:144
  17.7 7.3 %collective-permute-start.9 = (f32[32,256]{1,0:T(8,128)S(1)}, f32[32,256]{1,0:T(8,128)S(1)}, u32[]{:S(2)}, u32[]{:S(2)}) collective-permute-start(f32[32,256]{1,0:T(8,128)S(1)} %shrink.1.rest_0_), channel_id=1, source_target_pairs={{0,2},{1,3},{2,0},{3,1},{4,6},{5,7},{6,4},{7,5},{8,10},{9,11},{10,... | collective-permute-start | bytes 98312 | tf_op jit(solution)/shard_map/ppermute | solution.py:144
  19.5 17.1 %collective-permute-start.15 = (bf16[2,128,768]{2,1,0:T(8,128)(2,1)S(1)}, bf16[2,128,768]{2,1,0:T(8,128)(2,1)S(1)}, u32[]{:S(2)}, u32[]{:S(2)}) collective-permute-start(bf16[2,128,768]{2,1,0:T(8,128)(2,1)S(1)} %slice.53.rest_1_), channel_id=1, source_target_pairs={{0,1},{3,2},{4,5},{7,6},{8,9},{11,10},{12,13},{15,14},{16,17},{19,... | collective-permute-start | bytes 1179656 | tf_op jit(solution)/shard_map/ppermute | solution.py:144
  25.0 8.1 %collective-permute-start.11 = (f32[32,256]{1,0:T(8,128)S(1)}, f32[32,256]{1,0:T(8,128)S(1)}, u32[]{:S(2)}, u32[]{:S(2)}) collective-permute-start(f32[32,256]{1,0:T(8,128)S(1)} %add_add_fusion.1.rest_0_), channel_id=1, source_target_pairs={{0,8},{4,12},{8,0},{12,4},{16,24},{20,28},{24,16},{28,20},{1,9},{5... | collective-permute-start | bytes 98312 | tf_op jit(solution)/shard_map/ppermute | solution.py:141
  26.1 8.4 %collective-permute-start.12 = (f32[32,256]{1,0:T(8,128)S(1)}, f32[32,256]{1,0:T(8,128)S(1)}, u32[]{:S(2)}, u32[]{:S(2)}) collective-permute-start(f32[32,256]{1,0:T(8,128)S(1)} %add_add_fusion.1.rest_0_), channel_id=1, source_target_pairs={{0,16},{4,20},{8,24},{12,28},{16,0},{20,4},{24,8},{28,12},{1,17},{... | collective-permute-start | bytes 98312 | tf_op jit(solution)/shard_map/ppermute | solution.py:141
  27.2 7.3 %collective-permute-start.13 = (f32[32,256]{1,0:T(8,128)S(1)}, f32[32,256]{1,0:T(8,128)S(1)}, u32[]{:S(2)}, u32[]{:S(2)}) collective-permute-start(f32[32,256]{1,0:T(8,128)S(1)} %add_add_fusion.1.rest_0_), channel_id=1, source_target_pairs={{0,24},{4,28},{8,16},{12,20},{16,8},{20,12},{24,0},{28,4},{1,25},{... | collective-permute-start | bytes 98312 | tf_op jit(solution)/shard_map/ppermute | solution.py:141
  28.6 9.2 %collective-permute-start.7 = (bf16[2,256,256]{2,1,0:T(8,128)(2,1)S(1)}, bf16[2,256,256]{2,1,0:T(8,128)(2,1)S(1)}, u32[]{:S(2)}, u32[]{:S(2)}) collective-permute-start(bf16[2,256,256]{2,1,0:T(8,128)(2,1)S(1)} %project.6.part_ref), channel_id=1, source_target_pairs={{0,1},{3,2},{4,5},{7,6},{8,9},{11,10},{12,13},{15,14},{16,17},{19,... | collective-permute-start | bytes 786440 | tf_op jit(solution)/shard_map/ppermute | solution.py:144
  33.1 17.9 %collective-permute-start.19 = (bf16[2,256,512]{2,1,0:T(8,128)(2,1)S(1)}, bf16[2,256,512]{2,1,0:T(8,128)(2,1)S(1)}, u32[]{:S(2)}, u32[]{:S(2)}) collective-permute-start(bf16[2,256,512]{2,1,0:T(8,128)(2,1)S(1)} %project.7.part_ref), channel_id=1, source_target_pairs={{0,1},{3,2},{4,5},{7,6},{8,9},{11,10},{12,13},{15,14},{16,17},{19,... | collective-permute-start | bytes 1572872 | tf_op jit(solution)/shard_map/ppermute | solution.py:144
  34.5 1.3 collective-permute-start.14
  38.2 12.8 %collective-permute-start.16 = (bf16[2,256,256]{2,1,0:T(8,128)(2,1)S(1)}, bf16[2,256,256]{2,1,0:T(8,128)(2,1)S(1)}, u32[]{:S(2)}, u32[]{:S(2)}) collective-permute-start(bf16[2,256,256]{2,1,0:T(8,128)(2,1)S(1)} %fold.6.rest_2_.part_ref), channel_id=1, source_target_pairs={{1,2},{2,1},{5,6},{6,5},{9,10},{10,9},{13,14},{14,13},{17,18},{18,... | collective-permute-start | bytes 786440 | tf_op jit(solution)/shard_map/ppermute | solution.py:144
  43.8 25.1 %collective-permute-start.18 = (bf16[2,256,768]{2,1,0:T(8,128)(2,1)S(1)}, bf16[2,256,768]{2,1,0:T(8,128)(2,1)S(1)}, u32[]{:S(2)}, u32[]{:S(2)}) collective-permute-start(bf16[2,256,768]{2,1,0:T(8,128)(2,1)S(1)} %project.8.rest_1_.part_ref), channel_id=1, source_target_pairs={{0,1},{3,2},{4,5},{7,6},{8,9},{11,10},{12,13},{15,14},{16,17},{19,... | collective-permute-start | bytes 2359304 | tf_op jit(solution)/shard_map/ppermute | solution.py:144
  51.5 11.9 %collective-permute-start.20 = (bf16[2,256,512]{2,1,0:T(8,128)(2,1)S(1)}, bf16[2,256,512]{2,1,0:T(8,128)(2,1)S(1)}, u32[]{:S(2)}, u32[]{:S(2)}) collective-permute-start(bf16[2,256,512]{2,1,0:T(8,128)(2,1)S(1)} %fold.7.rest_2_.part_ref), channel_id=1, source_target_pairs={{1,2},{2,1},{5,6},{6,5},{9,10},{10,9},{13,14},{14,13},{17,18},{18,... | collective-permute-start | bytes 1572872 | tf_op jit(solution)/shard_map/ppermute | solution.py:144
  57.1 28.6 %collective-permute-start.23 = (bf16[2,256,768]{2,1,0:T(8,128)(2,1)S(1)}, bf16[2,256,768]{2,1,0:T(8,128)(2,1)}, u32[]{:S(2)}, u32[]{:S(2)}) collective-permute-start(bf16[2,256,768]{2,1,0:T(8,128)(2,1)S(1)} %project.9.rest_1_.part_ref), channel_id=1, source_target_pairs={{0,1},{3,2},{4,5},{7,6},{8,9},{11,10},{12,13},{15,14},{16,17},{19,... | collective-permute-start | bytes 2359304 | tf_op jit(solution)/shard_map/ppermute | solution.py:144
  62.1 8.5 %collective-permute-start.17 = (bf16[256,256]{1,0:T(8,128)(2,1)S(1)}, bf16[256,256]{1,0:T(8,128)(2,1)S(1)}, u32[]{:S(2)}, u32[]{:S(2)}) collective-permute-start(bf16[256,256]{1,0:T(8,128)(2,1)S(1)} %hidden.6.rest_3_), channel_id=1, source_target_pairs={{1,0},{2,3},{5,4},{6,7},{9,8},{10,11},{13,12},{14,15},{17,16},{18,... | collective-permute-start | bytes 393224 | tf_op jit(solution)/shard_map/ppermute | solution.py:144
  69.0 28.7 %collective-permute-start.22 = (bf16[2,256,768]{2,1,0:T(8,128)(2,1)S(1)}, bf16[2,256,768]{2,1,0:T(8,128)(2,1)}, u32[]{:S(2)}, u32[]{:S(2)}) collective-permute-start(bf16[2,256,768]{2,1,0:T(8,128)(2,1)S(1)} %fold.8.rest_2_.part_ref), channel_id=1, source_target_pairs={{1,2},{2,1},{5,6},{6,5},{9,10},{10,9},{13,14},{14,13},{17,18},{18,... | collective-permute-start | bytes 2359304 | tf_op jit(solution)/shard_map/ppermute | solution.py:144
  75.5 25.2 %collective-permute-start.21 = (bf16[256,512]{1,0:T(8,128)(2,1)S(1)}, bf16[256,512]{1,0:T(8,128)(2,1)S(1)}, u32[]{:S(2)}, u32[]{:S(2)}) collective-permute-start(bf16[256,512]{1,0:T(8,128)(2,1)S(1)} %hidden.7.rest_0_), channel_id=1, source_target_pairs={{1,0},{2,3},{5,4},{6,7},{9,8},{10,11},{13,12},{14,15},{17,16},{18,... | collective-permute-start | bytes 786440 | tf_op jit(solution)/shard_map/ppermute | solution.py:144
  76.8 26.4 %collective-permute-start.26 = (bf16[2,256,768]{2,1,0:T(8,128)(2,1)S(1)}, bf16[2,256,768]{2,1,0:T(8,128)(2,1)S(1)}, u32[]{:S(2)}, u32[]{:S(2)}) collective-permute-start(bf16[2,256,768]{2,1,0:T(8,128)(2,1)S(1)} %project.10.part_ref), channel_id=1, source_target_pairs={{0,1},{3,2},{4,5},{7,6},{8,9},{11,10},{12,13},{15,14},{16,17},{19,... | collective-permute-start | bytes 2359304 | tf_op jit(solution)/shard_map/ppermute | solution.py:144
  87.0 17.2 %collective-permute-start.25 = (bf16[2,256,768]{2,1,0:T(8,128)(2,1)S(1)}, bf16[2,256,768]{2,1,0:T(8,128)(2,1)S(1)}, u32[]{:S(2)}, u32[]{:S(2)}) collective-permute-start(bf16[2,256,768]{2,1,0:T(8,128)(2,1)S(1)} %fold.9.rest_2_.part_ref), channel_id=1, source_target_pairs={{1,2},{2,1},{5,6},{6,5},{9,10},{10,9},{13,14},{14,13},{17,18},{18,... | collective-permute-start | bytes 2359304 | tf_op jit(solution)/shard_map/ppermute | solution.py:144
  91.4 24.1 %collective-permute-start.29 = (bf16[2,256,512]{2,1,0:T(8,128)(2,1)S(1)}, bf16[2,256,512]{2,1,0:T(8,128)(2,1)S(1)}, u32[]{:S(2)}, u32[]{:S(2)}) collective-permute-start(bf16[2,256,512]{2,1,0:T(8,128)(2,1)S(1)} %project.11.rest_1_.part_ref), channel_id=1, source_target_pairs={{0,1},{3,2},{4,5},{7,6},{8,9},{11,10},{12,13},{15,14},{16,17},{19,... | collective-permute-start | bytes 1572872 | tf_op jit(solution)/shard_map/ppermute | solution.py:144
  97.7 21.5 %slice-start = ((s8[14680064]{0:T(1024)(128)(4,1)}), s8[4194304]{0:T(1024)(128)(4,1)S(1)}, s32[]{:S(2)}) async-start(s8[14680064]{0:T(1024)(128)(4,1)} %bitcast.28), calls=%async_computation | async-start | bytes 8388608
  99.3 13.1 %collective-permute-start.24 = (bf16[256,768]{1,0:T(8,128)(2,1)S(1)}, bf16[256,768]{1,0:T(8,128)(2,1)S(1)}, u32[]{:S(2)}, u32[]{:S(2)}) collective-permute-start(bf16[256,768]{1,0:T(8,128)(2,1)S(1)} %hidden.8), channel_id=1, source_target_pairs={{1,0},{2,3},{5,4},{6,7},{9,8},{10,11},{13,12},{14,15},{17,16},{18,... | collective-permute-start | bytes 1179656 | tf_op jit(solution)/shard_map/ppermute | solution.py:144
  100.7 18.5 %slice-start.1 = ((s8[14680064]{0:T(1024)(128)(4,1)}), s8[4194304]{0:T(1024)(128)(4,1)S(1)}, s32[]{:S(2)}) async-start(s8[14680064]{0:T(1024)(128)(4,1)} %bitcast.28), calls=%async_computation.1 | async-start | bytes 8388608
  103.4 15.9 %slice-start.2 = ((s8[14680064]{0:T(1024)(128)(4,1)}), s8[4194304]{0:T(1024)(128)(4,1)S(1)}, s32[]{:S(2)}) async-start(s8[14680064]{0:T(1024)(128)(4,1)} %bitcast.28), calls=%async_computation.2 | async-start | bytes 8388608
  103.4 14.1 %collective-permute-start.28 = (bf16[2,256,768]{2,1,0:T(8,128)(2,1)S(1)}, bf16[2,256,768]{2,1,0:T(8,128)(2,1)S(1)}, u32[]{:S(2)}, u32[]{:S(2)}) collective-permute-start(bf16[2,256,768]{2,1,0:T(8,128)(2,1)S(1)} %fold.10.rest_1_.part_ref), channel_id=1, source_target_pairs={{1,2},{2,1},{5,6},{6,5},{9,10},{10,9},{13,14},{14,13},{17,18},{18,... | collective-permute-start | bytes 2359304 | tf_op jit(solution)/shard_map/ppermute | solution.py:144
  104.6 12.9 %collective-permute-start.27 = (bf16[256,768]{1,0:T(8,128)(2,1)S(1)}, bf16[256,768]{1,0:T(8,128)(2,1)S(1)}, u32[]{:S(2)}, u32[]{:S(2)}) collective-permute-start(bf16[256,768]{1,0:T(8,128)(2,1)S(1)} %hidden.9), channel_id=1, source_target_pairs={{1,0},{2,3},{5,4},{6,7},{9,8},{10,11},{13,12},{14,15},{17,16},{18,... | collective-permute-start | bytes 1179656 | tf_op jit(solution)/shard_map/ppermute | solution.py:144
  112.5 6.8 %slice-start.3 = ((s8[14680064]{0:T(1024)(128)(4,1)}), s8[2097152]{0:T(1024)(128)(4,1)S(1)}, s32[]{:S(2)}) async-start(s8[14680064]{0:T(1024)(128)(4,1)} %bitcast.28), calls=%async_computation.3 | async-start | bytes 4194304
  115.6 4.6 %collective-permute-start.31 = (bf16[2,256,512]{2,1,0:T(8,128)(2,1)S(1)}, bf16[2,256,512]{2,1,0:T(8,128)(2,1)S(1)}, u32[]{:S(2)}, u32[]{:S(2)}) collective-permute-start(bf16[2,256,512]{2,1,0:T(8,128)(2,1)S(1)} %fold.11.rest_1_.part_ref), channel_id=1, source_target_pairs={{1,2},{2,1},{5,6},{6,5},{9,10},{10,9},{13,14},{14,13},{17,18},{18,... | collective-permute-start | bytes 1572872 | tf_op jit(solution)/shard_map/ppermute | solution.py:144
  117.9 16.7 %collective-permute-start.30 = (bf16[256,768]{1,0:T(8,128)(2,1)S(1)}, bf16[256,768]{1,0:T(8,128)(2,1)S(1)}, u32[]{:S(2)}, u32[]{:S(2)}) collective-permute-start(bf16[256,768]{1,0:T(8,128)(2,1)S(1)} %hidden.10), channel_id=1, source_target_pairs={{1,0},{2,3},{5,4},{6,7},{9,8},{10,11},{13,12},{14,15},{17,16},{18,... | collective-permute-start | bytes 1179656 | tf_op jit(solution)/shard_map/ppermute | solution.py:144
  120.5 17.3 %collective-permute-start.32 = (bf16[256,512]{1,0:T(8,128)(2,1)S(1)}, bf16[256,512]{1,0:T(8,128)(2,1)S(1)}, u32[]{:S(2)}, u32[]{:S(2)}) collective-permute-start(bf16[256,512]{1,0:T(8,128)(2,1)S(1)} %hidden.11), channel_id=1, source_target_pairs={{1,0},{2,3},{5,4},{6,7},{9,8},{10,11},{13,12},{14,15},{17,16},{18,... | collective-permute-start | bytes 786440 | tf_op jit(solution)/shard_map/ppermute | solution.py:144
  138.6 2.0 %collective-permute-start.33 = (bf16[2,64,2048]{2,1,0:T(8,128)(2,1)S(1)}, bf16[2,64,2048]{2,1,0:T(8,128)(2,1)S(1)}, u32[]{:S(2)}, u32[]{:S(2)}) collective-permute-start(bf16[2,64,2048]{2,1,0:T(8,128)(2,1)S(1)} %slice.87), channel_id=1, source_target_pairs={{0,4},{4,0},{8,12},{12,8},{16,20},{20,16},{24,28},{28,24},{1,5},{5... | collective-permute-start | bytes 1572872 | tf_op jit(solution)/shard_map/ppermute | solution.py:141
  140.8 6.4 %collective-permute-start.34 = (bf16[2,16,2048]{2,1,0:T(8,128)(2,1)S(1)}, bf16[2,16,2048]{2,1,0:T(8,128)(2,1)S(1)}, u32[]{:S(2)}, u32[]{:S(2)}) collective-permute-start(bf16[2,16,2048]{2,1,0:T(8,128)(2,1)S(1)} %get-tuple-element.23), channel_id=1, source_target_pairs={{0,8},{4,12},{8,0},{12,4},{16,24},{20,28},{24,16},{28,20},{1,9},{5... | collective-permute-start | bytes 393224 | tf_op jit(solution)/shard_map/ppermute | solution.py:141
  141.5 7.0 %collective-permute-start.35 = (bf16[2,16,2048]{2,1,0:T(8,128)(2,1)S(1)}, bf16[2,16,2048]{2,1,0:T(8,128)(2,1)S(1)}, u32[]{:S(2)}, u32[]{:S(2)}) collective-permute-start(bf16[2,16,2048]{2,1,0:T(8,128)(2,1)S(1)} %get-tuple-element.25), channel_id=1, source_target_pairs={{0,16},{4,20},{8,24},{12,28},{16,0},{20,4},{24,8},{28,12},{1,17},{... | collective-permute-start | bytes 393224 | tf_op jit(solution)/shard_map/ppermute | solution.py:141
  142.9 7.2 %collective-permute-start.36 = (bf16[2,16,2048]{2,1,0:T(8,128)(2,1)S(1)}, bf16[2,16,2048]{2,1,0:T(8,128)(2,1)S(1)}, u32[]{:S(2)}, u32[]{:S(2)}) collective-permute-start(bf16[2,16,2048]{2,1,0:T(8,128)(2,1)S(1)} %get-tuple-element.24), channel_id=1, source_target_pairs={{0,24},{4,28},{8,16},{12,20},{16,8},{20,12},{24,0},{28,4},{1,25},{... | collective-permute-start | bytes 393224 | tf_op jit(solution)/shard_map/ppermute | solution.py:141

commit v3 on v2

--- a/solution.py
+++ b/solution.py
@@ -213,7 +213,7 @@
         jnp.add, [gated(partial, parts[0])] + [tp_send(partial, [(s, s ^ k) for s in range(tp)]) for k in range(1, tp)]
     )
     for c in range(1, early):
-        parts[c] = project(c, low)
+        parts[c] = project(c, low, maps[1])
         first_got[c] = tp_send(parts[c], fold[0])
     low = functools.reduce(
         jnp.add, [gated(low, parts[early - 1])] + [dp_xor(low, k) for k in range(2, dp, 2)]

time: 152 us -> 150 us (0.987)
  waiting for transfers between devices: 45.9 us -> 42 us
  starting transfers between devices: 59.7 us -> 61.7 us
    ppermute x15, waiting for transfers between devices: 15.2 us -> 9.96 us  [dp_xor(): return lax.ppermute(value, 'dp', [(s, s ^ k) for s in range(dp)])]
    ppermute x22, starting transfers between devices: 47.4 us -> 49 us  [tp_send(): return lax.ppermute(value, 'tensor', pairs)]
  transfers between devices with their start and end apart: 37 -> 37, of which waited for: 16 -> 17; matrix products, arithmetic and copies ran while one was open for 8% -> 8% of each run, Pallas kernels for 20% -> 21%
where the time goes in v3:
time: 150 us; the launch traced here: 149 us
  starting transfers between devices  61.7 us (41%)
  waiting for transfers between devices  42 us (28%)
  Pallas kernels  31.3 us (21%)
  matrix products  9.83 us (7%)
  local copies, waits for them, and re-layouts  2.14 us (1%)
    ppermute x22, starting transfers between devices, tp_send(): return lax.ppermute(value, 'tensor', pairs)  49 us
    ppermute x22, waiting for transfers between devices, tp_send(): return lax.ppermute(value, 'tensor', pairs)  32.1 us
    pallas_call x6, Pallas kernels, project(): pl.pallas_call(functools.partial(project_kernel, c >= early), grid=((hi -...  23.5 us
    ppermute x15, starting transfers between devices, dp_xor(): return lax.ppermute(value, 'dp', [(s, s ^ k) for s in range(dp)])  12.7 us
    ppermute x15, waiting for transfers between devices, dp_xor(): return lax.ppermute(value, 'dp', [(s, s ^ k) for s in range(dp)])  9.96 us
    dot_general x6, matrix products, stage_down(): value = jnp.dot(hidden, down_weight[rows_of], preferred_element_type=f32)  9.83 us
  transfers between devices with their start and end apart: 37, of which 17 were waited for; matrix products, arithmetic and copies ran while one was open for 8% of the time, Pallas kernels for 21%

profile of v3, /device:TPU:0, one launch (start us, length us, event | category | flops | bytes accessed | tf_op | source)
XLA Modules:
  0.0 148.9 jit_solution(12322719698226784322)
XLA Ops:
  0.0 3.0 %collective-permute-start = (bf16[2,16,2048]{2,1,0:T(8,128)(2,1)}, bf16[2,16,2048]{2,1,0:T(8,128)(2,1)S(1)}, u32[]{:S(2)}, u32[]{:S(2)}) collective-permute-start(bf16[2,16,2048]{2,1,0:T(8,128)(2,1)} %param.8), channel_id=1, source_target_pairs={{0,8},{4,12},{8,0},{12,4},{16,24},{20,28},{24,16},{28,20},{1,9},{5... | collective-permute-start | bytes 393224 | tf_op jit(solution)/shard_map/ppermute | solution.py:141
  3.0 1.5 %collective-permute-start.1 = (bf16[2,16,2048]{2,1,0:T(8,128)(2,1)}, bf16[2,16,2048]{2,1,0:T(8,128)(2,1)S(1)}, u32[]{:S(2)}, u32[]{:S(2)}) collective-permute-start(bf16[2,16,2048]{2,1,0:T(8,128)(2,1)} %param.8), channel_id=1, source_target_pairs={{0,16},{4,20},{8,24},{12,28},{16,0},{20,4},{24,8},{28,12},{1,17},{... | collective-permute-start | bytes 393224 | tf_op jit(solution)/shard_map/ppermute | solution.py:141
  4.6 1.0 slice.53.rest_1_
  5.6 4.0 %collective-permute-start.11 = (bf16[2,128,768]{2,1,0:T(8,128)(2,1)S(1)}, bf16[2,128,768]{2,1,0:T(8,128)(2,1)S(1)}, u32[]{:S(2)}, u32[]{:S(2)}) collective-permute-start(bf16[2,128,768]{2,1,0:T(8,128)(2,1)S(1)} %slice.53.rest_1_), channel_id=1, source_target_pairs={{0,1},{3,2},{4,5},{7,6},{8,9},{11,10},{12,13},{15,14},{16,17},{19,... | collective-permute-start | bytes 1179656 | tf_op jit(solution)/shard_map/ppermute | solution.py:144
  9.6 0.9 constant_dynamic-update-slice_fusion.7
  11.2 0.4 collective-permute-start.6
  11.9 0.4 collective-permute-done.5
  12.6 1.4 shrink.1.rest_0_
  14.1 3.7 %collective-permute-start.10 = (f32[32,256]{1,0:T(8,128)S(1)}, f32[32,256]{1,0:T(8,128)S(1)}, u32[]{:S(2)}, u32[]{:S(2)}) collective-permute-start(f32[32,256]{1,0:T(8,128)S(1)} %shrink.1.rest_0_), channel_id=1, source_target_pairs={{0,3},{1,2},{2,1},{3,0},{4,7},{5,6},{6,5},{7,4},{8,11},{9,10},{10,... | collective-permute-start | bytes 98312 | tf_op jit(solution)/shard_map/ppermute | solution.py:144
  17.7 0.8 collective-permute-start.9
  18.5 2.3 %project.6.part_ref = bf16[2,256,256]{2,1,0:T(8,128)(2,1)S(1)} custom-call(bf16[256,2048]{1,0:T(8,128)(2,1)S(1)} %bitcast.14, bf16[2048,3584]{1,0:T(8,128)(2,1)} %gate_ref.11, bf16[2048,3584]{1,0:T(8,128)(2,1)} %up_ref.11, f32[32,256]{1,0:T(8,128)S(1)} %shrink.1.rest_0_), custom_call_target="tpu_custom_call" | custom-call | flops 1 | bytes 1 | tf_op jit(solution)/shard_map/project/pallas_call | solution.py:189
  20.8 1.9 %collective-permute-done.10 = f32[32,256]{1,0:T(8,128)S(1)} collective-permute-done((f32[32,256]{1,0:T(8,128)S(1)}, f32[32,256]{1,0:T(8,128)S(1)}, u32[]{:S(2)}, u32[]{:S(2)}) %collective-permute-start.10) | collective-permute-done | bytes 32800 | tf_op jit(solution)/shard_map/ppermute | solution.py:144
  23.0 1.2 collective-permute-start.12
  24.2 1.5 %collective-permute-start.13 = (f32[32,256]{1,0:T(8,128)S(1)}, f32[32,256]{1,0:T(8,128)S(1)}, u32[]{:S(2)}, u32[]{:S(2)}) collective-permute-start(f32[32,256]{1,0:T(8,128)S(1)} %add_add_fusion.1.rest_0_), channel_id=1, source_target_pairs={{0,16},{4,20},{8,24},{12,28},{16,0},{20,4},{24,8},{28,12},{1,17},{... | collective-permute-start | bytes 98312 | tf_op jit(solution)/shard_map/ppermute | solution.py:141
  25.7 0.9 collective-permute-start.14
  26.5 3.5 %collective-permute-start.7 = (bf16[2,256,256]{2,1,0:T(8,128)(2,1)S(1)}, bf16[2,256,256]{2,1,0:T(8,128)(2,1)S(1)}, u32[]{:S(2)}, u32[]{:S(2)}) collective-permute-start(bf16[2,256,256]{2,1,0:T(8,128)(2,1)S(1)} %project.6.part_ref), channel_id=1, source_target_pairs={{0,1},{3,2},{4,5},{7,6},{8,9},{11,10},{12,13},{15,14},{16,17},{19,... | collective-permute-start | bytes 786440 | tf_op jit(solution)/shard_map/ppermute | solution.py:144
  30.1 3.1 %project.7.part_ref = bf16[2,256,512]{2,1,0:T(8,128)(2,1)S(1)} custom-call(bf16[256,2048]{1,0:T(8,128)(2,1)S(1)} %bitcast.15, bf16[2048,3584]{1,0:T(8,128)(2,1)} %gate_ref.11, bf16[2048,3584]{1,0:T(8,128)(2,1)} %up_ref.11, f32[32,256]{1,0:T(8,128)S(1)} %add_add_fusion.1.rest_0_, bf16[2,128,768]{2,1,0:T(8,128)(2,1)S(1)} %collective-permute-done.11.rest_1_.rest_2_), custom_call_target="tpu_custom_call" | custom-call | flops 1 | bytes 1 | tf_op jit(solution)/shard_map/project/pallas_call | solution.py:189
  33.1 1.3 collective-permute-start.19
  34.7 1.1 collective-permute-done.15.refs_1_
  35.8 0.9 lows.1.rest_0_
  37.0 0.7 collective-permute-start.16
  37.7 4.9 %project.8.rest_1_.part_ref = bf16[2,256,768]{2,1,0:T(8,128)(2,1)S(1)} custom-call(bf16[256,2048]{1,0:T(8,128)(2,1)S(1)} %bitcast.16, bf16[2048,3584]{1,0:T(8,128)(2,1)} %gate_ref.11, bf16[2048,3584]{1,0:T(8,128)(2,1)} %up_ref.11, bf16[2,256,256]{2,1,0:T(8,128)(2,1)S(1)} %lows.1.rest_0_, bf16[2,128,3584]{2,1,0:T(8,128)(2,1)} %bitcast.24, ...), custom_call_target="tpu_custom_call" | custom-call | flops 1 | bytes 1 | tf_op jit(solution)/shard_map/project/pallas_call | solution.py:189
  42.6 4.9 %collective-permute-start.18 = (bf16[2,256,768]{2,1,0:T(8,128)(2,1)S(1)}, bf16[2,256,768]{2,1,0:T(8,128)(2,1)S(1)}, u32[]{:S(2)}, u32[]{:S(2)}) collective-permute-start(bf16[2,256,768]{2,1,0:T(8,128)(2,1)S(1)} %project.8.rest_1_.part_ref), channel_id=1, source_target_pairs={{0,1},{3,2},{4,5},{7,6},{8,9},{11,10},{12,13},{15,14},{16,17},{19,... | collective-permute-start | bytes 2359304 | tf_op jit(solution)/shard_map/ppermute | solution.py:144
  47.7 0.5 fold.7.rest_2_.part_ref
  48.2 0.7 collective-permute-start.20
  48.9 4.8 %project.9.rest_1_.part_ref = bf16[2,256,768]{2,1,0:T(8,128)(2,1)S(1)} custom-call(bf16[256,2048]{1,0:T(8,128)(2,1)S(1)} %bitcast.17, bf16[2048,3584]{1,0:T(8,128)(2,1)} %gate_ref.11, bf16[2048,3584]{1,0:T(8,128)(2,1)} %up_ref.11, bf16[2,256,256]{2,1,0:T(8,128)(2,1)S(1)} %lows.1.rest_0_, bf16[2,128,3584]{2,1,0:T(8,128)(2,1)} %bitcast.25, ...), custom_call_target="tpu_custom_call" | custom-call | flops 1 | bytes 1 | tf_op jit(solution)/shard_map/project/pallas_call | solution.py:189
  53.7 4.8 %collective-permute-start.23 = (bf16[2,256,768]{2,1,0:T(8,128)(2,1)S(1)}, bf16[2,256,768]{2,1,0:T(8,128)(2,1)}, u32[]{:S(2)}, u32[]{:S(2)}) collective-permute-start(bf16[2,256,768]{2,1,0:T(8,128)(2,1)S(1)} %project.9.rest_1_.part_ref), channel_id=1, source_target_pairs={{0,1},{3,2},{4,5},{7,6},{8,9},{11,10},{12,13},{15,14},{16,17},{19,... | collective-permute-start | bytes 2359304 | tf_op jit(solution)/shard_map/ppermute | solution.py:144
  58.5 1.3 collective-permute-start.17
  60.1 5.4 %collective-permute-done.18.got_ref = bf16[2,256,768]{2,1,0:T(8,128)(2,1)S(1)} collective-permute-done((bf16[2,256,768]{2,1,0:T(8,128)(2,1)S(1)}, bf16[2,256,768]{2,1,0:T(8,128)(2,1)S(1)}, u32[]{:S(2)}, u32[]{:S(2)}) %collective-permute-start.18) | collective-permute-done | bytes 786464 | tf_op jit(solution)/shard_map/ppermute | solution.py:144
  65.7 1.6 %collective-permute-start.22 = (bf16[2,256,768]{2,1,0:T(8,128)(2,1)S(1)}, bf16[2,256,768]{2,1,0:T(8,128)(2,1)}, u32[]{:S(2)}, u32[]{:S(2)}) collective-permute-start(bf16[2,256,768]{2,1,0:T(8,128)(2,1)S(1)} %fold.8.rest_2_.part_ref), channel_id=1, source_target_pairs={{1,2},{2,1},{5,6},{6,5},{9,10},{10,9},{13,14},{14,13},{17,18},{18,... | collective-permute-start | bytes 2359304 | tf_op jit(solution)/shard_map/ppermute | solution.py:144
  67.3 4.8 %project.10.part_ref = bf16[2,256,768]{2,1,0:T(8,128)(2,1)S(1)} custom-call(bf16[256,2048]{1,0:T(8,128)(2,1)S(1)} %bitcast.18, bf16[2048,3584]{1,0:T(8,128)(2,1)} %gate_ref.11, bf16[2048,3584]{1,0:T(8,128)(2,1)} %up_ref.11, bf16[2,256,256]{2,1,0:T(8,128)(2,1)S(1)} %lows.1.rest_0_, bf16[2,128,3584]{2,1,0:T(8,128)(2,1)} %bitcast.26, ...), custom_call_target="tpu_custom_call" | custom-call | flops 1 | bytes 1 | tf_op jit(solution)/shard_map/project/pallas_call | solution.py:189
  72.1 1.3 collective-permute-start.21
  73.4 6.0 %collective-permute-start.26 = (bf16[2,256,768]{2,1,0:T(8,128)(2,1)S(1)}, bf16[2,256,768]{2,1,0:T(8,128)(2,1)S(1)}, u32[]{:S(2)}, u32[]{:S(2)}) collective-permute-start(bf16[2,256,768]{2,1,0:T(8,128)(2,1)S(1)} %project.10.part_ref), channel_id=1, source_target_pairs={{0,1},{3,2},{4,5},{7,6},{8,9},{11,10},{12,13},{15,14},{16,17},{19,... | collective-permute-start | bytes 2359304 | tf_op jit(solution)/shard_map/ppermute | solution.py:144
  79.4 1.7 %fusion.17.rest_0_ = f32[256,2048]{1,0:T(8,128)S(1)} fusion(bf16[256,256]{1,0:T(8,128)(2,1)S(1)} %broadcast_select_fusion.5, bf16[3584,2048]{1,0:T(8,128)(2,1)} %param.11), kind=kOutput, calls=%fused_computation.15 | convolution fusion | flops 268435456 | bytes 3276800 | tf_op jit(solution)/shard_map/dot_general | solution.py:320
  81.1 1.3 collective-permute-done.23.got_ref
  82.3 1.3 fold.9.rest_2_.part_ref
  83.7 0.7 collective-permute-start.25
  84.4 3.6 %project.11.rest_1_.part_ref = bf16[2,256,512]{2,1,0:T(8,128)(2,1)S(1)} custom-call(bf16[256,2048]{1,0:T(8,128)(2,1)S(1)} %bitcast.19, bf16[2048,3584]{1,0:T(8,128)(2,1)} %gate_ref.11, bf16[2048,3584]{1,0:T(8,128)(2,1)} %up_ref.11, bf16[2,256,256]{2,1,0:T(8,128)(2,1)S(1)} %lows.1.rest_0_, bf16[2,128,3584]{2,1,0:T(8,128)(2,1)} %bitcast.27, ...), custom_call_target="tpu_custom_call" | custom-call | flops 1 | bytes 1 | tf_op jit(solution)/shard_map/project/pallas_call | solution.py:189
  88.0 6.9 %collective-permute-start.29 = (bf16[2,256,512]{2,1,0:T(8,128)(2,1)S(1)}, bf16[2,256,512]{2,1,0:T(8,128)(2,1)S(1)}, u32[]{:S(2)}, u32[]{:S(2)}) collective-permute-start(bf16[2,256,512]{2,1,0:T(8,128)(2,1)S(1)} %project.11.rest_1_.part_ref), channel_id=1, source_target_pairs={{0,1},{3,2},{4,5},{7,6},{8,9},{11,10},{12,13},{15,14},{16,17},{19,... | collective-permute-start | bytes 1572872 | tf_op jit(solution)/shard_map/ppermute | solution.py:144
  95.0 1.6 %hidden.8 = bf16[256,768]{1,0:T(8,128)(2,1)S(1)} custom-call(bf16[2,256,768]{2,1,0:T(8,128)(2,1)S(1)} %fold.8.rest_2_.part_ref, bf16[2,256,768]{2,1,0:T(8,128)(2,1)} %collective-permute-done.22.rest_0_, bf16[2,256,512]{2,1,0:T(8,128)(2,1)S(1)} %project.11.rest_1_.part_ref), custom_call_target="tpu_custom_call" | custom-call | flops 1 | bytes 1 | tf_op jit(solution)/shard_map/hidden/pallas_call | solution.py:235
  96.6 1.3 collective-permute-start.24
  98.0 2.5 %convolution_add_fusion.1.rest_0_ = f32[256,2048]{1,0:T(8,128)S(1)} fusion(f32[256,2048]{1,0:T(8,128)S(1)} %fusion.17.rest_0_, bf16[256,512]{1,0:T(8,128)(2,1)S(1)} %broadcast_select_fusion.4, bf16[3584,2048]{1,0:T(8,128)(2,1)} %param.11), kind=kOutput, calls=%fused_computation.10 | convolution fusion | flops 537395200 | bytes 6553600 | tf_op jit(solution)/shard_map/dot_general | solution.py:320
  100.6 0.8 collective-permute-start.28
  101.5 0.4 hidden.9
  101.9 1.3 collective-permute-start.27
  103.2 7.3 %collective-permute-done.24 = bf16[256,768]{1,0:T(8,128)(2,1)S(1)} collective-permute-done((bf16[256,768]{1,0:T(8,128)(2,1)S(1)}, bf16[256,768]{1,0:T(8,128)(2,1)S(1)}, u32[]{:S(2)}, u32[]{:S(2)}) %collective-permute-start.24) | collective-permute-done | bytes 393248 | tf_op jit(solution)/shard_map/ppermute | solution.py:144
  110.5 3.0 %fusion.6.rest_0_ = f32[256,2048]{1,0:T(8,128)S(1)} fusion(f32[256,2048]{1,0:T(8,128)S(1)} %convolution_add_fusion.1.rest_0_, bf16[256,768]{1,0:T(8,128)(2,1)S(1)} %broadcast_select_fusion.2, bf16[3584,2048]{1,0:T(8,128)(2,1)} %param.11), kind=kOutput, calls=%fused_computation.6 | convolution fusion | flops 805830656 | bytes 7733248 | tf_op jit(solution)/shard_map/dot_general | solution.py:320
  113.7 0.9 collective-permute-start.31
  114.8 0.4 hidden.10
  115.1 1.3 collective-permute-start.30
  116.5 1.0 fusion.9.rest_1_
  117.7 1.3 collective-permute-start.32
  119.0 13.4 %collective-permute-done.30 = bf16[256,768]{1,0:T(8,128)(2,1)S(1)} collective-permute-done((bf16[256,768]{1,0:T(8,128)(2,1)S(1)}, bf16[256,768]{1,0:T(8,128)(2,1)S(1)}, u32[]{:S(2)}, u32[]{:S(2)}) %collective-permute-start.30) | collective-permute-done | bytes 393248 | tf_op jit(solution)/shard_map/ppermute | solution.py:144
  132.5 1.0 fusion.12
  133.5 2.4 %collective-permute-done.32 = bf16[256,512]{1,0:T(8,128)(2,1)S(1)} collective-permute-done((bf16[256,512]{1,0:T(8,128)(2,1)S(1)}, bf16[256,512]{1,0:T(8,128)(2,1)S(1)}, u32[]{:S(2)}, u32[]{:S(2)}) %collective-permute-start.32) | collective-permute-done | bytes 262176 | tf_op jit(solution)/shard_map/ppermute | solution.py:144
  135.9 0.7 convolution_add_fusion
  136.7 1.9 %collective-permute-done.33 = bf16[2,64,2048]{2,1,0:T(8,128)(2,1)S(1)} collective-permute-done((bf16[2,64,2048]{2,1,0:T(8,128)(2,1)S(1)}, bf16[2,64,2048]{2,1,0:T(8,128)(2,1)S(1)}, u32[]{:S(2)}, u32[]{:S(2)}) %collective-permute-start.33) | collective-permute-done | bytes 524320 | tf_op jit(solution)/shard_map/ppermute | solution.py:141
  138.8 0.8 collective-permute-start.34
  139.6 1.5 %collective-permute-start.35 = (bf16[2,16,2048]{2,1,0:T(8,128)(2,1)S(1)}, bf16[2,16,2048]{2,1,0:T(8,128)(2,1)S(1)}, u32[]{:S(2)}, u32[]{:S(2)}) collective-permute-start(bf16[2,16,2048]{2,1,0:T(8,128)(2,1)S(1)} %get-tuple-element.25), channel_id=1, source_target_pairs={{0,16},{4,20},{8,24},{12,28},{16,0},{20,4},{24,8},{28,12},{1,17},{... | collective-permute-start | bytes 393224 | tf_op jit(solution)/shard_map/ppermute | solution.py:141
  141.2 1.2 collective-permute-start.36
  142.4 2.9 %collective-permute-done.34 = bf16[2,16,2048]{2,1,0:T(8,128)(2,1)S(1)} collective-permute-done((bf16[2,16,2048]{2,1,0:T(8,128)(2,1)S(1)}, bf16[2,16,2048]{2,1,0:T(8,128)(2,1)S(1)}, u32[]{:S(2)}, u32[]{:S(2)}) %collective-permute-start.34) | collective-permute-done | bytes 131104 | tf_op jit(solution)/shard_map/ppermute | solution.py:141
  145.2 1.6 %collective-permute-done.35 = bf16[2,16,2048]{2,1,0:T(8,128)(2,1)S(1)} collective-permute-done((bf16[2,16,2048]{2,1,0:T(8,128)(2,1)S(1)}, bf16[2,16,2048]{2,1,0:T(8,128)(2,1)S(1)}, u32[]{:S(2)}, u32[]{:S(2)}) %collective-permute-start.35) | collective-permute-done | bytes 131104 | tf_op jit(solution)/shard_map/ppermute | solution.py:141
  146.8 1.4 collective-permute-done.36
  148.2 0.7 fusion.21
  (74 shorter events, 3.8 us)
Async XLA Ops:
  0.0 12.6 %copy-start.2 = (s32[128]{0:T(128)S(1)}, s32[128]{0:T(128)}, u32[]{:S(2)}) copy-start(s32[128]{0:T(128)} %param.15) | copy-start | bytes 1540
  0.0 12.6 %copy-start = (bf16[2048,128]{1,0:T(8,128)(2,1)S(1)}, bf16[2048,128]{1,0:T(8,128)(2,1)}, u32[]{:S(2)}) copy-start(bf16[2048,128]{1,0:T(8,128)(2,1)} %shrink_ref.1) | copy-start | bytes 1572868
  0.0 12.6 %copy-start.1 = (f32[4]{0:T(128)S(1)}, f32[4]{0:T(128)}, u32[]{:S(2)}) copy-start(f32[4]{0:T(128)} %scale_ref.1) | copy-start | bytes 52
  0.0 10.5 %collective-permute-start = (bf16[2,16,2048]{2,1,0:T(8,128)(2,1)}, bf16[2,16,2048]{2,1,0:T(8,128)(2,1)S(1)}, u32[]{:S(2)}, u32[]{:S(2)}) collective-permute-start(bf16[2,16,2048]{2,1,0:T(8,128)(2,1)} %param.8), channel_id=1, source_target_pairs={{0,8},{4,12},{8,0},{12,4},{16,24},{20,28},{24,16},{28,20},{1,9},{5... | collective-permute-start | bytes 393224 | tf_op jit(solution)/shard_map/ppermute | solution.py:141
  3.0 8.0 %collective-permute-start.1 = (bf16[2,16,2048]{2,1,0:T(8,128)(2,1)}, bf16[2,16,2048]{2,1,0:T(8,128)(2,1)S(1)}, u32[]{:S(2)}, u32[]{:S(2)}) collective-permute-start(bf16[2,16,2048]{2,1,0:T(8,128)(2,1)} %param.8), channel_id=1, source_target_pairs={{0,16},{4,20},{8,24},{12,28},{16,0},{20,4},{24,8},{28,12},{1,17},{... | collective-permute-start | bytes 393224 | tf_op jit(solution)/shard_map/ppermute | solution.py:141
  4.5 6.6 %collective-permute-start.2 = (bf16[2,16,2048]{2,1,0:T(8,128)(2,1)}, bf16[2,16,2048]{2,1,0:T(8,128)(2,1)S(1)}, u32[]{:S(2)}, u32[]{:S(2)}) collective-permute-start(bf16[2,16,2048]{2,1,0:T(8,128)(2,1)} %param.8), channel_id=1, source_target_pairs={{0,24},{4,28},{8,16},{12,20},{16,8},{20,12},{24,0},{28,4},{1,25},{... | collective-permute-start | bytes 393224 | tf_op jit(solution)/shard_map/ppermute | solution.py:141
  4.6 7.1 %collective-permute-start.3 = (bf16[2,16,2048]{2,1,0:T(8,128)(2,1)}, bf16[2,16,2048]{2,1,0:T(8,128)(2,1)S(1)}, u32[]{:S(2)}, u32[]{:S(2)}) collective-permute-start(bf16[2,16,2048]{2,1,0:T(8,128)(2,1)} %param.8), channel_id=1, source_target_pairs={{0,4},{4,0},{8,12},{12,8},{16,20},{20,16},{24,28},{28,24},{1,5},{5... | collective-permute-start | bytes 393224 | tf_op jit(solution)/shard_map/ppermute | solution.py:141
  5.6 24.5 %collective-permute-start.11 = (bf16[2,128,768]{2,1,0:T(8,128)(2,1)S(1)}, bf16[2,128,768]{2,1,0:T(8,128)(2,1)S(1)}, u32[]{:S(2)}, u32[]{:S(2)}) collective-permute-start(bf16[2,128,768]{2,1,0:T(8,128)(2,1)S(1)} %slice.53.rest_1_), channel_id=1, source_target_pairs={{0,1},{3,2},{4,5},{7,6},{8,9},{11,10},{12,13},{15,14},{16,17},{19,... | collective-permute-start | bytes 1179656 | tf_op jit(solution)/shard_map/ppermute | solution.py:144
  10.5 1.4 collective-permute-start.4
  11.0 1.3 collective-permute-start.5
  11.2 1.4 collective-permute-start.6
  14.1 8.6 %collective-permute-start.10 = (f32[32,256]{1,0:T(8,128)S(1)}, f32[32,256]{1,0:T(8,128)S(1)}, u32[]{:S(2)}, u32[]{:S(2)}) collective-permute-start(f32[32,256]{1,0:T(8,128)S(1)} %shrink.1.rest_0_), channel_id=1, source_target_pairs={{0,3},{1,2},{2,1},{3,0},{4,7},{5,6},{6,5},{7,4},{8,11},{9,10},{10,... | collective-permute-start | bytes 98312 | tf_op jit(solution)/shard_map/ppermute | solution.py:144
  17.7 5.2 %collective-permute-start.8 = (f32[32,256]{1,0:T(8,128)S(1)}, f32[32,256]{1,0:T(8,128)S(1)}, u32[]{:S(2)}, u32[]{:S(2)}) collective-permute-start(f32[32,256]{1,0:T(8,128)S(1)} %shrink.1.rest_0_), channel_id=1, source_target_pairs={{0,1},{1,0},{2,3},{3,2},{4,5},{5,4},{6,7},{7,6},{8,9},{9,8},{10,11... | collective-permute-start | bytes 98312 | tf_op jit(solution)/shard_map/ppermute | solution.py:144
  17.7 5.2 %collective-permute-start.9 = (f32[32,256]{1,0:T(8,128)S(1)}, f32[32,256]{1,0:T(8,128)S(1)}, u32[]{:S(2)}, u32[]{:S(2)}) collective-permute-start(f32[32,256]{1,0:T(8,128)S(1)} %shrink.1.rest_0_), channel_id=1, source_target_pairs={{0,2},{1,3},{2,0},{3,1},{4,6},{5,7},{6,4},{7,5},{8,10},{9,11},{10,... | collective-permute-start | bytes 98312 | tf_op jit(solution)/shard_map/ppermute | solution.py:144
  23.0 11.5 %collective-permute-start.12 = (f32[32,256]{1,0:T(8,128)S(1)}, f32[32,256]{1,0:T(8,128)S(1)}, u32[]{:S(2)}, u32[]{:S(2)}) collective-permute-start(f32[32,256]{1,0:T(8,128)S(1)} %add_add_fusion.1.rest_0_), channel_id=1, source_target_pairs={{0,8},{4,12},{8,0},{12,4},{16,24},{20,28},{24,16},{28,20},{1,9},{5... | collective-permute-start | bytes 98312 | tf_op jit(solution)/shard_map/ppermute | solution.py:141
  24.2 10.3 %collective-permute-start.13 = (f32[32,256]{1,0:T(8,128)S(1)}, f32[32,256]{1,0:T(8,128)S(1)}, u32[]{:S(2)}, u32[]{:S(2)}) collective-permute-start(f32[32,256]{1,0:T(8,128)S(1)} %add_add_fusion.1.rest_0_), channel_id=1, source_target_pairs={{0,16},{4,20},{8,24},{12,28},{16,0},{20,4},{24,8},{28,12},{1,17},{... | collective-permute-start | bytes 98312 | tf_op jit(solution)/shard_map/ppermute | solution.py:141
  25.7 8.8 %collective-permute-start.14 = (f32[32,256]{1,0:T(8,128)S(1)}, f32[32,256]{1,0:T(8,128)S(1)}, u32[]{:S(2)}, u32[]{:S(2)}) collective-permute-start(f32[32,256]{1,0:T(8,128)S(1)} %add_add_fusion.1.rest_0_), channel_id=1, source_target_pairs={{0,24},{4,28},{8,16},{12,20},{16,8},{20,12},{24,0},{28,4},{1,25},{... | collective-permute-start | bytes 98312 | tf_op jit(solution)/shard_map/ppermute | solution.py:141
  26.5 10.1 %collective-permute-start.7 = (bf16[2,256,256]{2,1,0:T(8,128)(2,1)S(1)}, bf16[2,256,256]{2,1,0:T(8,128)(2,1)S(1)}, u32[]{:S(2)}, u32[]{:S(2)}) collective-permute-start(bf16[2,256,256]{2,1,0:T(8,128)(2,1)S(1)} %project.6.part_ref), channel_id=1, source_target_pairs={{0,1},{3,2},{4,5},{7,6},{8,9},{11,10},{12,13},{15,14},{16,17},{19,... | collective-permute-start | bytes 786440 | tf_op jit(solution)/shard_map/ppermute | solution.py:144
  33.1 14.6 %collective-permute-start.19 = (bf16[2,256,512]{2,1,0:T(8,128)(2,1)S(1)}, bf16[2,256,512]{2,1,0:T(8,128)(2,1)S(1)}, u32[]{:S(2)}, u32[]{:S(2)}) collective-permute-start(bf16[2,256,512]{2,1,0:T(8,128)(2,1)S(1)} %project.7.part_ref), channel_id=1, source_target_pairs={{0,1},{3,2},{4,5},{7,6},{8,9},{11,10},{12,13},{15,14},{16,17},{19,... | collective-permute-start | bytes 1572872 | tf_op jit(solution)/shard_map/ppermute | solution.py:144
  34.5 1.3 collective-permute-start.15
  37.0 10.6 %collective-permute-start.16 = (bf16[2,256,256]{2,1,0:T(8,128)(2,1)S(1)}, bf16[2,256,256]{2,1,0:T(8,128)(2,1)S(1)}, u32[]{:S(2)}, u32[]{:S(2)}) collective-permute-start(bf16[2,256,256]{2,1,0:T(8,128)(2,1)S(1)} %fold.6.rest_2_.part_ref), channel_id=1, source_target_pairs={{1,2},{2,1},{5,6},{6,5},{9,10},{10,9},{13,14},{14,13},{17,18},{18,... | collective-permute-start | bytes 786440 | tf_op jit(solution)/shard_map/ppermute | solution.py:144
  42.6 22.9 %collective-permute-start.18 = (bf16[2,256,768]{2,1,0:T(8,128)(2,1)S(1)}, bf16[2,256,768]{2,1,0:T(8,128)(2,1)S(1)}, u32[]{:S(2)}, u32[]{:S(2)}) collective-permute-start(bf16[2,256,768]{2,1,0:T(8,128)(2,1)S(1)} %project.8.rest_1_.part_ref), channel_id=1, source_target_pairs={{0,1},{3,2},{4,5},{7,6},{8,9},{11,10},{12,13},{15,14},{16,17},{19,... | collective-permute-start | bytes 2359304 | tf_op jit(solution)/shard_map/ppermute | solution.py:144
  48.2 11.6 %collective-permute-start.20 = (bf16[2,256,512]{2,1,0:T(8,128)(2,1)S(1)}, bf16[2,256,512]{2,1,0:T(8,128)(2,1)S(1)}, u32[]{:S(2)}, u32[]{:S(2)}) collective-permute-start(bf16[2,256,512]{2,1,0:T(8,128)(2,1)S(1)} %fold.7.rest_2_.part_ref), channel_id=1, source_target_pairs={{1,2},{2,1},{5,6},{6,5},{9,10},{10,9},{13,14},{14,13},{17,18},{18,... | collective-permute-start | bytes 1572872 | tf_op jit(solution)/shard_map/ppermute | solution.py:144
  53.7 28.6 %collective-permute-start.23 = (bf16[2,256,768]{2,1,0:T(8,128)(2,1)S(1)}, bf16[2,256,768]{2,1,0:T(8,128)(2,1)}, u32[]{:S(2)}, u32[]{:S(2)}) collective-permute-start(bf16[2,256,768]{2,1,0:T(8,128)(2,1)S(1)} %project.9.rest_1_.part_ref), channel_id=1, source_target_pairs={{0,1},{3,2},{4,5},{7,6},{8,9},{11,10},{12,13},{15,14},{16,17},{19,... | collective-permute-start | bytes 2359304 | tf_op jit(solution)/shard_map/ppermute | solution.py:144
  58.5 8.7 %collective-permute-start.17 = (bf16[256,256]{1,0:T(8,128)(2,1)S(1)}, bf16[256,256]{1,0:T(8,128)(2,1)S(1)}, u32[]{:S(2)}, u32[]{:S(2)}) collective-permute-start(bf16[256,256]{1,0:T(8,128)(2,1)S(1)} %hidden.6.rest_3_), channel_id=1, source_target_pairs={{1,0},{2,3},{5,4},{6,7},{9,8},{10,11},{13,12},{14,15},{17,16},{18,... | collective-permute-start | bytes 393224 | tf_op jit(solution)/shard_map/ppermute | solution.py:144
  65.7 29.3 %collective-permute-start.22 = (bf16[2,256,768]{2,1,0:T(8,128)(2,1)S(1)}, bf16[2,256,768]{2,1,0:T(8,128)(2,1)}, u32[]{:S(2)}, u32[]{:S(2)}) collective-permute-start(bf16[2,256,768]{2,1,0:T(8,128)(2,1)S(1)} %fold.8.rest_2_.part_ref), channel_id=1, source_target_pairs={{1,2},{2,1},{5,6},{6,5},{9,10},{10,9},{13,14},{14,13},{17,18},{18,... | collective-permute-start | bytes 2359304 | tf_op jit(solution)/shard_map/ppermute | solution.py:144
  72.1 25.8 %collective-permute-start.21 = (bf16[256,512]{1,0:T(8,128)(2,1)S(1)}, bf16[256,512]{1,0:T(8,128)(2,1)S(1)}, u32[]{:S(2)}, u32[]{:S(2)}) collective-permute-start(bf16[256,512]{1,0:T(8,128)(2,1)S(1)} %hidden.7.rest_0_), channel_id=1, source_target_pairs={{1,0},{2,3},{5,4},{6,7},{9,8},{10,11},{13,12},{14,15},{17,16},{18,... | collective-permute-start | bytes 786440 | tf_op jit(solution)/shard_map/ppermute | solution.py:144
  73.4 27.0 %collective-permute-start.26 = (bf16[2,256,768]{2,1,0:T(8,128)(2,1)S(1)}, bf16[2,256,768]{2,1,0:T(8,128)(2,1)S(1)}, u32[]{:S(2)}, u32[]{:S(2)}) collective-permute-start(bf16[2,256,768]{2,1,0:T(8,128)(2,1)S(1)} %project.10.part_ref), channel_id=1, source_target_pairs={{0,1},{3,2},{4,5},{7,6},{8,9},{11,10},{12,13},{15,14},{16,17},{19,... | collective-permute-start | bytes 2359304 | tf_op jit(solution)/shard_map/ppermute | solution.py:144
  83.7 17.8 %collective-permute-start.25 = (bf16[2,256,768]{2,1,0:T(8,128)(2,1)S(1)}, bf16[2,256,768]{2,1,0:T(8,128)(2,1)S(1)}, u32[]{:S(2)}, u32[]{:S(2)}) collective-permute-start(bf16[2,256,768]{2,1,0:T(8,128)(2,1)S(1)} %fold.9.rest_2_.part_ref), channel_id=1, source_target_pairs={{1,2},{2,1},{5,6},{6,5},{9,10},{10,9},{13,14},{14,13},{17,18},{18,... | collective-permute-start | bytes 2359304 | tf_op jit(solution)/shard_map/ppermute | solution.py:144
  88.0 25.5 %collective-permute-start.29 = (bf16[2,256,512]{2,1,0:T(8,128)(2,1)S(1)}, bf16[2,256,512]{2,1,0:T(8,128)(2,1)S(1)}, u32[]{:S(2)}, u32[]{:S(2)}) collective-permute-start(bf16[2,256,512]{2,1,0:T(8,128)(2,1)S(1)} %project.11.rest_1_.part_ref), channel_id=1, source_target_pairs={{0,1},{3,2},{4,5},{7,6},{8,9},{11,10},{12,13},{15,14},{16,17},{19,... | collective-permute-start | bytes 1572872 | tf_op jit(solution)/shard_map/ppermute | solution.py:144
  95.0 21.5 %slice-start = ((s8[14680064]{0:T(1024)(128)(4,1)}), s8[4194304]{0:T(1024)(128)(4,1)S(1)}, s32[]{:S(2)}) async-start(s8[14680064]{0:T(1024)(128)(4,1)} %bitcast.28), calls=%async_computation | async-start | bytes 8388608
  96.6 13.8 %collective-permute-start.24 = (bf16[256,768]{1,0:T(8,128)(2,1)S(1)}, bf16[256,768]{1,0:T(8,128)(2,1)S(1)}, u32[]{:S(2)}, u32[]{:S(2)}) collective-permute-start(bf16[256,768]{1,0:T(8,128)(2,1)S(1)} %hidden.8), channel_id=1, source_target_pairs={{1,0},{2,3},{5,4},{6,7},{9,8},{10,11},{13,12},{14,15},{17,16},{18,... | collective-permute-start | bytes 1179656 | tf_op jit(solution)/shard_map/ppermute | solution.py:144
  98.0 18.5 %slice-start.1 = ((s8[14680064]{0:T(1024)(128)(4,1)}), s8[4194304]{0:T(1024)(128)(4,1)S(1)}, s32[]{:S(2)}) async-start(s8[14680064]{0:T(1024)(128)(4,1)} %bitcast.28), calls=%async_computation.1 | async-start | bytes 8388608
  100.6 15.8 %slice-start.2 = ((s8[14680064]{0:T(1024)(128)(4,1)}), s8[4194304]{0:T(1024)(128)(4,1)S(1)}, s32[]{:S(2)}) async-start(s8[14680064]{0:T(1024)(128)(4,1)} %bitcast.28), calls=%async_computation.2 | async-start | bytes 8388608
  100.6 14.1 %collective-permute-start.28 = (bf16[2,256,768]{2,1,0:T(8,128)(2,1)S(1)}, bf16[2,256,768]{2,1,0:T(8,128)(2,1)S(1)}, u32[]{:S(2)}, u32[]{:S(2)}) collective-permute-start(bf16[2,256,768]{2,1,0:T(8,128)(2,1)S(1)} %fold.10.rest_1_.part_ref), channel_id=1, source_target_pairs={{1,2},{2,1},{5,6},{6,5},{9,10},{10,9},{13,14},{14,13},{17,18},{18,... | collective-permute-start | bytes 2359304 | tf_op jit(solution)/shard_map/ppermute | solution.py:144
  101.9 12.8 %collective-permute-start.27 = (bf16[256,768]{1,0:T(8,128)(2,1)S(1)}, bf16[256,768]{1,0:T(8,128)(2,1)S(1)}, u32[]{:S(2)}, u32[]{:S(2)}) collective-permute-start(bf16[256,768]{1,0:T(8,128)(2,1)S(1)} %hidden.9), channel_id=1, source_target_pairs={{1,0},{2,3},{5,4},{6,7},{9,8},{10,11},{13,12},{14,15},{17,16},{18,... | collective-permute-start | bytes 1179656 | tf_op jit(solution)/shard_map/ppermute | solution.py:144
  110.5 6.0 %slice-start.3 = ((s8[14680064]{0:T(1024)(128)(4,1)}), s8[2097152]{0:T(1024)(128)(4,1)S(1)}, s32[]{:S(2)}) async-start(s8[14680064]{0:T(1024)(128)(4,1)} %bitcast.28), calls=%async_computation.3 | async-start | bytes 4194304
  113.7 3.8 %collective-permute-start.31 = (bf16[2,256,512]{2,1,0:T(8,128)(2,1)S(1)}, bf16[2,256,512]{2,1,0:T(8,128)(2,1)S(1)}, u32[]{:S(2)}, u32[]{:S(2)}) collective-permute-start(bf16[2,256,512]{2,1,0:T(8,128)(2,1)S(1)} %fold.11.rest_1_.part_ref), channel_id=1, source_target_pairs={{1,2},{2,1},{5,6},{6,5},{9,10},{10,9},{13,14},{14,13},{17,18},{18,... | collective-permute-start | bytes 1572872 | tf_op jit(solution)/shard_map/ppermute | solution.py:144
  115.1 17.3 %collective-permute-start.30 = (bf16[256,768]{1,0:T(8,128)(2,1)S(1)}, bf16[256,768]{1,0:T(8,128)(2,1)S(1)}, u32[]{:S(2)}, u32[]{:S(2)}) collective-permute-start(bf16[256,768]{1,0:T(8,128)(2,1)S(1)} %hidden.10), channel_id=1, source_target_pairs={{1,0},{2,3},{5,4},{6,7},{9,8},{10,11},{13,12},{14,15},{17,16},{18,... | collective-permute-start | bytes 1179656 | tf_op jit(solution)/shard_map/ppermute | solution.py:144
  117.7 18.1 %collective-permute-start.32 = (bf16[256,512]{1,0:T(8,128)(2,1)S(1)}, bf16[256,512]{1,0:T(8,128)(2,1)S(1)}, u32[]{:S(2)}, u32[]{:S(2)}) collective-permute-start(bf16[256,512]{1,0:T(8,128)(2,1)S(1)} %hidden.11), channel_id=1, source_target_pairs={{1,0},{2,3},{5,4},{6,7},{9,8},{10,11},{13,12},{14,15},{17,16},{18,... | collective-permute-start | bytes 786440 | tf_op jit(solution)/shard_map/ppermute | solution.py:144
  136.7 2.0 %collective-permute-start.33 = (bf16[2,64,2048]{2,1,0:T(8,128)(2,1)S(1)}, bf16[2,64,2048]{2,1,0:T(8,128)(2,1)S(1)}, u32[]{:S(2)}, u32[]{:S(2)}) collective-permute-start(bf16[2,64,2048]{2,1,0:T(8,128)(2,1)S(1)} %slice.87), channel_id=1, source_target_pairs={{0,4},{4,0},{8,12},{12,8},{16,20},{20,16},{24,28},{28,24},{1,5},{5... | collective-permute-start | bytes 1572872 | tf_op jit(solution)/shard_map/ppermute | solution.py:141
  138.8 6.4 %collective-permute-start.34 = (bf16[2,16,2048]{2,1,0:T(8,128)(2,1)S(1)}, bf16[2,16,2048]{2,1,0:T(8,128)(2,1)S(1)}, u32[]{:S(2)}, u32[]{:S(2)}) collective-permute-start(bf16[2,16,2048]{2,1,0:T(8,128)(2,1)S(1)} %get-tuple-element.23), channel_id=1, source_target_pairs={{0,8},{4,12},{8,0},{12,4},{16,24},{20,28},{24,16},{28,20},{1,9},{5... | collective-permute-start | bytes 393224 | tf_op jit(solution)/shard_map/ppermute | solution.py:141
  139.6 7.1 %collective-permute-start.35 = (bf16[2,16,2048]{2,1,0:T(8,128)(2,1)S(1)}, bf16[2,16,2048]{2,1,0:T(8,128)(2,1)S(1)}, u32[]{:S(2)}, u32[]{:S(2)}) collective-permute-start(bf16[2,16,2048]{2,1,0:T(8,128)(2,1)S(1)} %get-tuple-element.25), channel_id=1, source_target_pairs={{0,16},{4,20},{8,24},{12,28},{16,0},{20,4},{24,8},{28,12},{1,17},{... | collective-permute-start | bytes 393224 | tf_op jit(solution)/shard_map/ppermute | solution.py:141
  141.2 7.0 %collective-permute-start.36 = (bf16[2,16,2048]{2,1,0:T(8,128)(2,1)S(1)}, bf16[2,16,2048]{2,1,0:T(8,128)(2,1)S(1)}, u32[]{:S(2)}, u32[]{:S(2)}) collective-permute-start(bf16[2,16,2048]{2,1,0:T(8,128)(2,1)S(1)} %get-tuple-element.24), channel_id=1, source_target_pairs={{0,24},{4,28},{8,16},{12,20},{16,8},{20,12},{24,0},{28,4},{1,25},{... | collective-permute-start | bytes 393224 | tf_op jit(solution)/shard_map/ppermute | solution.py:141

commit v4 on v3

--- a/solution.py
+++ b/solution.py
@@ -343,7 +343,7 @@
     pair = total[:, : rows // 2] + got.astype(f32)
     pair_sent = pair.astype(bf16)
     mixed = pair[:, :home]
-    for e in range(1, dp // 2):
+    for e in range(dp // 2 - 1, 0, -1):
         mixed = mixed + dp_xor(pair_sent[:, e * home : (e + 1) * home], 2 * e).astype(f32)
     mixed = mixed.astype(bf16)
     return mixed

time: 150 us -> 150 us (level)
  no operation moved by 1% of the time
where the time goes in v4:
time: 150 us; the launch traced here: 149 us
  starting transfers between devices  61.7 us (41%)
  waiting for transfers between devices  42.1 us (28%)
  Pallas kernels  31.3 us (21%)
  matrix products  9.83 us (7%)
  local copies, waits for them, and re-layouts  2.14 us (1%)
    ppermute x22, starting transfers between devices, tp_send(): return lax.ppermute(value, 'tensor', pairs)  49 us
    ppermute x22, waiting for transfers between devices, tp_send(): return lax.ppermute(value, 'tensor', pairs)  32.1 us
    pallas_call x6, Pallas kernels, project(): pl.pallas_call(functools.partial(project_kernel, c >= early), grid=((hi -...  23.5 us
    ppermute x15, starting transfers between devices, dp_xor(): return lax.ppermute(value, 'dp', [(s, s ^ k) for s in range(dp)])  12.7 us
    ppermute x15, waiting for transfers between devices, dp_xor(): return lax.ppermute(value, 'dp', [(s, s ^ k) for s in range(dp)])  10 us
    dot_general x6, matrix products, stage_down(): value = jnp.dot(hidden, down_weight[rows_of], preferred_element_type=f32)  9.83 us
  transfers between devices with their start and end apart: 37, of which 17 were waited for; matrix products, arithmetic and copies ran while one was open for 8% of the time, Pallas kernels for 21%

profile of v4, /device:TPU:0, one launch (start us, length us, event | category | flops | bytes accessed | tf_op | source)
XLA Modules:
  0.0 148.9 jit_solution(9601121139268562939)
XLA Ops:
  0.0 3.0 %collective-permute-start = (bf16[2,16,2048]{2,1,0:T(8,128)(2,1)}, bf16[2,16,2048]{2,1,0:T(8,128)(2,1)S(1)}, u32[]{:S(2)}, u32[]{:S(2)}) collective-permute-start(bf16[2,16,2048]{2,1,0:T(8,128)(2,1)} %param.8), channel_id=1, source_target_pairs={{0,8},{4,12},{8,0},{12,4},{16,24},{20,28},{24,16},{28,20},{1,9},{5... | collective-permute-start | bytes 393224 | tf_op jit(solution)/shard_map/ppermute | solution.py:141
  3.0 1.5 %collective-permute-start.1 = (bf16[2,16,2048]{2,1,0:T(8,128)(2,1)}, bf16[2,16,2048]{2,1,0:T(8,128)(2,1)S(1)}, u32[]{:S(2)}, u32[]{:S(2)}) collective-permute-start(bf16[2,16,2048]{2,1,0:T(8,128)(2,1)} %param.8), channel_id=1, source_target_pairs={{0,16},{4,20},{8,24},{12,28},{16,0},{20,4},{24,8},{28,12},{1,17},{... | collective-permute-start | bytes 393224 | tf_op jit(solution)/shard_map/ppermute | solution.py:141
  4.6 1.0 slice.53.rest_1_
  5.6 4.0 %collective-permute-start.11 = (bf16[2,128,768]{2,1,0:T(8,128)(2,1)S(1)}, bf16[2,128,768]{2,1,0:T(8,128)(2,1)S(1)}, u32[]{:S(2)}, u32[]{:S(2)}) collective-permute-start(bf16[2,128,768]{2,1,0:T(8,128)(2,1)S(1)} %slice.53.rest_1_), channel_id=1, source_target_pairs={{0,1},{3,2},{4,5},{7,6},{8,9},{11,10},{12,13},{15,14},{16,17},{19,... | collective-permute-start | bytes 1179656 | tf_op jit(solution)/shard_map/ppermute | solution.py:144
  9.6 0.9 constant_dynamic-update-slice_fusion.7
  11.2 0.4 collective-permute-start.6
  11.9 0.4 collective-permute-done.5
  12.6 1.4 shrink.1.rest_0_
  14.1 3.7 %collective-permute-start.10 = (f32[32,256]{1,0:T(8,128)S(1)}, f32[32,256]{1,0:T(8,128)S(1)}, u32[]{:S(2)}, u32[]{:S(2)}) collective-permute-start(f32[32,256]{1,0:T(8,128)S(1)} %shrink.1.rest_0_), channel_id=1, source_target_pairs={{0,3},{1,2},{2,1},{3,0},{4,7},{5,6},{6,5},{7,4},{8,11},{9,10},{10,... | collective-permute-start | bytes 98312 | tf_op jit(solution)/shard_map/ppermute | solution.py:144
  17.7 0.8 collective-permute-start.9
  18.5 2.3 %project.6.part_ref = bf16[2,256,256]{2,1,0:T(8,128)(2,1)S(1)} custom-call(bf16[256,2048]{1,0:T(8,128)(2,1)S(1)} %bitcast.14, bf16[2048,3584]{1,0:T(8,128)(2,1)} %gate_ref.11, bf16[2048,3584]{1,0:T(8,128)(2,1)} %up_ref.11, f32[32,256]{1,0:T(8,128)S(1)} %shrink.1.rest_0_), custom_call_target="tpu_custom_call" | custom-call | flops 1 | bytes 1 | tf_op jit(solution)/shard_map/project/pallas_call | solution.py:189
  20.8 1.9 %collective-permute-done.10 = f32[32,256]{1,0:T(8,128)S(1)} collective-permute-done((f32[32,256]{1,0:T(8,128)S(1)}, f32[32,256]{1,0:T(8,128)S(1)}, u32[]{:S(2)}, u32[]{:S(2)}) %collective-permute-start.10) | collective-permute-done | bytes 32800 | tf_op jit(solution)/shard_map/ppermute | solution.py:144
  23.0 1.2 collective-permute-start.12
  24.2 1.5 %collective-permute-start.13 = (f32[32,256]{1,0:T(8,128)S(1)}, f32[32,256]{1,0:T(8,128)S(1)}, u32[]{:S(2)}, u32[]{:S(2)}) collective-permute-start(f32[32,256]{1,0:T(8,128)S(1)} %add_add_fusion.1.rest_0_), channel_id=1, source_target_pairs={{0,16},{4,20},{8,24},{12,28},{16,0},{20,4},{24,8},{28,12},{1,17},{... | collective-permute-start | bytes 98312 | tf_op jit(solution)/shard_map/ppermute | solution.py:141
  25.7 0.9 collective-permute-start.14
  26.5 3.5 %collective-permute-start.7 = (bf16[2,256,256]{2,1,0:T(8,128)(2,1)S(1)}, bf16[2,256,256]{2,1,0:T(8,128)(2,1)S(1)}, u32[]{:S(2)}, u32[]{:S(2)}) collective-permute-start(bf16[2,256,256]{2,1,0:T(8,128)(2,1)S(1)} %project.6.part_ref), channel_id=1, source_target_pairs={{0,1},{3,2},{4,5},{7,6},{8,9},{11,10},{12,13},{15,14},{16,17},{19,... | collective-permute-start | bytes 786440 | tf_op jit(solution)/shard_map/ppermute | solution.py:144
  30.1 3.1 %project.7.part_ref = bf16[2,256,512]{2,1,0:T(8,128)(2,1)S(1)} custom-call(bf16[256,2048]{1,0:T(8,128)(2,1)S(1)} %bitcast.15, bf16[2048,3584]{1,0:T(8,128)(2,1)} %gate_ref.11, bf16[2048,3584]{1,0:T(8,128)(2,1)} %up_ref.11, f32[32,256]{1,0:T(8,128)S(1)} %add_add_fusion.1.rest_0_, bf16[2,128,768]{2,1,0:T(8,128)(2,1)S(1)} %collective-permute-done.11.rest_1_.rest_2_), custom_call_target="tpu_custom_call" | custom-call | flops 1 | bytes 1 | tf_op jit(solution)/shard_map/project/pallas_call | solution.py:189
  33.1 1.3 collective-permute-start.19
  34.7 1.1 collective-permute-done.15.refs_1_
  35.8 0.9 lows.1.rest_0_
  36.7 0.3 fold.6.rest_2_.part_ref
  37.0 0.7 collective-permute-start.16
  37.7 4.9 %project.8.rest_1_.part_ref = bf16[2,256,768]{2,1,0:T(8,128)(2,1)S(1)} custom-call(bf16[256,2048]{1,0:T(8,128)(2,1)S(1)} %bitcast.16, bf16[2048,3584]{1,0:T(8,128)(2,1)} %gate_ref.11, bf16[2048,3584]{1,0:T(8,128)(2,1)} %up_ref.11, bf16[2,256,256]{2,1,0:T(8,128)(2,1)S(1)} %lows.1.rest_0_, bf16[2,128,3584]{2,1,0:T(8,128)(2,1)} %bitcast.24, ...), custom_call_target="tpu_custom_call" | custom-call | flops 1 | bytes 1 | tf_op jit(solution)/shard_map/project/pallas_call | solution.py:189
  42.6 4.9 %collective-permute-start.18 = (bf16[2,256,768]{2,1,0:T(8,128)(2,1)S(1)}, bf16[2,256,768]{2,1,0:T(8,128)(2,1)S(1)}, u32[]{:S(2)}, u32[]{:S(2)}) collective-permute-start(bf16[2,256,768]{2,1,0:T(8,128)(2,1)S(1)} %project.8.rest_1_.part_ref), channel_id=1, source_target_pairs={{0,1},{3,2},{4,5},{7,6},{8,9},{11,10},{12,13},{15,14},{16,17},{19,... | collective-permute-start | bytes 2359304 | tf_op jit(solution)/shard_map/ppermute | solution.py:144
  47.7 0.5 fold.7.rest_2_.part_ref
  48.2 0.7 collective-permute-start.20
  48.9 4.8 %project.9.rest_1_.part_ref = bf16[2,256,768]{2,1,0:T(8,128)(2,1)S(1)} custom-call(bf16[256,2048]{1,0:T(8,128)(2,1)S(1)} %bitcast.17, bf16[2048,3584]{1,0:T(8,128)(2,1)} %gate_ref.11, bf16[2048,3584]{1,0:T(8,128)(2,1)} %up_ref.11, bf16[2,256,256]{2,1,0:T(8,128)(2,1)S(1)} %lows.1.rest_0_, bf16[2,128,3584]{2,1,0:T(8,128)(2,1)} %bitcast.25, ...), custom_call_target="tpu_custom_call" | custom-call | flops 1 | bytes 1 | tf_op jit(solution)/shard_map/project/pallas_call | solution.py:189
  53.7 4.8 %collective-permute-start.23 = (bf16[2,256,768]{2,1,0:T(8,128)(2,1)S(1)}, bf16[2,256,768]{2,1,0:T(8,128)(2,1)}, u32[]{:S(2)}, u32[]{:S(2)}) collective-permute-start(bf16[2,256,768]{2,1,0:T(8,128)(2,1)S(1)} %project.9.rest_1_.part_ref), channel_id=1, source_target_pairs={{0,1},{3,2},{4,5},{7,6},{8,9},{11,10},{12,13},{15,14},{16,17},{19,... | collective-permute-start | bytes 2359304 | tf_op jit(solution)/shard_map/ppermute | solution.py:144
  58.5 1.3 collective-permute-start.17
  60.1 5.4 %collective-permute-done.18.got_ref = bf16[2,256,768]{2,1,0:T(8,128)(2,1)S(1)} collective-permute-done((bf16[2,256,768]{2,1,0:T(8,128)(2,1)S(1)}, bf16[2,256,768]{2,1,0:T(8,128)(2,1)S(1)}, u32[]{:S(2)}, u32[]{:S(2)}) %collective-permute-start.18) | collective-permute-done | bytes 786464 | tf_op jit(solution)/shard_map/ppermute | solution.py:144
  65.7 1.6 %collective-permute-start.22 = (bf16[2,256,768]{2,1,0:T(8,128)(2,1)S(1)}, bf16[2,256,768]{2,1,0:T(8,128)(2,1)}, u32[]{:S(2)}, u32[]{:S(2)}) collective-permute-start(bf16[2,256,768]{2,1,0:T(8,128)(2,1)S(1)} %fold.8.rest_2_.part_ref), channel_id=1, source_target_pairs={{1,2},{2,1},{5,6},{6,5},{9,10},{10,9},{13,14},{14,13},{17,18},{18,... | collective-permute-start | bytes 2359304 | tf_op jit(solution)/shard_map/ppermute | solution.py:144
  67.3 4.8 %project.10.part_ref = bf16[2,256,768]{2,1,0:T(8,128)(2,1)S(1)} custom-call(bf16[256,2048]{1,0:T(8,128)(2,1)S(1)} %bitcast.18, bf16[2048,3584]{1,0:T(8,128)(2,1)} %gate_ref.11, bf16[2048,3584]{1,0:T(8,128)(2,1)} %up_ref.11, bf16[2,256,256]{2,1,0:T(8,128)(2,1)S(1)} %lows.1.rest_0_, bf16[2,128,3584]{2,1,0:T(8,128)(2,1)} %bitcast.26, ...), custom_call_target="tpu_custom_call" | custom-call | flops 1 | bytes 1 | tf_op jit(solution)/shard_map/project/pallas_call | solution.py:189
  72.1 1.3 collective-permute-start.21
  73.4 6.0 %collective-permute-start.26 = (bf16[2,256,768]{2,1,0:T(8,128)(2,1)S(1)}, bf16[2,256,768]{2,1,0:T(8,128)(2,1)S(1)}, u32[]{:S(2)}, u32[]{:S(2)}) collective-permute-start(bf16[2,256,768]{2,1,0:T(8,128)(2,1)S(1)} %project.10.part_ref), channel_id=1, source_target_pairs={{0,1},{3,2},{4,5},{7,6},{8,9},{11,10},{12,13},{15,14},{16,17},{19,... | collective-permute-start | bytes 2359304 | tf_op jit(solution)/shard_map/ppermute | solution.py:144
  79.4 1.7 %fusion.17.rest_0_ = f32[256,2048]{1,0:T(8,128)S(1)} fusion(bf16[256,256]{1,0:T(8,128)(2,1)S(1)} %broadcast_select_fusion.5, bf16[3584,2048]{1,0:T(8,128)(2,1)} %param.11), kind=kOutput, calls=%fused_computation.15 | convolution fusion | flops 268435456 | bytes 3276800 | tf_op jit(solution)/shard_map/dot_general | solution.py:320
  81.1 1.3 collective-permute-done.23.got_ref
  82.3 1.3 fold.9.rest_2_.part_ref
  83.7 0.7 collective-permute-start.25
  84.4 3.6 %project.11.rest_1_.part_ref = bf16[2,256,512]{2,1,0:T(8,128)(2,1)S(1)} custom-call(bf16[256,2048]{1,0:T(8,128)(2,1)S(1)} %bitcast.19, bf16[2048,3584]{1,0:T(8,128)(2,1)} %gate_ref.11, bf16[2048,3584]{1,0:T(8,128)(2,1)} %up_ref.11, bf16[2,256,256]{2,1,0:T(8,128)(2,1)S(1)} %lows.1.rest_0_, bf16[2,128,3584]{2,1,0:T(8,128)(2,1)} %bitcast.27, ...), custom_call_target="tpu_custom_call" | custom-call | flops 1 | bytes 1 | tf_op jit(solution)/shard_map/project/pallas_call | solution.py:189
  88.0 6.9 %collective-permute-start.29 = (bf16[2,256,512]{2,1,0:T(8,128)(2,1)S(1)}, bf16[2,256,512]{2,1,0:T(8,128)(2,1)S(1)}, u32[]{:S(2)}, u32[]{:S(2)}) collective-permute-start(bf16[2,256,512]{2,1,0:T(8,128)(2,1)S(1)} %project.11.rest_1_.part_ref), channel_id=1, source_target_pairs={{0,1},{3,2},{4,5},{7,6},{8,9},{11,10},{12,13},{15,14},{16,17},{19,... | collective-permute-start | bytes 1572872 | tf_op jit(solution)/shard_map/ppermute | solution.py:144
  95.0 1.6 %hidden.8 = bf16[256,768]{1,0:T(8,128)(2,1)S(1)} custom-call(bf16[2,256,768]{2,1,0:T(8,128)(2,1)S(1)} %fold.8.rest_2_.part_ref, bf16[2,256,768]{2,1,0:T(8,128)(2,1)} %collective-permute-done.22.rest_0_, bf16[2,256,512]{2,1,0:T(8,128)(2,1)S(1)} %project.11.rest_1_.part_ref), custom_call_target="tpu_custom_call" | custom-call | flops 1 | bytes 1 | tf_op jit(solution)/shard_map/hidden/pallas_call | solution.py:235
  96.6 1.3 collective-permute-start.24
  98.0 2.5 %convolution_add_fusion.1.rest_0_ = f32[256,2048]{1,0:T(8,128)S(1)} fusion(f32[256,2048]{1,0:T(8,128)S(1)} %fusion.17.rest_0_, bf16[256,512]{1,0:T(8,128)(2,1)S(1)} %broadcast_select_fusion.4, bf16[3584,2048]{1,0:T(8,128)(2,1)} %param.11), kind=kOutput, calls=%fused_computation.10 | convolution fusion | flops 537395200 | bytes 6553600 | tf_op jit(solution)/shard_map/dot_general | solution.py:320
  100.6 0.8 collective-permute-start.28
  101.5 0.4 hidden.9
  101.9 1.3 collective-permute-start.27
  103.2 7.3 %collective-permute-done.24 = bf16[256,768]{1,0:T(8,128)(2,1)S(1)} collective-permute-done((bf16[256,768]{1,0:T(8,128)(2,1)S(1)}, bf16[256,768]{1,0:T(8,128)(2,1)S(1)}, u32[]{:S(2)}, u32[]{:S(2)}) %collective-permute-start.24) | collective-permute-done | bytes 393248 | tf_op jit(solution)/shard_map/ppermute | solution.py:144
  110.5 3.0 %fusion.6.rest_0_ = f32[256,2048]{1,0:T(8,128)S(1)} fusion(f32[256,2048]{1,0:T(8,128)S(1)} %convolution_add_fusion.1.rest_0_, bf16[256,768]{1,0:T(8,128)(2,1)S(1)} %broadcast_select_fusion.2, bf16[3584,2048]{1,0:T(8,128)(2,1)} %param.11), kind=kOutput, calls=%fused_computation.6 | convolution fusion | flops 805830656 | bytes 7733248 | tf_op jit(solution)/shard_map/dot_general | solution.py:320
  113.7 0.9 collective-permute-start.31
  114.8 0.4 hidden.10
  115.1 1.3 collective-permute-start.30
  116.5 1.0 fusion.9.rest_1_
  117.7 1.3 collective-permute-start.32
  119.0 13.4 %collective-permute-done.30 = bf16[256,768]{1,0:T(8,128)(2,1)S(1)} collective-permute-done((bf16[256,768]{1,0:T(8,128)(2,1)S(1)}, bf16[256,768]{1,0:T(8,128)(2,1)S(1)}, u32[]{:S(2)}, u32[]{:S(2)}) %collective-permute-start.30) | collective-permute-done | bytes 393248 | tf_op jit(solution)/shard_map/ppermute | solution.py:144
  132.5 1.0 fusion.12
  133.5 2.4 %collective-permute-done.32 = bf16[256,512]{1,0:T(8,128)(2,1)S(1)} collective-permute-done((bf16[256,512]{1,0:T(8,128)(2,1)S(1)}, bf16[256,512]{1,0:T(8,128)(2,1)S(1)}, u32[]{:S(2)}, u32[]{:S(2)}) %collective-permute-start.32) | collective-permute-done | bytes 262176 | tf_op jit(solution)/shard_map/ppermute | solution.py:144
  135.9 0.7 convolution_add_fusion
  136.7 1.9 %collective-permute-done.33 = bf16[2,64,2048]{2,1,0:T(8,128)(2,1)S(1)} collective-permute-done((bf16[2,64,2048]{2,1,0:T(8,128)(2,1)S(1)}, bf16[2,64,2048]{2,1,0:T(8,128)(2,1)S(1)}, u32[]{:S(2)}, u32[]{:S(2)}) %collective-permute-start.33) | collective-permute-done | bytes 524320 | tf_op jit(solution)/shard_map/ppermute | solution.py:141
  138.8 1.8 %collective-permute-start.34 = (bf16[2,16,2048]{2,1,0:T(8,128)(2,1)S(1)}, bf16[2,16,2048]{2,1,0:T(8,128)(2,1)S(1)}, u32[]{:S(2)}, u32[]{:S(2)}) collective-permute-start(bf16[2,16,2048]{2,1,0:T(8,128)(2,1)S(1)} %get-tuple-element.23), channel_id=1, source_target_pairs={{0,24},{4,28},{8,16},{12,20},{16,8},{20,12},{24,0},{28,4},{1,25},{... | collective-permute-start | bytes 393224 | tf_op jit(solution)/shard_map/ppermute | solution.py:141
  140.6 0.5 collective-permute-start.35
  141.1 1.3 collective-permute-start.36
  142.4 3.7 %collective-permute-done.34 = bf16[2,16,2048]{2,1,0:T(8,128)(2,1)S(1)} collective-permute-done((bf16[2,16,2048]{2,1,0:T(8,128)(2,1)S(1)}, bf16[2,16,2048]{2,1,0:T(8,128)(2,1)S(1)}, u32[]{:S(2)}, u32[]{:S(2)}) %collective-permute-start.34) | collective-permute-done | bytes 131104 | tf_op jit(solution)/shard_map/ppermute | solution.py:141
  146.1 2.0 %collective-permute-done.35 = bf16[2,16,2048]{2,1,0:T(8,128)(2,1)S(1)} collective-permute-done((bf16[2,16,2048]{2,1,0:T(8,128)(2,1)S(1)}, bf16[2,16,2048]{2,1,0:T(8,128)(2,1)S(1)}, u32[]{:S(2)}, u32[]{:S(2)}) %collective-permute-start.35) | collective-permute-done | bytes 131104 | tf_op jit(solution)/shard_map/ppermute | solution.py:141
  148.2 0.7 fusion.21
  (74 shorter events, 3.6 us)
Async XLA Ops:
  0.0 12.6 %copy-start.2 = (s32[128]{0:T(128)S(1)}, s32[128]{0:T(128)}, u32[]{:S(2)}) copy-start(s32[128]{0:T(128)} %param.15) | copy-start | bytes 1540
  0.0 12.6 %copy-start = (bf16[2048,128]{1,0:T(8,128)(2,1)S(1)}, bf16[2048,128]{1,0:T(8,128)(2,1)}, u32[]{:S(2)}) copy-start(bf16[2048,128]{1,0:T(8,128)(2,1)} %shrink_ref.1) | copy-start | bytes 1572868
  0.0 12.6 %copy-start.1 = (f32[4]{0:T(128)S(1)}, f32[4]{0:T(128)}, u32[]{:S(2)}) copy-start(f32[4]{0:T(128)} %scale_ref.1) | copy-start | bytes 52
  0.0 10.5 %collective-permute-start = (bf16[2,16,2048]{2,1,0:T(8,128)(2,1)}, bf16[2,16,2048]{2,1,0:T(8,128)(2,1)S(1)}, u32[]{:S(2)}, u32[]{:S(2)}) collective-permute-start(bf16[2,16,2048]{2,1,0:T(8,128)(2,1)} %param.8), channel_id=1, source_target_pairs={{0,8},{4,12},{8,0},{12,4},{16,24},{20,28},{24,16},{28,20},{1,9},{5... | collective-permute-start | bytes 393224 | tf_op jit(solution)/shard_map/ppermute | solution.py:141
  3.0 8.0 %collective-permute-start.1 = (bf16[2,16,2048]{2,1,0:T(8,128)(2,1)}, bf16[2,16,2048]{2,1,0:T(8,128)(2,1)S(1)}, u32[]{:S(2)}, u32[]{:S(2)}) collective-permute-start(bf16[2,16,2048]{2,1,0:T(8,128)(2,1)} %param.8), channel_id=1, source_target_pairs={{0,16},{4,20},{8,24},{12,28},{16,0},{20,4},{24,8},{28,12},{1,17},{... | collective-permute-start | bytes 393224 | tf_op jit(solution)/shard_map/ppermute | solution.py:141
  4.5 6.6 %collective-permute-start.2 = (bf16[2,16,2048]{2,1,0:T(8,128)(2,1)}, bf16[2,16,2048]{2,1,0:T(8,128)(2,1)S(1)}, u32[]{:S(2)}, u32[]{:S(2)}) collective-permute-start(bf16[2,16,2048]{2,1,0:T(8,128)(2,1)} %param.8), channel_id=1, source_target_pairs={{0,24},{4,28},{8,16},{12,20},{16,8},{20,12},{24,0},{28,4},{1,25},{... | collective-permute-start | bytes 393224 | tf_op jit(solution)/shard_map/ppermute | solution.py:141
  4.6 7.1 %collective-permute-start.3 = (bf16[2,16,2048]{2,1,0:T(8,128)(2,1)}, bf16[2,16,2048]{2,1,0:T(8,128)(2,1)S(1)}, u32[]{:S(2)}, u32[]{:S(2)}) collective-permute-start(bf16[2,16,2048]{2,1,0:T(8,128)(2,1)} %param.8), channel_id=1, source_target_pairs={{0,4},{4,0},{8,12},{12,8},{16,20},{20,16},{24,28},{28,24},{1,5},{5... | collective-permute-start | bytes 393224 | tf_op jit(solution)/shard_map/ppermute | solution.py:141
  5.6 24.5 %collective-permute-start.11 = (bf16[2,128,768]{2,1,0:T(8,128)(2,1)S(1)}, bf16[2,128,768]{2,1,0:T(8,128)(2,1)S(1)}, u32[]{:S(2)}, u32[]{:S(2)}) collective-permute-start(bf16[2,128,768]{2,1,0:T(8,128)(2,1)S(1)} %slice.53.rest_1_), channel_id=1, source_target_pairs={{0,1},{3,2},{4,5},{7,6},{8,9},{11,10},{12,13},{15,14},{16,17},{19,... | collective-permute-start | bytes 1179656 | tf_op jit(solution)/shard_map/ppermute | solution.py:144
  10.5 1.4 collective-permute-start.4
  11.0 1.3 collective-permute-start.5
  11.2 1.4 collective-permute-start.6
  14.1 8.6 %collective-permute-start.10 = (f32[32,256]{1,0:T(8,128)S(1)}, f32[32,256]{1,0:T(8,128)S(1)}, u32[]{:S(2)}, u32[]{:S(2)}) collective-permute-start(f32[32,256]{1,0:T(8,128)S(1)} %shrink.1.rest_0_), channel_id=1, source_target_pairs={{0,3},{1,2},{2,1},{3,0},{4,7},{5,6},{6,5},{7,4},{8,11},{9,10},{10,... | collective-permute-start | bytes 98312 | tf_op jit(solution)/shard_map/ppermute | solution.py:144
  17.7 5.2 %collective-permute-start.8 = (f32[32,256]{1,0:T(8,128)S(1)}, f32[32,256]{1,0:T(8,128)S(1)}, u32[]{:S(2)}, u32[]{:S(2)}) collective-permute-start(f32[32,256]{1,0:T(8,128)S(1)} %shrink.1.rest_0_), channel_id=1, source_target_pairs={{0,1},{1,0},{2,3},{3,2},{4,5},{5,4},{6,7},{7,6},{8,9},{9,8},{10,11... | collective-permute-start | bytes 98312 | tf_op jit(solution)/shard_map/ppermute | solution.py:144
  17.7 5.2 %collective-permute-start.9 = (f32[32,256]{1,0:T(8,128)S(1)}, f32[32,256]{1,0:T(8,128)S(1)}, u32[]{:S(2)}, u32[]{:S(2)}) collective-permute-start(f32[32,256]{1,0:T(8,128)S(1)} %shrink.1.rest_0_), channel_id=1, source_target_pairs={{0,2},{1,3},{2,0},{3,1},{4,6},{5,7},{6,4},{7,5},{8,10},{9,11},{10,... | collective-permute-start | bytes 98312 | tf_op jit(solution)/shard_map/ppermute | solution.py:144
  23.0 11.5 %collective-permute-start.12 = (f32[32,256]{1,0:T(8,128)S(1)}, f32[32,256]{1,0:T(8,128)S(1)}, u32[]{:S(2)}, u32[]{:S(2)}) collective-permute-start(f32[32,256]{1,0:T(8,128)S(1)} %add_add_fusion.1.rest_0_), channel_id=1, source_target_pairs={{0,8},{4,12},{8,0},{12,4},{16,24},{20,28},{24,16},{28,20},{1,9},{5... | collective-permute-start | bytes 98312 | tf_op jit(solution)/shard_map/ppermute | solution.py:141
  24.2 10.3 %collective-permute-start.13 = (f32[32,256]{1,0:T(8,128)S(1)}, f32[32,256]{1,0:T(8,128)S(1)}, u32[]{:S(2)}, u32[]{:S(2)}) collective-permute-start(f32[32,256]{1,0:T(8,128)S(1)} %add_add_fusion.1.rest_0_), channel_id=1, source_target_pairs={{0,16},{4,20},{8,24},{12,28},{16,0},{20,4},{24,8},{28,12},{1,17},{... | collective-permute-start | bytes 98312 | tf_op jit(solution)/shard_map/ppermute | solution.py:141
  25.7 8.8 %collective-permute-start.14 = (f32[32,256]{1,0:T(8,128)S(1)}, f32[32,256]{1,0:T(8,128)S(1)}, u32[]{:S(2)}, u32[]{:S(2)}) collective-permute-start(f32[32,256]{1,0:T(8,128)S(1)} %add_add_fusion.1.rest_0_), channel_id=1, source_target_pairs={{0,24},{4,28},{8,16},{12,20},{16,8},{20,12},{24,0},{28,4},{1,25},{... | collective-permute-start | bytes 98312 | tf_op jit(solution)/shard_map/ppermute | solution.py:141
  26.5 10.1 %collective-permute-start.7 = (bf16[2,256,256]{2,1,0:T(8,128)(2,1)S(1)}, bf16[2,256,256]{2,1,0:T(8,128)(2,1)S(1)}, u32[]{:S(2)}, u32[]{:S(2)}) collective-permute-start(bf16[2,256,256]{2,1,0:T(8,128)(2,1)S(1)} %project.6.part_ref), channel_id=1, source_target_pairs={{0,1},{3,2},{4,5},{7,6},{8,9},{11,10},{12,13},{15,14},{16,17},{19,... | collective-permute-start | bytes 786440 | tf_op jit(solution)/shard_map/ppermute | solution.py:144
  33.1 14.6 %collective-permute-start.19 = (bf16[2,256,512]{2,1,0:T(8,128)(2,1)S(1)}, bf16[2,256,512]{2,1,0:T(8,128)(2,1)S(1)}, u32[]{:S(2)}, u32[]{:S(2)}) collective-permute-start(bf16[2,256,512]{2,1,0:T(8,128)(2,1)S(1)} %project.7.part_ref), channel_id=1, source_target_pairs={{0,1},{3,2},{4,5},{7,6},{8,9},{11,10},{12,13},{15,14},{16,17},{19,... | collective-permute-start | bytes 1572872 | tf_op jit(solution)/shard_map/ppermute | solution.py:144
  34.5 1.3 collective-permute-start.15
  37.0 10.6 %collective-permute-start.16 = (bf16[2,256,256]{2,1,0:T(8,128)(2,1)S(1)}, bf16[2,256,256]{2,1,0:T(8,128)(2,1)S(1)}, u32[]{:S(2)}, u32[]{:S(2)}) collective-permute-start(bf16[2,256,256]{2,1,0:T(8,128)(2,1)S(1)} %fold.6.rest_2_.part_ref), channel_id=1, source_target_pairs={{1,2},{2,1},{5,6},{6,5},{9,10},{10,9},{13,14},{14,13},{17,18},{18,... | collective-permute-start | bytes 786440 | tf_op jit(solution)/shard_map/ppermute | solution.py:144
  42.6 22.9 %collective-permute-start.18 = (bf16[2,256,768]{2,1,0:T(8,128)(2,1)S(1)}, bf16[2,256,768]{2,1,0:T(8,128)(2,1)S(1)}, u32[]{:S(2)}, u32[]{:S(2)}) collective-permute-start(bf16[2,256,768]{2,1,0:T(8,128)(2,1)S(1)} %project.8.rest_1_.part_ref), channel_id=1, source_target_pairs={{0,1},{3,2},{4,5},{7,6},{8,9},{11,10},{12,13},{15,14},{16,17},{19,... | collective-permute-start | bytes 2359304 | tf_op jit(solution)/shard_map/ppermute | solution.py:144
  48.2 11.6 %collective-permute-start.20 = (bf16[2,256,512]{2,1,0:T(8,128)(2,1)S(1)}, bf16[2,256,512]{2,1,0:T(8,128)(2,1)S(1)}, u32[]{:S(2)}, u32[]{:S(2)}) collective-permute-start(bf16[2,256,512]{2,1,0:T(8,128)(2,1)S(1)} %fold.7.rest_2_.part_ref), channel_id=1, source_target_pairs={{1,2},{2,1},{5,6},{6,5},{9,10},{10,9},{13,14},{14,13},{17,18},{18,... | collective-permute-start | bytes 1572872 | tf_op jit(solution)/shard_map/ppermute | solution.py:144
  53.7 28.6 %collective-permute-start.23 = (bf16[2,256,768]{2,1,0:T(8,128)(2,1)S(1)}, bf16[2,256,768]{2,1,0:T(8,128)(2,1)}, u32[]{:S(2)}, u32[]{:S(2)}) collective-permute-start(bf16[2,256,768]{2,1,0:T(8,128)(2,1)S(1)} %project.9.rest_1_.part_ref), channel_id=1, source_target_pairs={{0,1},{3,2},{4,5},{7,6},{8,9},{11,10},{12,13},{15,14},{16,17},{19,... | collective-permute-start | bytes 2359304 | tf_op jit(solution)/shard_map/ppermute | solution.py:144
  58.5 8.7 %collective-permute-start.17 = (bf16[256,256]{1,0:T(8,128)(2,1)S(1)}, bf16[256,256]{1,0:T(8,128)(2,1)S(1)}, u32[]{:S(2)}, u32[]{:S(2)}) collective-permute-start(bf16[256,256]{1,0:T(8,128)(2,1)S(1)} %hidden.6.rest_3_), channel_id=1, source_target_pairs={{1,0},{2,3},{5,4},{6,7},{9,8},{10,11},{13,12},{14,15},{17,16},{18,... | collective-permute-start | bytes 393224 | tf_op jit(solution)/shard_map/ppermute | solution.py:144
  65.7 29.3 %collective-permute-start.22 = (bf16[2,256,768]{2,1,0:T(8,128)(2,1)S(1)}, bf16[2,256,768]{2,1,0:T(8,128)(2,1)}, u32[]{:S(2)}, u32[]{:S(2)}) collective-permute-start(bf16[2,256,768]{2,1,0:T(8,128)(2,1)S(1)} %fold.8.rest_2_.part_ref), channel_id=1, source_target_pairs={{1,2},{2,1},{5,6},{6,5},{9,10},{10,9},{13,14},{14,13},{17,18},{18,... | collective-permute-start | bytes 2359304 | tf_op jit(solution)/shard_map/ppermute | solution.py:144
  72.1 25.8 %collective-permute-start.21 = (bf16[256,512]{1,0:T(8,128)(2,1)S(1)}, bf16[256,512]{1,0:T(8,128)(2,1)S(1)}, u32[]{:S(2)}, u32[]{:S(2)}) collective-permute-start(bf16[256,512]{1,0:T(8,128)(2,1)S(1)} %hidden.7.rest_0_), channel_id=1, source_target_pairs={{1,0},{2,3},{5,4},{6,7},{9,8},{10,11},{13,12},{14,15},{17,16},{18,... | collective-permute-start | bytes 786440 | tf_op jit(solution)/shard_map/ppermute | solution.py:144
  73.4 27.0 %collective-permute-start.26 = (bf16[2,256,768]{2,1,0:T(8,128)(2,1)S(1)}, bf16[2,256,768]{2,1,0:T(8,128)(2,1)S(1)}, u32[]{:S(2)}, u32[]{:S(2)}) collective-permute-start(bf16[2,256,768]{2,1,0:T(8,128)(2,1)S(1)} %project.10.part_ref), channel_id=1, source_target_pairs={{0,1},{3,2},{4,5},{7,6},{8,9},{11,10},{12,13},{15,14},{16,17},{19,... | collective-permute-start | bytes 2359304 | tf_op jit(solution)/shard_map/ppermute | solution.py:144
  83.7 17.8 %collective-permute-start.25 = (bf16[2,256,768]{2,1,0:T(8,128)(2,1)S(1)}, bf16[2,256,768]{2,1,0:T(8,128)(2,1)S(1)}, u32[]{:S(2)}, u32[]{:S(2)}) collective-permute-start(bf16[2,256,768]{2,1,0:T(8,128)(2,1)S(1)} %fold.9.rest_2_.part_ref), channel_id=1, source_target_pairs={{1,2},{2,1},{5,6},{6,5},{9,10},{10,9},{13,14},{14,13},{17,18},{18,... | collective-permute-start | bytes 2359304 | tf_op jit(solution)/shard_map/ppermute | solution.py:144
  88.0 25.5 %collective-permute-start.29 = (bf16[2,256,512]{2,1,0:T(8,128)(2,1)S(1)}, bf16[2,256,512]{2,1,0:T(8,128)(2,1)S(1)}, u32[]{:S(2)}, u32[]{:S(2)}) collective-permute-start(bf16[2,256,512]{2,1,0:T(8,128)(2,1)S(1)} %project.11.rest_1_.part_ref), channel_id=1, source_target_pairs={{0,1},{3,2},{4,5},{7,6},{8,9},{11,10},{12,13},{15,14},{16,17},{19,... | collective-permute-start | bytes 1572872 | tf_op jit(solution)/shard_map/ppermute | solution.py:144
  95.0 21.5 %slice-start = ((s8[14680064]{0:T(1024)(128)(4,1)}), s8[4194304]{0:T(1024)(128)(4,1)S(1)}, s32[]{:S(2)}) async-start(s8[14680064]{0:T(1024)(128)(4,1)} %bitcast.28), calls=%async_computation | async-start | bytes 8388608
  96.6 13.8 %collective-permute-start.24 = (bf16[256,768]{1,0:T(8,128)(2,1)S(1)}, bf16[256,768]{1,0:T(8,128)(2,1)S(1)}, u32[]{:S(2)}, u32[]{:S(2)}) collective-permute-start(bf16[256,768]{1,0:T(8,128)(2,1)S(1)} %hidden.8), channel_id=1, source_target_pairs={{1,0},{2,3},{5,4},{6,7},{9,8},{10,11},{13,12},{14,15},{17,16},{18,... | collective-permute-start | bytes 1179656 | tf_op jit(solution)/shard_map/ppermute | solution.py:144
  98.0 18.5 %slice-start.1 = ((s8[14680064]{0:T(1024)(128)(4,1)}), s8[4194304]{0:T(1024)(128)(4,1)S(1)}, s32[]{:S(2)}) async-start(s8[14680064]{0:T(1024)(128)(4,1)} %bitcast.28), calls=%async_computation.1 | async-start | bytes 8388608
  100.6 15.8 %slice-start.2 = ((s8[14680064]{0:T(1024)(128)(4,1)}), s8[4194304]{0:T(1024)(128)(4,1)S(1)}, s32[]{:S(2)}) async-start(s8[14680064]{0:T(1024)(128)(4,1)} %bitcast.28), calls=%async_computation.2 | async-start | bytes 8388608
  100.6 14.1 %collective-permute-start.28 = (bf16[2,256,768]{2,1,0:T(8,128)(2,1)S(1)}, bf16[2,256,768]{2,1,0:T(8,128)(2,1)S(1)}, u32[]{:S(2)}, u32[]{:S(2)}) collective-permute-start(bf16[2,256,768]{2,1,0:T(8,128)(2,1)S(1)} %fold.10.rest_1_.part_ref), channel_id=1, source_target_pairs={{1,2},{2,1},{5,6},{6,5},{9,10},{10,9},{13,14},{14,13},{17,18},{18,... | collective-permute-start | bytes 2359304 | tf_op jit(solution)/shard_map/ppermute | solution.py:144
  101.9 12.8 %collective-permute-start.27 = (bf16[256,768]{1,0:T(8,128)(2,1)S(1)}, bf16[256,768]{1,0:T(8,128)(2,1)S(1)}, u32[]{:S(2)}, u32[]{:S(2)}) collective-permute-start(bf16[256,768]{1,0:T(8,128)(2,1)S(1)} %hidden.9), channel_id=1, source_target_pairs={{1,0},{2,3},{5,4},{6,7},{9,8},{10,11},{13,12},{14,15},{17,16},{18,... | collective-permute-start | bytes 1179656 | tf_op jit(solution)/shard_map/ppermute | solution.py:144
  110.5 6.0 %slice-start.3 = ((s8[14680064]{0:T(1024)(128)(4,1)}), s8[2097152]{0:T(1024)(128)(4,1)S(1)}, s32[]{:S(2)}) async-start(s8[14680064]{0:T(1024)(128)(4,1)} %bitcast.28), calls=%async_computation.3 | async-start | bytes 4194304
  113.7 3.8 %collective-permute-start.31 = (bf16[2,256,512]{2,1,0:T(8,128)(2,1)S(1)}, bf16[2,256,512]{2,1,0:T(8,128)(2,1)S(1)}, u32[]{:S(2)}, u32[]{:S(2)}) collective-permute-start(bf16[2,256,512]{2,1,0:T(8,128)(2,1)S(1)} %fold.11.rest_1_.part_ref), channel_id=1, source_target_pairs={{1,2},{2,1},{5,6},{6,5},{9,10},{10,9},{13,14},{14,13},{17,18},{18,... | collective-permute-start | bytes 1572872 | tf_op jit(solution)/shard_map/ppermute | solution.py:144
  115.1 17.3 %collective-permute-start.30 = (bf16[256,768]{1,0:T(8,128)(2,1)S(1)}, bf16[256,768]{1,0:T(8,128)(2,1)S(1)}, u32[]{:S(2)}, u32[]{:S(2)}) collective-permute-start(bf16[256,768]{1,0:T(8,128)(2,1)S(1)} %hidden.10), channel_id=1, source_target_pairs={{1,0},{2,3},{5,4},{6,7},{9,8},{10,11},{13,12},{14,15},{17,16},{18,... | collective-permute-start | bytes 1179656 | tf_op jit(solution)/shard_map/ppermute | solution.py:144
  117.7 18.1 %collective-permute-start.32 = (bf16[256,512]{1,0:T(8,128)(2,1)S(1)}, bf16[256,512]{1,0:T(8,128)(2,1)S(1)}, u32[]{:S(2)}, u32[]{:S(2)}) collective-permute-start(bf16[256,512]{1,0:T(8,128)(2,1)S(1)} %hidden.11), channel_id=1, source_target_pairs={{1,0},{2,3},{5,4},{6,7},{9,8},{10,11},{13,12},{14,15},{17,16},{18,... | collective-permute-start | bytes 786440 | tf_op jit(solution)/shard_map/ppermute | solution.py:144
  136.7 2.0 %collective-permute-start.33 = (bf16[2,64,2048]{2,1,0:T(8,128)(2,1)S(1)}, bf16[2,64,2048]{2,1,0:T(8,128)(2,1)S(1)}, u32[]{:S(2)}, u32[]{:S(2)}) collective-permute-start(bf16[2,64,2048]{2,1,0:T(8,128)(2,1)S(1)} %slice.87), channel_id=1, source_target_pairs={{0,4},{4,0},{8,12},{12,8},{16,20},{20,16},{24,28},{28,24},{1,5},{5... | collective-permute-start | bytes 1572872 | tf_op jit(solution)/shard_map/ppermute | solution.py:141
  138.8 7.3 %collective-permute-start.34 = (bf16[2,16,2048]{2,1,0:T(8,128)(2,1)S(1)}, bf16[2,16,2048]{2,1,0:T(8,128)(2,1)S(1)}, u32[]{:S(2)}, u32[]{:S(2)}) collective-permute-start(bf16[2,16,2048]{2,1,0:T(8,128)(2,1)S(1)} %get-tuple-element.23), channel_id=1, source_target_pairs={{0,24},{4,28},{8,16},{12,20},{16,8},{20,12},{24,0},{28,4},{1,25},{... | collective-permute-start | bytes 393224 | tf_op jit(solution)/shard_map/ppermute | solution.py:141
  140.6 7.5 %collective-permute-start.35 = (bf16[2,16,2048]{2,1,0:T(8,128)(2,1)S(1)}, bf16[2,16,2048]{2,1,0:T(8,128)(2,1)S(1)}, u32[]{:S(2)}, u32[]{:S(2)}) collective-permute-start(bf16[2,16,2048]{2,1,0:T(8,128)(2,1)S(1)} %get-tuple-element.25), channel_id=1, source_target_pairs={{0,16},{4,20},{8,24},{12,28},{16,0},{20,4},{24,8},{28,12},{1,17},{... | collective-permute-start | bytes 393224 | tf_op jit(solution)/shard_map/ppermute | solution.py:141
  141.1 7.1 %collective-permute-start.36 = (bf16[2,16,2048]{2,1,0:T(8,128)(2,1)S(1)}, bf16[2,16,2048]{2,1,0:T(8,128)(2,1)S(1)}, u32[]{:S(2)}, u32[]{:S(2)}) collective-permute-start(bf16[2,16,2048]{2,1,0:T(8,128)(2,1)S(1)} %get-tuple-element.24), channel_id=1, source_target_pairs={{0,8},{4,12},{8,0},{12,4},{16,24},{20,28},{24,16},{28,20},{1,9},{5... | collective-permute-start | bytes 393224 | tf_op jit(solution)/shard_map/ppermute | solution.py:141
